TPU v7x, 256 devices: a whole 4x4x8 slice. The times are simulated.
256 devices in a mesh: cent: 128 (over y, x, z), rep: 2 (over core).
Axes of the slice: x: 4, y: 4, z: 8, core: 2. Of those that a mesh axis runs over, the one named last changes fastest.
Arguments:
- new_vectors: float32 [8192, 1024], P(('cent', 'rep')), may hold values from -6 to 6
- centroids: float32 [65536, 1024], P('cent'), may hold values from -6 to 6
- primary_owner: int32 [8192, 1], P(('cent', 'rep')), may hold values from 0 to 127; in each aligned block of 32 rows (0 to 31, 32 to 63, ...) at most 2 rows name the same one
- primary_row: int32 [8192, 1], P(('cent', 'rep')), may hold values from 0 to 511
- cand_owner: int32 [8192, 4], P(('cent', 'rep')), may hold values from 0 to 127, all different within a row; in each aligned block of 32 rows (0 to 31, 32 to 63, ...) at most 2 rows name the same one
- cand_row: int32 [8192, 256], P(('cent', 'rep')), may hold values from 0 to 511
Outputs:
- spill_loss: float32 [8192, 256], P(('cent', 'rep'))
Inputs may be any that keep to these rules, and one draw needn't show every extreme that they name: `primary_owner`: in each aligned block of 32 vectors (the vectors of one device) no shard is named by more than 2 vectors, a bound that some block reaches. `cand_owner`: each vector names 4 different shards; in each aligned block of 32 vectors (the vectors of one device) no shard is named by more than 2 vectors, a bound that some block reaches.
All inputs are finite; a program needn't handle non-finite values.
Results may differ from a plain program's by a relative error of at most 0.00007.
Values sent between devices are 32-bit elements; how exact they have to be, the bound alone decides.
No kernel may reach another device: no remote copies, remote signals or barrier semaphores. Data moves between devices by JAX's collectives and lax.ppermute only.
A program may use at most 64 MiB of HBM per device.

v0:
```python
import jax
import jax.numpy as jnp
from jax import lax
from jax.sharding import PartitionSpec as P

CGROUPS = 4


amplify = 1.0
tiny = 1e-06


def slot_ranks(owners, shard_count):
    column = jnp.arange(shard_count, dtype=jnp.int32)
    onehot = (owners[:, None] == column[None, :]).astype(jnp.int32)
    before = jnp.cumsum(onehot, axis=0) - onehot
    return jnp.sum(before * onehot, axis=1)


def placement(owners, shard_count, capacity):
    slot_rank = slot_ranks(owners, shard_count)
    slot_index = owners * capacity + slot_rank
    slots_all = jnp.arange(shard_count * capacity, dtype=jnp.int32)
    return (slots_all[:, None] == slot_index[None, :]).astype(jnp.float32)


def spread_rows(place, items):
    return jnp.dot(
        place, items, precision=lax.Precision.HIGHEST, preferred_element_type=jnp.float32
    )


def collect_rows(place, slots):
    return jnp.dot(
        place.T, slots, precision=lax.Precision.HIGHEST, preferred_element_type=jnp.float32
    )


def fetch_primary(centroids, owners, local_rows, shard_count, capacity):
    slot_rank = slot_ranks(owners, shard_count)
    shard_hit = (owners[:, None] == jnp.arange(shard_count, dtype=jnp.int32)[None, :]).astype(
        jnp.int32
    )
    rank_hit = (slot_rank[:, None] == jnp.arange(capacity, dtype=jnp.int32)[None, :]).astype(
        jnp.int32
    )
    requests = jnp.sum(
        local_rows[:, None, None] * shard_hit[:, :, None] * rank_hit[:, None, :], axis=0
    )
    picked = jnp.take(
        centroids, lax.all_to_all(requests, "cent", split_axis=0, concat_axis=0, tiled=True), axis=0
    )
    fetched = lax.all_to_all(picked, "cent", split_axis=0, concat_axis=0, tiled=True)
    place = placement(owners, shard_count, capacity)
    return collect_rows(place, fetched.reshape(shard_count * capacity, fetched.shape[2]))


def shards(new_vectors, centroids, primary_owner, primary_row, cand_owner, cand_row):
    shard_count = lax.axis_size("cent")
    vec_count = new_vectors.shape[0]
    width = new_vectors.shape[1]
    groups_here = cand_owner.shape[1]
    group_size = cand_row.shape[1] // groups_here
    capacity = max(2, 2 * vec_count // shard_count)
    slot_cap = max(2, 3 * vec_count * CGROUPS // (2 * shard_count))
    primary = fetch_primary(
        centroids, primary_owner[:, 0], primary_row[:, 0], shard_count, capacity
    )
    residual = new_vectors - primary
    item_count = vec_count * groups_here
    owners = cand_owner.reshape(item_count)
    place = placement(owners, shard_count, slot_cap)
    joined = jnp.concatenate([new_vectors, residual], axis=1)
    joined_items = jnp.broadcast_to(
        joined[:, None, :], (vec_count, groups_here, 2 * width)
    ).reshape(item_count, 2 * width)
    row_items = cand_row.reshape(item_count, group_size).astype(jnp.float32)
    payload = spread_rows(place, joined_items).reshape(shard_count, slot_cap, 2 * width)
    row_slots = spread_rows(place, row_items).reshape(shard_count, slot_cap, group_size)
    norms_here = jnp.sum(centroids * centroids, axis=1)
    arrived = lax.all_to_all(payload, "cent", split_axis=0, concat_axis=0, tiled=True)
    arrived_rows = lax.all_to_all(row_slots, "cent", split_axis=0, concat_axis=0, tiled=True)
    sources = arrived.shape[0]
    slots = arrived.shape[1]
    total = sources * slots
    flat = arrived.reshape(total, 2 * width)
    vectors_in = flat[:, :width]
    resid_in = flat[:, width:]
    row_ids = arrived_rows.reshape(total, group_size).astype(jnp.int32)
    stacked = jnp.concatenate([vectors_in, resid_in], axis=0)
    scores = jnp.einsum("md,cd->mc", stacked, centroids, precision=lax.Precision.HIGHEST)
    cross_x = jnp.take_along_axis(scores[:total], row_ids, axis=1)
    cross_r = jnp.take_along_axis(scores[total:], row_ids, axis=1)
    cand_norms = jnp.take(norms_here, row_ids, axis=0)
    sq_x = jnp.sum(vectors_in * vectors_in, axis=1)[:, None]
    sq_r = jnp.sum(resid_in * resid_in, axis=1)[:, None]
    dot_rx = jnp.sum(resid_in * vectors_in, axis=1)[:, None]
    gap = dot_rx - cross_r
    losses = (sq_x - 2.0 * cross_x + cand_norms + amplify * gap * gap / (sq_r + tiny)) / width
    tiles = losses.reshape(sources, slots, group_size)
    returned = lax.all_to_all(tiles, "cent", split_axis=0, concat_axis=0, tiled=True)
    picked_back = collect_rows(place, returned.reshape(shard_count * slot_cap, group_size))
    return picked_back.reshape(vec_count, groups_here * group_size)


def solution(mesh):
    in_specs = (
        P(("cent", "rep"), None),
        P("cent", None),
        P(("cent", "rep"), None),
        P(("cent", "rep"), None),
        P(("cent", "rep"), None),
        P(("cent", "rep"), None),
    )
    out_specs = P(("cent", "rep"), None)
    return jax.shard_map(shards, mesh=mesh, in_specs=in_specs, out_specs=out_specs, check_vma=False)
```

profile of v0, /device:TPU:2, one launch (start us, length us, event | category | flops | bytes accessed | tf_op | source)
XLA Modules:
  0.0 497.2 jit_solution(8226585479916305538)
XLA Ops:
  0.0 0.7 fusion.24
  0.8 0.8 fusion.23
  1.9 26.3 %all_to_all.35 = s32[128,1,2]{2,1,0:T(1,128)S(1)} all-to-all(s32[128,1,2]{2,1,0:T(1,128)S(1)} %copy.21), channel_id=1, replica_groups=mesh['cent'=128,'rep'=2] {'cent'}, dimensions={0} | all-to-all | bytes 2048 | tf_op jit(solution)/shard_map/all_to_all | solution.py:51
  28.3 3.2 gather_fusion
  32.2 1.5 broadcast_select_fusion
  33.7 6.8 %all-to-all-start.1 = ((f32[128,2,1024]{2,1,0:T(2,128)}), f32[128,2,1024]{2,1,0:T(2,128)S(1)}, u32[]{:S(2)}, u32[]{:S(2)}) async-start(f32[128,2,1024]{2,1,0:T(2,128)} %broadcast_select_fusion), calls=%async_computation.1 | async-start | bytes 2097152 | tf_op jit(solution)/shard_map/all_to_all | solution.py:53
  41.7 0.8 reshape.272
  42.4 26.3 %all-to-all-done.1 = f32[128,2,1024]{2,1,0:T(2,128)S(1)} async-done(((f32[128,2,1024]{2,1,0:T(2,128)}), f32[128,2,1024]{2,1,0:T(2,128)S(1)}, u32[]{:S(2)}, u32[]{:S(2)}) %all-to-all-start.1) | async-done | bytes 1048608 | tf_op jit(solution)/shard_map/all_to_all | solution.py:53
  68.7 8.7 %all-to-all-start.3 = ((f32[128,1,128]{2,1,0:T(1,128)}), f32[128,1,128]{2,1,0:T(1,128)S(1)}, u32[]{:S(2)}, u32[]{:S(2)}) async-start(f32[128,1,128]{2,1,0:T(1,128)} %reshape.272), calls=%async_computation.3 | async-start | bytes 131072 | tf_op jit(solution)/shard_map/all_to_all | solution.py:82
  77.4 0.7 reshape.212
  79.4 1.0 fusion.6
  80.4 2.9 copy.22
  83.3 5.2 %all-to-all-done.3 = f32[128,1,128]{2,1,0:T(1,128)S(1)} async-done(((f32[128,1,128]{2,1,0:T(1,128)}), f32[128,1,128]{2,1,0:T(1,128)S(1)}, u32[]{:S(2)}, u32[]{:S(2)}) %all-to-all-start.3) | async-done | bytes 65568 | tf_op jit(solution)/shard_map/all_to_all | solution.py:82
  88.6 9.2 %all-to-all-start.2 = ((f32[128,2,2048]{2,1,0:T(2,128)}), f32[128,2,2048]{2,1,0:T(2,128)}, u32[]{:S(2)}, u32[]{:S(2)}) async-start(f32[128,2,2048]{2,1,0:T(2,128)} %copy.22), calls=%async_computation.2 | async-start | bytes 4194304 | tf_op jit(solution)/shard_map/all_to_all | solution.py:81
  98.6 0.8 reduce
  99.8 101.9 %gather_fusion.1 = f32[16384]{0:T(1024)S(1)} fusion(f32[512]{0:T(512)S(1)} %multiply_reduce_fusion, s32[16384]{0:T(1024)S(1)} %broadcast_clamp_fusion), kind=kCustom, calls=%fused_computation.3 | custom fusion | bytes 196608 | tf_op jit(solution)/shard_map/jit(_take)/gather | solution.py:94
  201.9 3.7 reshape.214
  205.5 2.0 multiply_reduce_fusion.3
  207.5 3.5 fusion
  211.1 129.5 %gather_fusion.2 = f32[16384]{0:T(1024)S(1)} fusion(f32[256,512]{1,0:T(8,128)S(1)} %get-tuple-element.11, s32[16384]{0:T(1024)S(1)} %reshape.260), kind=kCustom, calls=%fused_computation.clone | custom fusion | bytes 262144 | tf_op jit(solution)/shard_map/jit(take_along_axis)/gather | solution.py:92
  340.7 129.5 %gather_fusion.3 = f32[16384]{0:T(1024)S(1)} fusion(f32[256,512]{1,0:T(8,128)S(1)} %get-tuple-element.12, s32[16384]{0:T(1024)S(1)} %reshape.260), kind=kCustom, calls=%fused_computation.1.clone | custom fusion | bytes 262144 | tf_op jit(solution)/shard_map/jit(take_along_axis)/gather | solution.py:93
  470.6 24.7 %all_to_all.36 = f32[128,1,128]{2,1,0:T(1,128)S(1)} all-to-all(f32[128,1,128]{2,1,0:T(1,128)S(1)} %reshape.274), channel_id=1, replica_groups=mesh['cent'=128,'rep'=2] {'cent'}, dimensions={0} | all-to-all | bytes 131072 | tf_op jit(solution)/shard_map/all_to_all | solution.py:101
  495.3 0.8 reduce.1
  496.5 0.7 reshape.217
  (54 shorter events, 5.6 us)
Async XLA Ops:
  32.1 8.3 %copy-start.4 = (s32[32,4]{0,1:T(4,128)S(1)}, s32[32,4]{0,1:T(4,128)}, u32[]{:S(2)}) copy-start(s32[32,4]{0,1:T(4,128)} %param.12) | copy-start | bytes 1540
  32.2 8.8 %copy-start.2 = (s32[32,256]{1,0:T(8,128)S(1)}, s32[32,256]{1,0:T(8,128)}, u32[]{:S(2)}) copy-start(s32[32,256]{1,0:T(8,128)} %param.13) | copy-start | bytes 98308
  32.2 10.3 %copy-start.3 = (s32[32,1]{0,1:T(1,128)S(1)}, s32[32,1]{0,1:T(1,128)}, u32[]{:S(2)}) copy-start(s32[32,1]{0,1:T(1,128)} %param.10) | copy-start | bytes 388
  33.7 35.0 %all-to-all-start.1 = ((f32[128,2,1024]{2,1,0:T(2,128)}), f32[128,2,1024]{2,1,0:T(2,128)S(1)}, u32[]{:S(2)}, u32[]{:S(2)}) async-start(f32[128,2,1024]{2,1,0:T(2,128)} %broadcast_select_fusion), calls=%async_computation.1 | async-start | bytes 2097152 | tf_op jit(solution)/shard_map/all_to_all | solution.py:53
  40.5 37.7 %copy-start.1 = (f32[32,1024]{1,0:T(8,128)S(1)}, f32[32,1024]{1,0:T(8,128)}, u32[]{:S(2)}) copy-start(f32[32,1024]{1,0:T(8,128)} %param.8) | copy-start | bytes 393220
  68.7 19.8 %all-to-all-start.3 = ((f32[128,1,128]{2,1,0:T(1,128)}), f32[128,1,128]{2,1,0:T(1,128)S(1)}, u32[]{:S(2)}, u32[]{:S(2)}) async-start(f32[128,1,128]{2,1,0:T(1,128)} %reshape.272), calls=%async_computation.3 | async-start | bytes 131072 | tf_op jit(solution)/shard_map/all_to_all | solution.py:82
  83.3 14.5 %copy-start = (f32[512,1024]{1,0:T(8,128)S(1)}, f32[512,1024]{1,0:T(8,128)}, u32[]{:S(2)}) copy-start(f32[512,1024]{1,0:T(8,128)} %param.9) | copy-start | bytes 6291460
  88.6 113.3 %all-to-all-start.2 = ((f32[128,2,2048]{2,1,0:T(2,128)}), f32[128,2,2048]{2,1,0:T(2,128)}, u32[]{:S(2)}, u32[]{:S(2)}) async-start(f32[128,2,2048]{2,1,0:T(2,128)} %copy.22), calls=%async_computation.2 | async-start | bytes 4194304 | tf_op jit(solution)/shard_map/all_to_all | solution.py:81
where the time goes:
time: 498 us; the launch traced here: 497 us
  local copies, waits for them, and re-layouts  376 us (76%)
  blocking collectives  51 us (10%)
  waiting for transfers between devices  31.5 us (6%)
  starting transfers between devices  24.7 us (5%)
  other arithmetic  7.86 us (2%)
  matrix products  5.66 us (1%)
    gather x3, local copies, waits for them, and re-layouts, shards(): cross_x = jnp.take_along_axis(scores[:total], row_ids, axis=1)  130 us
    gather x2, local copies, waits for them, and re-layouts, shards(): cross_r = jnp.take_along_axis(scores[total:], row_ids, axis=1)  130 us
    gather x2, local copies, waits for them, and re-layouts, shards(): cand_norms = jnp.take(norms_here, row_ids, axis=0)  102 us
    all_to_all x1, blocking collectives, fetch_primary(): lax.all_to_all(requests, 'cent', split_axis=0, concat_axis=0, tiled=True)  26.3 us
    all_to_all x1, waiting for transfers between devices, fetch_primary(): lax.all_to_all(picked, 'cent', split_axis=0, concat_axis=0, tiled=True)  26.3 us
    all_to_all x1, blocking collectives, shards(): lax.all_to_all(tiles, 'cent', split_axis=0, concat_axis=0, tiled=True)  24.7 us
  transfers between devices with their start and end apart: 3, of which 2 were waited for; matrix products, arithmetic and copies ran while one was open for 22% of the time, Pallas kernels for 0%

commit v1 on v0

v1 whole, which is shorter than its diff:
```python
import jax
import jax.numpy as jnp
from jax import lax
from jax.experimental import pallas as pl
from jax.experimental.pallas import tpu as pltpu
from jax.sharding import Mesh, PartitionSpec as P

D = 1024
V = 32
GROUPS = 4
GSIZE = 64
ROWS = 512
NY, NX, NZ = 4, 4, 8
COLS = NY * NX
COLV = NZ * V
SLOTS = COLS * NZ * 2
K = 32
amplify = 1.0
tiny = 1e-06

F32, BF16, I32 = jnp.float32, jnp.bfloat16, jnp.int32
VMEM = pl.BlockSpec(memory_space=pltpu.VMEM)
SMEM = pl.BlockSpec(memory_space=pltpu.SMEM)
NN = (((1,), (0,)), ((), ()))
NT = (((1,), (1,)), ((), ()))
TN = (((0,), (0,)), ((), ()))


def call(kernel, out_shape, *operands, smem=(), name=None):
    specs = [SMEM if i in smem else VMEM for i in range(len(operands))]
    many = isinstance(out_shape, (list, tuple))
    return pl.pallas_call(
        kernel,
        out_shape=out_shape,
        in_specs=specs,
        out_specs=[VMEM] * len(out_shape) if many else VMEM,
        compiler_params=pltpu.CompilerParams(vmem_limit_bytes=48 * 2**20),
        name=name,
    )(*operands)


def shape(dims, dtype=F32):
    return jax.ShapeDtypeStruct(dims, dtype)


def split3(a):
    hi = a.astype(BF16)
    rest = a - hi.astype(F32)
    mid = rest.astype(BF16)
    lo = (rest - mid.astype(F32)).astype(BF16)
    return hi, mid, lo


def dot(a, b, dims=NN):
    return lax.dot_general(a, b, dims, preferred_element_type=F32)


def pick(onehot, pieces):
    hi, mid, lo = pieces
    return dot(onehot, hi) + dot(onehot, mid) + dot(onehot, lo)


def bits(mask):
    return jnp.where(mask, 1.0, 0.0)


def iota(dims, axis):
    return lax.broadcasted_iota(I32, dims, axis)


def before_same_block(rows):
    u, w = iota((rows, rows), 0), iota((rows, rows), 1)
    return bits((w < u) & ((u >> 5) == (w >> 5))).astype(BF16)


def before_all(rows):
    return bits(iota((rows, rows), 1) < iota((rows, rows), 0)).astype(BF16)


def prepare_kernel(c_ref, pieces_ref, norms_ref):
    c = c_ref[...]
    for i, piece in enumerate(split3(c)):
        pieces_ref[i] = piece
    squares = split3(c * c)
    ones = jnp.ones((8, D), BF16)
    norms_ref[...] = sum(dot(ones, s, NT) for s in squares)


def request_kernel(me_ref, info_ref, out_ref):
    me = me_ref[0]
    lane = iota((COLV, 128), 1)
    owner = info_ref[:, 0:1]
    row = info_ref[:, 1:2].astype(F32)
    hit = (owner == lane * NZ + me) & (lane < COLS)
    hits = bits(hit)
    rank = dot(before_same_block(COLV), hits.astype(BF16))
    sums = [
        jnp.where(hit & (rank == float(k)), row, 0.0).reshape(NZ, V, 128).sum(axis=1)
        for k in range(2)
    ]
    plane_from = bits(((owner & 7) == lane) & (lane < NZ)).astype(BF16)
    wanted = lane < 0
    for g in range(GROUPS):
        wanted = wanted | ((info_ref[:, 2 + g : 3 + g] & 7) == lane)
    plane_to = bits(wanted & (lane < NZ)).astype(BF16)
    most = jnp.max(dot(plane_from, plane_to, TN))
    small = iota((NZ, 128), 1)
    for a in range(COLS):
        tile = jnp.where(
            small == 0,
            sums[0][:, a : a + 1],
            jnp.where(small == 1, sums[1][:, a : a + 1], most),
        )
        out_ref[a] = tile.astype(I32)


def slots_kernel(me_ref, info_ref, out_ref):
    me = me_ref[0]
    lane = iota((COLV, 128), 1)
    hits = []
    for g in range(GROUPS):
        owner = info_ref[:, 2 + g : 3 + g]
        hits.append((owner == lane * NZ + me) & (lane < COLS))
    any_hit = bits(hits[0] | hits[1] | hits[2] | hits[3])
    rank = dot(before_same_block(COLV), any_hit.astype(BF16))
    block = iota((NZ, COLV), 1) >> 5
    mine = block == iota((NZ, COLV), 0)
    for g in range(GROUPS):
        for k in range(2):
            turned = bits(hits[g] & (rank == float(k))).T
            for b in range(COLS):
                tile = jnp.where(mine, turned[b : b + 1, :], 0.0)
                out_ref[g, b * 16 + k * 8 : b * 16 + k * 8 + 8, :] = tile


def relay_kernel(me_ref, turn_ref, info_ref, slots_ref, send_ref, take_ref):
    me = me_ref[0]
    base = (turn_ref[0] * K).astype(F32)
    lane = iota((COLV, 128), 1)
    u = iota((COLV, 1), 0)
    owner = info_ref[:, 0:1]
    hits = bits((owner == lane * NZ + me) & (lane < COLS))
    rank = dot(before_same_block(COLV), hits.astype(BF16))
    rank = jnp.sum(rank * hits, axis=1, keepdims=True)
    here = (owner & 7) == me
    wanted = lane < 0
    to_me = u < 0
    for g in range(GROUPS):
        plane = info_ref[:, 2 + g : 3 + g] & 7
        wanted = wanted | (plane == lane)
        to_me = to_me | (plane == me)
    earlier = before_all(COLV)
    leaves = wanted & (lane < NZ) & here
    order = dot(earlier, bits(leaves).astype(BF16))
    place = jnp.where(leaves, order - base, -1.0).T
    depth = iota((K, COLV), 0).astype(F32)
    rows = jnp.concatenate([bits(place[z : z + 1, :] == depth) for z in range(NZ)], axis=0)
    slot = (owner >> 3) * 16 + rank.astype(I32) * 8 + (u >> 5)
    held = bits((slot == iota((COLV, SLOTS), 1)) & here)
    send_ref[...] = dot(rows.astype(BF16), held.astype(BF16)).astype(BF16)
    comes = ((owner & 7) == lane) & (lane < NZ) & to_me
    order = dot(earlier, bits(comes).astype(BF16)) - base
    fits = comes & (order >= 0.0) & (order < float(K))
    at = jnp.sum(jnp.where(fits, lane.astype(F32) * K + order + 1.0, 0.0), axis=1, keepdims=True)
    found = bits(at == iota((COLV, NZ * K), 1).astype(F32) + 1.0).astype(BF16)
    all_slots = slots_ref[0] + slots_ref[1] + slots_ref[2] + slots_ref[3]
    take_ref[...] = dot(all_slots.astype(BF16), found).astype(BF16)


def fetch_kernel(asked_ref, pieces_ref, out_ref, most_ref):
    column = iota((COLS * NZ, ROWS), 1)
    pieces = [pieces_ref[i] for i in range(3)]
    for k in range(2):
        onehot = bits(asked_ref[:, k : k + 1] == column).astype(BF16)
        out_ref[:, k * 8 : k * 8 + 8, :] = pick(onehot, pieces).reshape(COLS, 8, D)
    most = jnp.max(asked_ref[:, 2:3].astype(F32)).astype(I32)
    most_ref[...] = jnp.full((8, 128), most, I32)


def move_kernel(onehot_ref, in_ref, out_ref):
    out_ref[...] = pick(onehot_ref[...], split3(in_ref[...]))


def vectors_kernel(slots_ref, in_ref, out_ref):
    slots = [slots_ref[g] for g in range(GROUPS)]
    every = (slots[0] + slots[1] + slots[2] + slots[3]).astype(BF16)
    out_ref[:, :D] = pick(every, split3(in_ref[:, :D]))
    rows = jnp.zeros((SLOTS, 128), F32)
    for h in range(2):
        pieces = split3(in_ref[:, D + 128 * h : D + 128 * h + 128])
        rows = rows + jnp.where(iota((SLOTS, 128), 1) < GSIZE, pick(slots[2 * h].astype(BF16), pieces), 0.0)
        odd = pltpu.roll(pick(slots[2 * h + 1].astype(BF16), pieces), GSIZE, 1)
        rows = rows + jnp.where(iota((SLOTS, 128), 1) < GSIZE, odd, 0.0)
    out_ref[:, D:] = rows


def lookup(table, rows):
    low, high = rows & 127, rows >> 7
    found = jnp.zeros(rows.shape, F32)
    for i in range(ROWS // 128):
        part = jnp.take_along_axis(table[:, 128 * i : 128 * i + 128], low, axis=1)
        found = jnp.where(high == i, part, found)
    return found


def scores(a, pieces_ref):
    hi, mid, lo = split3(a)
    chi, cmid, clo = (pieces_ref[i] for i in range(3))
    small = dot(mid, cmid, NT) + dot(lo, chi, NT) + dot(hi, clo, NT)
    return dot(hi, chi, NT) + (dot(hi, cmid, NT) + dot(mid, chi, NT) + small)


def near_kernel(x_ref, pieces_ref, norms_ref, out_ref):
    x = x_ref[:, :D]
    rows = x_ref[:, D:].astype(I32)
    square = jnp.sum(x * x, axis=1, keepdims=True)
    table = square - 2.0 * scores(x, pieces_ref) + norms_ref[0:1, :]
    out_ref[...] = lookup(table, rows)


def loss_kernel(p_ref, x_ref, near_ref, pieces_ref, out_ref):
    x = x_ref[:, :D]
    rows = x_ref[:, D:].astype(I32)
    r = x - p_ref[...]
    rx = jnp.sum(r * x, axis=1, keepdims=True)
    rr = jnp.sum(r * r, axis=1, keepdims=True)
    gap = rx - lookup(scores(r, pieces_ref), rows)
    loss = (near_ref[...] + amplify * gap * gap / (rr + tiny)) / D
    loss = loss.reshape(COLS, 2, NZ, 128)
    second = pltpu.roll(loss[:, 1].reshape(COLS * NZ, 128), GSIZE, 1)
    first = loss[:, 0].reshape(COLS * NZ, 128)
    out_ref[...] = jnp.where(iota((COLS * NZ, 128), 1) < GSIZE, first, second)


def collect_kernel(owner_ref, in_ref, out_ref):
    lane = iota((V, 128), 1)
    hits = [owner_ref[:, g : g + 1] == lane for g in range(GROUPS)]
    rank = dot(before_same_block(V), bits(hits[0] | hits[1] | hits[2] | hits[3]).astype(BF16))
    a = in_ref[...]
    plain, rolled = split3(a), split3(pltpu.roll(a, GSIZE, 1))
    for h in range(2):
        halves = []
        for g in (2 * h, 2 * h + 1):
            first = bits(hits[g] & (rank == 0.0)).astype(BF16)
            second = bits(hits[g] & (rank == 1.0)).astype(BF16)
            if g % 2 == 0:
                halves.append(pick(first, plain) + pick(second, rolled))
            else:
                halves.append(pick(first, rolled) + pick(second, plain))
        out_ref[:, 128 * h : 128 * h + 128] = jnp.where(lane < GSIZE, halves[0], halves[1])


def swap(a, axes):
    return lax.all_to_all(a, axes, split_axis=0, concat_axis=0, tiled=True)


def shards(new_vectors, centroids, primary_owner, primary_row, cand_owner, cand_row):
    plane = ("y", "x")
    me = lax.axis_index("z").astype(I32).reshape(1)
    info = jnp.concatenate([primary_owner, primary_row, cand_owner], axis=1)
    info = jnp.pad(info, ((0, 0), (0, 128 - info.shape[1])))
    with jax.named_scope("column_info"):
        info = swap(jnp.broadcast_to(info[None], (NZ, V, 128)), "z").reshape(COLV, 128)
    with jax.named_scope("column_vectors"):
        wide = jnp.concatenate([new_vectors, cand_row.astype(F32)], axis=1)
        column = swap(jnp.broadcast_to(wide[None], (NZ,) + wide.shape), "z").reshape(COLV, D + 256)
    pieces, norms = call(
        prepare_kernel, [shape((3, ROWS, D), BF16), shape((8, ROWS))], centroids, name="prepare"
    )
    with jax.named_scope("requests"):
        asks = call(request_kernel, shape((COLS, NZ, 128), I32), me, info, smem=(0,), name="request")
        asked = swap(asks, plane).reshape(COLS * NZ, 128)
    slots = call(slots_kernel, shape((GROUPS, SLOTS, COLV)), me, info, smem=(0,), name="slots")

    def relay(turn):
        return call(
            relay_kernel,
            [shape((NZ * K, SLOTS), BF16), shape((SLOTS, NZ * K), BF16)],
            me,
            turn.reshape(1),
            info,
            slots,
            smem=(0, 1),
            name="relay",
        )

    send, take = relay(jnp.int32(0))
    with jax.named_scope("primary_rows"):
        found, most = call(
            fetch_kernel, [shape((COLS, 16, D)), shape((8, 128), I32)], asked, pieces, name="fetch"
        )
        fetched = swap(found, plane).reshape(SLOTS, D)
        most = most[0, 0]
        most = jnp.maximum(most, lax.ppermute(most.reshape(1, 1), "rep", [(0, 1), (1, 0)])[0, 0])

    def across(send, take):
        out = call(move_kernel, shape((NZ * K, D)), send, fetched, name="send")
        got = swap(out.reshape(NZ, K, D), "z").reshape(NZ * K, D)
        return call(move_kernel, shape((SLOTS, D)), take, got, name="take")

    def more(state):
        turn, total = state
        return turn + 1, total + across(*relay(turn))

    with jax.named_scope("primary_across"):
        primaries = across(send, take)
        _, primaries = lax.while_loop(lambda s: s[0] * K < most, more, (jnp.int32(1), primaries))
    with jax.named_scope("vectors_out"):
        vectors = call(vectors_kernel, shape((SLOTS, D + 128)), slots, column, name="vectors")
        vectors = swap(vectors.reshape(COLS, 16, D + 128), plane).reshape(SLOTS, D + 128)
    near = call(near_kernel, shape((SLOTS, 128)), vectors, pieces, norms, name="near")
    with jax.named_scope("primaries_out"):
        primaries = swap(primaries.reshape(COLS, 16, D), plane).reshape(SLOTS, D)
    losses = call(loss_kernel, shape((COLS * NZ, 128)), primaries, vectors, near, pieces, name="loss")
    with jax.named_scope("losses_back"):
        back = swap(losses.reshape(COLS * NZ, 1, 128), ("y", "x", "z")).reshape(COLS * NZ, 128)
    return call(collect_kernel, shape((V, GROUPS * GSIZE)), cand_owner, back, name="collect")


def solution(mesh):
    fine = Mesh(mesh.devices.reshape(NY, NX, NZ, 2), ("y", "x", "z", "rep"))
    rows = P(("y", "x", "z", "rep"), None)
    in_specs = (rows, P(("y", "x", "z"), None), rows, rows, rows, rows)
    return jax.shard_map(shards, mesh=fine, in_specs=in_specs, out_specs=rows, check_vma=False)
```

time: 498 us -> 188 us (0.38)
  local copies, waits for them, and re-layouts: 376 us -> 10.8 us
  waiting for transfers between devices: 31.5 us -> 94.9 us
  blocking collectives: 51 us -> 20.9 us
  Pallas kernels: 0 us -> 17.9 us
  starting transfers between devices: 24.7 us -> 40.1 us
  other arithmetic: 7.86 us -> 0.73 us
  matrix products: 5.66 us -> 0 us
    gather x9 -> x0, local copies, waits for them, and re-layouts: 365 us -> none  [the longest x3 130 us: shards(): cross_x = jnp.take_along_axis(scores[:total], row_ids, axis=1)]
    all_to_all x3 -> x7, waiting for transfers between devices: 31.5 us -> 93.6 us  [swap(): return lax.all_to_all(a, axes, split_axis=0, concat_axis=0, tiled=True)]
    all_to_all x2 -> x1, blocking collectives: 51 us -> 20.9 us  [swap(): return lax.all_to_all(a, axes, split_axis=0, concat_axis=0, tiled=True)]
    pallas_call x0 -> x11, Pallas kernels: none -> 17.9 us  [call(): pl.pallas_call(kernel, out_shape=out_shape, in_specs=specs, out_specs=[VM...]
    all_to_all x3 -> x7, starting transfers between devices: 24.7 us -> 40.1 us  [swap(): return lax.all_to_all(a, axes, split_axis=0, concat_axis=0, tiled=True)]
    unnamed x15 -> x34, local copies, waits for them, and re-layouts: 1.29 us -> 8.29 us
    dot_general x5 -> x0, matrix products: 5.66 us -> none  [the longest x1 3.55 us: shards(): jnp.einsum('md,cd->mc', stacked, centroids, precision=lax.Precision.HIGHEST)]
    reshape x5 -> x0, local copies, waits for them, and re-layouts: 5.54 us -> none  [the longest x1 3.66 us: shards(): flat = arrived.reshape(total, 2 * width)]
  transfers between devices with their start and end apart: 3 -> 8, of which waited for: 2 -> 8; matrix products, arithmetic and copies ran while one was open for 22% -> 0% of each run, Pallas kernels for 0% -> 4%
where the time goes in v1:
time: 188 us; the launch traced here: 187 us
  waiting for transfers between devices  94.9 us (50%)
  starting transfers between devices  40.1 us (21%)
  blocking collectives  20.9 us (11%)
  Pallas kernels  17.9 us (10%)
  local copies, waits for them, and re-layouts  10.8 us (6%)
    all_to_all x7, waiting for transfers between devices, swap(): return lax.all_to_all(a, axes, split_axis=0, concat_axis=0, tiled=True)  93.6 us
    all_to_all x7, starting transfers between devices, swap(): return lax.all_to_all(a, axes, split_axis=0, concat_axis=0, tiled=True)  40.1 us
    all_to_all x1, blocking collectives, swap(): return lax.all_to_all(a, axes, split_axis=0, concat_axis=0, tiled=True)  20.9 us
    pallas_call x11, Pallas kernels, call(): pl.pallas_call(kernel, out_shape=out_shape, in_specs=specs, out_specs=[VM...  17.9 us
    unnamed x34, local copies, waits for them, and re-layouts  8.29 us
  transfers between devices with their start and end apart: 8, of which 8 were waited for; matrix products, arithmetic and copies ran while one was open for 0% of the time, Pallas kernels for 4%

profile of v1, /device:TPU:2, one launch (start us, length us, event | category | flops | bytes accessed | tf_op | source)
XLA Modules:
  0.0 186.7 jit_solution(15316705561020394163)
XLA Ops:
  1.5 8.5 %all-to-all-start.1 = ((s32[8,32,128]{2,1,0:T(8,128)}), s32[8,32,128]{2,1,0:T(8,128)S(1)}, u32[]{:S(2)}, u32[]{:S(2)}) async-start(s32[8,32,128]{2,1,0:T(8,128)} %broadcast_in_dim.4), calls=%async_computation.1 | async-start | bytes 262144 | tf_op jit(solution)/shard_map/column_info/all_to_all | solution.py:254
  9.9 9.1 %all-to-all-done.1 = s32[8,32,128]{2,1,0:T(8,128)S(1)} async-done(((s32[8,32,128]{2,1,0:T(8,128)}), s32[8,32,128]{2,1,0:T(8,128)S(1)}, u32[]{:S(2)}, u32[]{:S(2)}) %all-to-all-start.1) | async-done | bytes 131104 | tf_op jit(solution)/shard_map/column_info/all_to_all | solution.py:254
  19.0 1.8 request.1
  20.8 7.5 %all-to-all-start.2 = ((s32[16,8,128]{2,1,0:T(8,128)}), s32[16,8,128]{2,1,0:T(8,128)S(1)}, u32[]{:S(2)}, u32[]{:S(2)}) async-start(s32[16,8,128]{2,1,0:T(8,128)} %request.1), calls=%async_computation.2 | async-start | bytes 131072 | tf_op jit(solution)/shard_map/requests/all_to_all | solution.py:254
  28.3 1.6 copy-done.5
  29.8 1.5 prepare.1
  31.3 3.3 %all-to-all-done.2 = s32[16,8,128]{2,1,0:T(8,128)S(1)} async-done(((s32[16,8,128]{2,1,0:T(8,128)}), s32[16,8,128]{2,1,0:T(8,128)S(1)}, u32[]{:S(2)}, u32[]{:S(2)}) %all-to-all-start.2) | async-done | bytes 65568 | tf_op jit(solution)/shard_map/requests/all_to_all | solution.py:254
  36.6 5.0 %all-to-all-start.3 = ((f32[16,16,1024]{2,1,0:T(8,128)}), f32[16,16,1024]{2,1,0:T(8,128)S(1)}, u32[]{:S(2)}, u32[]{:S(2)}) async-start(f32[16,16,1024]{2,1,0:T(8,128)} %copy-done.6), calls=%async_computation.3 | async-start | bytes 2097152 | tf_op jit(solution)/shard_map/primary_rows/all_to_all | solution.py:254
  41.7 13.8 %all-to-all-done.3 = f32[16,16,1024]{2,1,0:T(8,128)S(1)} async-done(((f32[16,16,1024]{2,1,0:T(8,128)}), f32[16,16,1024]{2,1,0:T(8,128)S(1)}, u32[]{:S(2)}, u32[]{:S(2)}) %all-to-all-start.3) | async-done | bytes 1048608 | tf_op jit(solution)/shard_map/primary_rows/all_to_all | solution.py:254
  55.5 1.3 broadcast_in_dim.5
  56.8 3.7 %all-to-all-start.6 = ((f32[8,32,1280]{2,1,0:T(8,128)}), f32[8,32,1280]{2,1,0:T(8,128)S(1)}, u32[]{:S(2)}, u32[]{:S(2)}) async-start(f32[8,32,1280]{2,1,0:T(8,128)} %broadcast_in_dim.5), calls=%async_computation.6 | async-start | bytes 2621440 | tf_op jit(solution)/shard_map/column_vectors/all_to_all | solution.py:254
  63.3 1.6 send.2
  64.9 26.4 %all-to-all-done.6 = f32[8,32,1280]{2,1,0:T(8,128)S(1)} async-done(((f32[8,32,1280]{2,1,0:T(8,128)}), f32[8,32,1280]{2,1,0:T(8,128)S(1)}, u32[]{:S(2)}, u32[]{:S(2)}) %all-to-all-start.6) | async-done | bytes 1310752 | tf_op jit(solution)/shard_map/column_vectors/all_to_all | solution.py:254
  91.4 3.6 %all-to-all-start.4 = ((f32[8,32,1024]{2,1,0:T(8,128)}), f32[8,32,1024]{2,1,0:T(8,128)S(1)}, u32[]{:S(2)}, u32[]{:S(2)}) async-start(f32[8,32,1024]{2,1,0:T(8,128)} %bitcast.7), calls=%async_computation.4 | async-start | bytes 2097152 | tf_op jit(solution)/shard_map/primary_across/all_to_all | solution.py:254
  95.4 1.3 collective-permute-done
  98.0 2.4 %vectors.1 = f32[256,1152]{1,0:T(8,128)S(1)} custom-call(f32[4,256,256]{2,1,0:T(8,128)} %copy-done.7, f32[256,1280]{1,0:T(8,128)S(1)} %bitcast.28), custom_call_target="tpu_custom_call" | custom-call | tf_op jit(solution)/shard_map/vectors_out/vectors/pallas_call | solution.py:32
  101.4 19.6 %all-to-all-done.4 = f32[8,32,1024]{2,1,0:T(8,128)S(1)} async-done(((f32[8,32,1024]{2,1,0:T(8,128)}), f32[8,32,1024]{2,1,0:T(8,128)S(1)}, u32[]{:S(2)}, u32[]{:S(2)}) %all-to-all-start.4) | async-done | bytes 1048608 | tf_op jit(solution)/shard_map/primary_across/all_to_all | solution.py:254
  122.6 20.9 %all_to_all.46 = f32[16,16,1152]{2,1,0:T(8,128)} all-to-all(f32[16,16,1152]{2,1,0:T(8,128)} %bitcast.29), channel_id=1, replica_groups=mesh['y'=4,'x'=4,'z'=8,'rep'=2] {'y','x'}, dimensions={0} | all-to-all | bytes 2359296 | tf_op jit(solution)/shard_map/vectors_out/all_to_all | solution.py:254
  143.6 5.5 %all-to-all-start.5 = ((f32[16,16,1024]{2,1,0:T(8,128)}), f32[16,16,1024]{2,1,0:T(8,128)}, u32[]{:S(2)}, u32[]{:S(2)}) async-start(f32[16,16,1024]{2,1,0:T(8,128)} %bitcast.33), calls=%async_computation.5 | async-start | bytes 2097152 | tf_op jit(solution)/shard_map/primaries_out/all_to_all | solution.py:254
  150.4 2.1 %near.1.near_ref = f32[256,128]{1,0:T(8,128)S(1)} custom-call(f32[256,1152]{1,0:T(8,128)S(1)} %bitcast.26, bf16[3,512,1024]{2,1,0:T(8,128)(2,1)S(1)} %copy-done.1, f32[8,512]{1,0:T(8,128)S(1)} %get-tuple-element.57.norms_ref), custom_call_target="tpu_custom_call" | custom-call | tf_op jit(solution)/shard_map/near/pallas_call | solution.py:32
  152.5 10.4 %all-to-all-done.5 = f32[16,16,1024]{2,1,0:T(8,128)} async-done(((f32[16,16,1024]{2,1,0:T(8,128)}), f32[16,16,1024]{2,1,0:T(8,128)}, u32[]{:S(2)}, u32[]{:S(2)}) %all-to-all-start.5) | async-done | bytes 1048608 | tf_op jit(solution)/shard_map/primaries_out/all_to_all | solution.py:254
  164.1 4.0 %loss.1 = f32[128,128]{1,0:T(8,128)} custom-call(f32[256,1024]{1,0:T(8,128)} %bitcast.11.p_ref, f32[256,1152]{1,0:T(8,128)S(1)} %bitcast.27, f32[256,128]{1,0:T(8,128)S(1)} %near.1.near_ref, bf16[3,512,1024]{2,1,0:T(8,128)(2,1)S(1)} %copy-done.1), custom_call_target="tpu_custom_call" | custom-call | tf_op jit(solution)/shard_map/loss/pallas_call | solution.py:32
  168.2 6.3 %all-to-all-start.8 = ((f32[128,1,128]{2,1,0:T(1,128)}), f32[128,1,128]{2,1,0:T(1,128)S(1)}, u32[]{:S(2)}, u32[]{:S(2)}) async-start(f32[128,1,128]{2,1,0:T(1,128)} %bitcast.16), calls=%async_computation.8 | async-start | bytes 131072 | tf_op jit(solution)/shard_map/losses_back/all_to_all | solution.py:254
  174.6 11.0 %all-to-all-done.8 = f32[128,1,128]{2,1,0:T(1,128)S(1)} async-done(((f32[128,1,128]{2,1,0:T(1,128)}), f32[128,1,128]{2,1,0:T(1,128)S(1)}, u32[]{:S(2)}, u32[]{:S(2)}) %all-to-all-start.8) | async-done | bytes 65568 | tf_op jit(solution)/shard_map/losses_back/all_to_all | solution.py:254
  (46 shorter events, 13.2 us)
Async XLA Ops:
  1.5 17.6 %all-to-all-start.1 = ((s32[8,32,128]{2,1,0:T(8,128)}), s32[8,32,128]{2,1,0:T(8,128)S(1)}, u32[]{:S(2)}, u32[]{:S(2)}) async-start(s32[8,32,128]{2,1,0:T(8,128)} %broadcast_in_dim.4), calls=%async_computation.1 | async-start | bytes 262144 | tf_op jit(solution)/shard_map/column_info/all_to_all | solution.py:254
  19.0 1.8 copy-start.13
  20.8 13.8 %all-to-all-start.2 = ((s32[16,8,128]{2,1,0:T(8,128)}), s32[16,8,128]{2,1,0:T(8,128)S(1)}, u32[]{:S(2)}, u32[]{:S(2)}) async-start(s32[16,8,128]{2,1,0:T(8,128)} %request.1), calls=%async_computation.2 | async-start | bytes 131072 | tf_op jit(solution)/shard_map/requests/all_to_all | solution.py:254
  28.3 1.6 copy-start.5
  31.3 4.3 %copy-start = (bf16[3,512,1024]{2,1,0:T(8,128)(2,1)}, bf16[3,512,1024]{2,1,0:T(8,128)(2,1)S(1)}, u32[]{:S(2)}) copy-start(bf16[3,512,1024]{2,1,0:T(8,128)(2,1)S(1)} %get-tuple-element.53.pieces_ref) | copy-start | bytes 9437188
  35.6 1.0 copy-start.6
  36.6 5.0 %copy-start.16 = (s32[32,256]{1,0:T(8,128)S(1)}, s32[32,256]{1,0:T(8,128)}, u32[]{:S(2)}) copy-start(s32[32,256]{1,0:T(8,128)} %param.13) | copy-start | bytes 98308
  36.6 5.0 %copy-start.15 = (f32[32,1024]{1,0:T(8,128)S(1)}, f32[32,1024]{1,0:T(8,128)}, u32[]{:S(2)}) copy-start(f32[32,1024]{1,0:T(8,128)} %param.8) | copy-start | bytes 393220
  36.6 18.9 %all-to-all-start.3 = ((f32[16,16,1024]{2,1,0:T(8,128)}), f32[16,16,1024]{2,1,0:T(8,128)S(1)}, u32[]{:S(2)}, u32[]{:S(2)}) async-start(f32[16,16,1024]{2,1,0:T(8,128)} %copy-done.6), calls=%async_computation.3 | async-start | bytes 2097152 | tf_op jit(solution)/shard_map/primary_rows/all_to_all | solution.py:254
  55.5 7.8 %copy-start.11 = (f32[16,16,1024]{2,1,0:T(8,128)}, f32[16,16,1024]{2,1,0:T(8,128)S(1)}, u32[]{:S(2)}) copy-start(f32[16,16,1024]{2,1,0:T(8,128)S(1)} %all-to-all-done.3) | copy-start | bytes 3145732
  56.8 3.7 %copy-start.14 = (s32[8,32,128]{2,1,0:T(8,128)S(1)}, s32[8,32,128]{2,1,0:T(8,128)}, u32[]{:S(2)}) copy-start(s32[8,32,128]{2,1,0:T(8,128)} %copy-done.13) | copy-start | bytes 393220
  56.8 34.6 %all-to-all-start.6 = ((f32[8,32,1280]{2,1,0:T(8,128)}), f32[8,32,1280]{2,1,0:T(8,128)S(1)}, u32[]{:S(2)}, u32[]{:S(2)}) async-start(f32[8,32,1280]{2,1,0:T(8,128)} %broadcast_in_dim.5), calls=%async_computation.6 | async-start | bytes 2621440 | tf_op jit(solution)/shard_map/column_vectors/all_to_all | solution.py:254
  61.2 1.0 copy-start.7
  91.4 29.6 %all-to-all-start.4 = ((f32[8,32,1024]{2,1,0:T(8,128)}), f32[8,32,1024]{2,1,0:T(8,128)S(1)}, u32[]{:S(2)}, u32[]{:S(2)}) async-start(f32[8,32,1024]{2,1,0:T(8,128)} %bitcast.7), calls=%async_computation.4 | async-start | bytes 2097152 | tf_op jit(solution)/shard_map/primary_across/all_to_all | solution.py:254
  95.4 1.3 collective-permute-start
  100.3 1.0 copy-start.4
  101.4 20.2 %copy-start.8 = (f32[4,256,256]{2,1,0:T(8,128)S(1)}, f32[4,256,256]{2,1,0:T(8,128)}, u32[]{:S(2)}) copy-start(f32[4,256,256]{2,1,0:T(8,128)} %copy-done.7) | copy-start | bytes 3145732
  121.6 1.0 copy-start.10
  122.6 26.5 %copy-start.1 = (bf16[3,512,1024]{2,1,0:T(8,128)(2,1)S(1)}, bf16[3,512,1024]{2,1,0:T(8,128)(2,1)}, u32[]{:S(2)}) copy-start(bf16[3,512,1024]{2,1,0:T(8,128)(2,1)} %copy-done) | copy-start | bytes 9437188
  143.6 19.3 %all-to-all-start.5 = ((f32[16,16,1024]{2,1,0:T(8,128)}), f32[16,16,1024]{2,1,0:T(8,128)}, u32[]{:S(2)}, u32[]{:S(2)}) async-start(f32[16,16,1024]{2,1,0:T(8,128)} %bitcast.33), calls=%async_computation.5 | async-start | bytes 2097152 | tf_op jit(solution)/shard_map/primaries_out/all_to_all | solution.py:254
  149.1 1.3 copy-start.2
  162.9 1.3 copy-start.3
  164.1 10.4 %copy-start.17 = (s32[32,4]{0,1:T(4,128)S(1)}, s32[32,4]{0,1:T(4,128)}, u32[]{:S(2)}) copy-start(s32[32,4]{0,1:T(4,128)} %param.12) | copy-start | bytes 1540
  168.2 17.4 %all-to-all-start.8 = ((f32[128,1,128]{2,1,0:T(1,128)}), f32[128,1,128]{2,1,0:T(1,128)S(1)}, u32[]{:S(2)}, u32[]{:S(2)}) async-start(f32[128,1,128]{2,1,0:T(1,128)} %bitcast.16), calls=%async_computation.8 | async-start | bytes 131072 | tf_op jit(solution)/shard_map/losses_back/all_to_all | solution.py:254

commit v2 on v1

--- a/solution.py
+++ b/solution.py
@@ -21,20 +21,23 @@
 F32, BF16, I32 = jnp.float32, jnp.bfloat16, jnp.int32
 VMEM = pl.BlockSpec(memory_space=pltpu.VMEM)
 SMEM = pl.BlockSpec(memory_space=pltpu.SMEM)
+ANY = pl.BlockSpec(memory_space=pl.ANY)
 NN = (((1,), (0,)), ((), ()))
 NT = (((1,), (1,)), ((), ()))
 TN = (((0,), (0,)), ((), ()))
 
 
-def call(kernel, out_shape, *operands, smem=(), name=None):
-    specs = [SMEM if i in smem else VMEM for i in range(len(operands))]
+def call(kernel, out_shape, *operands, smem=(), outside=(), scratch=(), far=False, name=None):
+    specs = [SMEM if i in smem else ANY if i in outside else VMEM for i in range(len(operands))]
     many = isinstance(out_shape, (list, tuple))
+    out_spec = ANY if far else VMEM
     return pl.pallas_call(
         kernel,
         out_shape=out_shape,
         in_specs=specs,
-        out_specs=[VMEM] * len(out_shape) if many else VMEM,
-        compiler_params=pltpu.CompilerParams(vmem_limit_bytes=48 * 2**20),
+        out_specs=[out_spec] * len(out_shape) if many else out_spec,
+        scratch_shapes=list(scratch),
+        compiler_params=pltpu.CompilerParams(vmem_limit_bytes=24 * 2**20),
         name=name,
     )(*operands)
 
@@ -86,8 +89,27 @@
     norms_ref[...] = sum(dot(ones, s, NT) for s in squares)
 
 
-def request_kernel(me_ref, info_ref, out_ref):
+def info_kernel(owner_ref, row_ref, cand_ref, out_ref):
+    tile = jnp.concatenate(
+        [owner_ref[...], row_ref[...], cand_ref[...], jnp.zeros((2, V), I32)], axis=0
+    )
+    tile = jnp.concatenate([tile, jnp.zeros((8, 128 - V), I32)], axis=1)
+    for z in range(NZ):
+        out_ref[z] = tile
+
+
+def unpack_kernel(tiles_ref, out_ref):
+    quarters = []
+    for h in range(2):
+        quarters.append(jnp.concatenate([tiles_ref[4 * h + i][:, :V] for i in range(4)], axis=1))
+    wide = jnp.concatenate(quarters, axis=1)
+    wide = jnp.concatenate([wide, jnp.zeros((120, COLV), I32)], axis=0)
+    out_ref[...] = wide.T
+
+
+def request_kernel(me_ref, tiles_ref, out_ref, info_ref):
     me = me_ref[0]
+    unpack_kernel(tiles_ref, info_ref)
     lane = iota((COLV, 128), 1)
     owner = info_ref[:, 0:1]
     row = info_ref[:, 1:2].astype(F32)
@@ -147,7 +169,7 @@
     to_me = u < 0
     for g in range(GROUPS):
         plane = info_ref[:, 2 + g : 3 + g] & 7
-        wanted = wanted | (plane == lane)
+        wanted = wanted | (((plane - me) & 7) == lane)
         to_me = to_me | (plane == me)
     earlier = before_all(COLV)
     leaves = wanted & (lane < NZ) & here
@@ -158,7 +180,7 @@
     slot = (owner >> 3) * 16 + rank.astype(I32) * 8 + (u >> 5)
     held = bits((slot == iota((COLV, SLOTS), 1)) & here)
     send_ref[...] = dot(rows.astype(BF16), held.astype(BF16)).astype(BF16)
-    comes = ((owner & 7) == lane) & (lane < NZ) & to_me
+    comes = (((me - owner) & 7) == lane) & (lane < NZ) & to_me
     order = dot(earlier, bits(comes).astype(BF16)) - base
     fits = comes & (order >= 0.0) & (order < float(K))
     at = jnp.sum(jnp.where(fits, lane.astype(F32) * K + order + 1.0, 0.0), axis=1, keepdims=True)
@@ -167,18 +189,58 @@
     take_ref[...] = dot(all_slots.astype(BF16), found).astype(BF16)
 
 
-def fetch_kernel(asked_ref, pieces_ref, out_ref, most_ref):
+def fetch_kernel(asked_ref, pieces_ref, *rest):
+    out_ref, most_ref, hold, small, sems = rest[-5:]
     column = iota((COLS * NZ, ROWS), 1)
     pieces = [pieces_ref[i] for i in range(3)]
+    copies = []
     for k in range(2):
         onehot = bits(asked_ref[:, k : k + 1] == column).astype(BF16)
-        out_ref[:, k * 8 : k * 8 + 8, :] = pick(onehot, pieces).reshape(COLS, 8, D)
+        hold[k] = pick(onehot, pieces).reshape(COLS, 8, D)
+        copies.append(
+            pltpu.make_async_copy(hold.at[k], out_ref.at[:, pl.ds(k * 8, 8), :], sems.at[k])
+        )
+        copies[-1].start()
     most = jnp.max(asked_ref[:, 2:3].astype(F32)).astype(I32)
-    most_ref[...] = jnp.full((8, 128), most, I32)
-
-
-def move_kernel(onehot_ref, in_ref, out_ref):
-    out_ref[...] = pick(onehot_ref[...], split3(in_ref[...]))
+    small[...] = jnp.full((8, 128), most, I32)
+    copies.append(pltpu.make_async_copy(small, most_ref, sems.at[2]))
+    copies[-1].start()
+    for copy in copies:
+        copy.wait()
+
+
+def send_kernel(onehot_ref, in_ref, *rest):
+    outs, hold, sems = rest[-NZ - 2 : -2], rest[-2], rest[-1]
+    onehot = onehot_ref[...]
+    copies = []
+    for c in range(2):
+        cut = slice(c * D // 2, (c + 1) * D // 2)
+        hold[c] = pick(onehot, split3(in_ref[:, cut]))
+        for d in range(NZ):
+            copies.append(
+                pltpu.make_async_copy(
+                    hold.at[c, pl.ds(d * K, K), :], outs[d].at[:, pl.ds(c * D // 2, D // 2)], sems.at[c, d]
+                )
+            )
+            copies[-1].start()
+    for copy in copies:
+        copy.wait()
+
+
+def take_kernel(onehot_ref, *rest):
+    parts, out_ref, hold, sems = rest[:NZ], rest[NZ], rest[NZ + 1], rest[NZ + 2]
+    onehot = onehot_ref[...]
+    copies = []
+    for c in range(2):
+        cut = slice(c * D // 2, (c + 1) * D // 2)
+        got = jnp.concatenate([p[:, cut] for p in parts], axis=0)
+        hold[c] = pick(onehot, split3(got))
+        copies.append(
+            pltpu.make_async_copy(hold.at[c], out_ref.at[:, pl.ds(c * D // 2, D // 2)], sems.at[c])
+        )
+        copies[-1].start()
+    for copy in copies:
+        copy.wait()
 
 
 def vectors_kernel(slots_ref, in_ref, out_ref):
@@ -257,18 +319,32 @@
 def shards(new_vectors, centroids, primary_owner, primary_row, cand_owner, cand_row):
     plane = ("y", "x")
     me = lax.axis_index("z").astype(I32).reshape(1)
-    info = jnp.concatenate([primary_owner, primary_row, cand_owner], axis=1)
-    info = jnp.pad(info, ((0, 0), (0, 128 - info.shape[1])))
+    half = pltpu.VMEM((2, SLOTS, D // 2), F32)
     with jax.named_scope("column_info"):
-        info = swap(jnp.broadcast_to(info[None], (NZ, V, 128)), "z").reshape(COLV, 128)
+        tiles = call(
+            info_kernel,
+            shape((NZ, 8, 128), I32),
+            primary_owner.T,
+            primary_row.T,
+            cand_owner.T,
+            name="info",
+        )
+        tiles = swap(tiles, "z")
     with jax.named_scope("column_vectors"):
         wide = jnp.concatenate([new_vectors, cand_row.astype(F32)], axis=1)
-        column = swap(jnp.broadcast_to(wide[None], (NZ,) + wide.shape), "z").reshape(COLV, D + 256)
+        column = lax.all_gather(wide, "z", axis=0, tiled=True)
     pieces, norms = call(
         prepare_kernel, [shape((3, ROWS, D), BF16), shape((8, ROWS))], centroids, name="prepare"
     )
     with jax.named_scope("requests"):
-        asks = call(request_kernel, shape((COLS, NZ, 128), I32), me, info, smem=(0,), name="request")
+        asks, info = call(
+            request_kernel,
+            [shape((COLS, NZ, 128), I32), shape((COLV, 128), I32)],
+            me,
+            tiles,
+            smem=(0,),
+            name="request",
+        )
         asked = swap(asks, plane).reshape(COLS * NZ, 128)
     slots = call(slots_kernel, shape((GROUPS, SLOTS, COLV)), me, info, smem=(0,), name="slots")
 
@@ -287,28 +363,59 @@
     send, take = relay(jnp.int32(0))
     with jax.named_scope("primary_rows"):
         found, most = call(
-            fetch_kernel, [shape((COLS, 16, D)), shape((8, 128), I32)], asked, pieces, name="fetch"
+            fetch_kernel,
+            [shape((COLS, 16, D)), shape((8, 128), I32)],
+            asked,
+            pieces,
+            send,
+            take,
+            outside=(2, 3),
+            far=True,
+            scratch=[
+                pltpu.VMEM((2, COLS, 8, D), F32),
+                pltpu.VMEM((8, 128), I32),
+                pltpu.SemaphoreType.DMA((3,)),
+            ],
+            name="fetch",
         )
         fetched = swap(found, plane).reshape(SLOTS, D)
         most = most[0, 0]
         most = jnp.maximum(most, lax.ppermute(most.reshape(1, 1), "rep", [(0, 1), (1, 0)])[0, 0])
 
     def across(send, take):
-        out = call(move_kernel, shape((NZ * K, D)), send, fetched, name="send")
-        got = swap(out.reshape(NZ, K, D), "z").reshape(NZ * K, D)
-        return call(move_kernel, shape((SLOTS, D)), take, got, name="take")
+        parts = call(
+            send_kernel,
+            [shape((K, D))] * NZ,
+            send,
+            fetched,
+            far=True,
+            scratch=[half, pltpu.SemaphoreType.DMA((2, NZ))],
+            name="send",
+        )
+        got = [parts[0]]
+        for d in range(1, NZ):
+            got.append(lax.ppermute(parts[d], "z", [(z, (z + d) % NZ) for z in range(NZ)]))
+        return call(
+            take_kernel,
+            shape((SLOTS, D)),
+            take,
+            *got,
+            far=True,
+            scratch=[half, pltpu.SemaphoreType.DMA((2,))],
+            name="take",
+        )
 
     def more(state):
         turn, total = state
         return turn + 1, total + across(*relay(turn))
 
-    with jax.named_scope("primary_across"):
-        primaries = across(send, take)
-        _, primaries = lax.while_loop(lambda s: s[0] * K < most, more, (jnp.int32(1), primaries))
     with jax.named_scope("vectors_out"):
         vectors = call(vectors_kernel, shape((SLOTS, D + 128)), slots, column, name="vectors")
         vectors = swap(vectors.reshape(COLS, 16, D + 128), plane).reshape(SLOTS, D + 128)
     near = call(near_kernel, shape((SLOTS, 128)), vectors, pieces, norms, name="near")
+    with jax.named_scope("primary_across"):
+        primaries = across(send, take)
+        _, primaries = lax.while_loop(lambda s: s[0] * K < most, more, (jnp.int32(1), primaries))
     with jax.named_scope("primaries_out"):
         primaries = swap(primaries.reshape(COLS, 16, D), plane).reshape(SLOTS, D)
     losses = call(loss_kernel, shape((COLS * NZ, 128)), primaries, vectors, near, pieces, name="loss")

time: 188 us -> 165 us (0.88)
  waiting for transfers between devices: 94.9 us -> 51.2 us
  blocking collectives: 20.9 us -> 0 us
  starting transfers between devices: 40.1 us -> 59.5 us
  between operations: 1.44 us -> 14.7 us
  Pallas kernels: 17.9 us -> 25 us
    all_to_all x7 -> x6, waiting for transfers between devices: 93.6 us -> 37.3 us  [swap(): return lax.all_to_all(a, axes, split_axis=0, concat_axis=0, tiled=True)]
    all_to_all x1 -> x0, blocking collectives: 20.9 us -> none  [swap(): return lax.all_to_all(a, axes, split_axis=0, concat_axis=0, tiled=True)]
    ppermute x0 -> x7, waiting for transfers between devices: none -> 14 us  [across(): lax.ppermute(parts[d], 'z', [(z, (z + d) % NZ) for z in range(NZ)])]
    ppermute x0 -> x7, starting transfers between devices: none -> 12.6 us  [across(): lax.ppermute(parts[d], 'z', [(z, (z + d) % NZ) for z in range(NZ)])]
    pallas_call x11 -> x12, Pallas kernels: 17.9 us -> 25 us  [call(): pl.pallas_call(kernel, out_shape=out_shape, in_specs=specs, out_specs=[ou...]
    all_to_all x7 -> x6, starting transfers between devices: 40.1 us -> 46.9 us  [swap(): return lax.all_to_all(a, axes, split_axis=0, concat_axis=0, tiled=True)]
    broadcast_in_dim x2 -> x0, local copies, waits for them, and re-layouts: 1.93 us -> none  [the longest x1 1.28 us: shards(): jnp.broadcast_to(wide[None], (NZ,) + wide.shape)]
    unnamed x34 -> x27, local copies, waits for them, and re-layouts: 8.29 us -> 9.56 us
  transfers between devices with their start and end apart: 8 -> 15, of which waited for: 8 -> 9; matrix products, arithmetic and copies ran while one was open for 0% -> 1% of each run, Pallas kernels for 4% -> 10%
where the time goes in v2:
time: 165 us; the launch traced here: 164 us
  starting transfers between devices  59.5 us (36%)
  waiting for transfers between devices  51.2 us (31%)
  Pallas kernels  25 us (15%)
  between operations  14.7 us (9%)
  local copies, waits for them, and re-layouts  10.7 us (6%)
  other arithmetic  2.34 us (1%)
    all_to_all x6, starting transfers between devices, swap(): return lax.all_to_all(a, axes, split_axis=0, concat_axis=0, tiled=True)  46.9 us
    all_to_all x6, waiting for transfers between devices, swap(): return lax.all_to_all(a, axes, split_axis=0, concat_axis=0, tiled=True)  37.3 us
    pallas_call x12, Pallas kernels, call(): pl.pallas_call(kernel, out_shape=out_shape, in_specs=specs, out_specs=[ou...  25 us
    ppermute x7, waiting for transfers between devices, across(): lax.ppermute(parts[d], 'z', [(z, (z + d) % NZ) for z in range(NZ)])  14 us
    ppermute x7, starting transfers between devices, across(): lax.ppermute(parts[d], 'z', [(z, (z + d) % NZ) for z in range(NZ)])  12.6 us
    unnamed x27, local copies, waits for them, and re-layouts  9.56 us
  transfers between devices with their start and end apart: 15, of which 9 were waited for; matrix products, arithmetic and copies ran while one was open for 1% of the time, Pallas kernels for 10%

profile of v2, /device:TPU:2, one launch (start us, length us, event | category | flops | bytes accessed | tf_op | source)
XLA Modules:
  0.0 163.5 jit_solution(8947964848892050113)
XLA Ops:
  7.3 1.6 pad_maximum_fusion
  11.5 8.5 %all-to-all-start = ((s32[8,8,128]{2,1,0:T(8,128)}), s32[8,8,128]{2,1,0:T(8,128)S(1)}, u32[]{:S(2)}, u32[]{:S(2)}) async-start(s32[8,8,128]{2,1,0:T(8,128)} %info.1), calls=%async_computation | async-start | bytes 65536 | tf_op jit(solution)/shard_map/column_info/all_to_all | solution.py:316
  20.0 8.0 %all-to-all-done.tiles_ref = s32[8,8,128]{2,1,0:T(8,128)S(1)} async-done(((s32[8,8,128]{2,1,0:T(8,128)}), s32[8,8,128]{2,1,0:T(8,128)S(1)}, u32[]{:S(2)}, u32[]{:S(2)}) %all-to-all-start) | async-done | bytes 32800 | tf_op jit(solution)/shard_map/column_info/all_to_all | solution.py:316
  28.0 1.8 %request.1 = (s32[16,8,128]{2,1,0:T(8,128)}, s32[256,128]{1,0:T(8,128)S(1)}) custom-call(s32[1]{0:T(128)} %bitcast.1.me_ref, s32[8,8,128]{2,1,0:T(8,128)S(1)} %all-to-all-done.tiles_ref), custom_call_target="tpu_custom_call" | custom-call | tf_op jit(solution)/shard_map/requests/request/pallas_call | solution.py:34
  29.8 7.5 %all-to-all-start.1 = ((s32[16,8,128]{2,1,0:T(8,128)}), s32[16,8,128]{2,1,0:T(8,128)S(1)}, u32[]{:S(2)}, u32[]{:S(2)}) async-start(s32[16,8,128]{2,1,0:T(8,128)} %get-tuple-element.72), calls=%async_computation.1 | async-start | bytes 131072 | tf_op jit(solution)/shard_map/requests/all_to_all | solution.py:316
  37.3 1.6 copy-done.3
  42.1 2.0 %relay.2 = (bf16[256,256]{1,0:T(8,128)(2,1)S(1)}, bf16[256,256]{1,0:T(8,128)(2,1)S(1)}) custom-call(s32[1]{0:T(128)} %bitcast.1.me_ref, s32[1]{0:T(128)} %constant.13.clone.1.turn_ref, s32[256,128]{1,0:T(8,128)} %copy-done.16, f32[4,256,256]{2,1,0:T(8,128)S(1)} %slots.1.slots_ref), custom_call_target="tpu_custom_call" | custom-call | tf_op jit(solution)/shard_map/relay/pallas_call | solution.py:34
  46.6 7.2 %all-to-all-start.2 = ((f32[16,16,1024]{2,1,0:T(8,128)}), f32[16,16,1024]{2,1,0:T(8,128)}, u32[]{:S(2)}, u32[]{:S(2)}) async-start(f32[16,16,1024]{2,1,0:T(8,128)} %copy-done.5), calls=%async_computation.2 | async-start | bytes 2097152 | tf_op jit(solution)/shard_map/primary_rows/all_to_all | solution.py:316
  55.1 2.4 %vectors.1 = f32[256,1152]{1,0:T(8,128)S(1)} custom-call(f32[4,256,256]{2,1,0:T(8,128)} %copy-done.13, f32[256,1280]{1,0:T(8,128)S(1)} %copy-done.4), custom_call_target="tpu_custom_call" | custom-call | tf_op jit(solution)/shard_map/vectors_out/vectors/pallas_call | solution.py:34
  58.6 9.6 %all-to-all-done.2 = f32[16,16,1024]{2,1,0:T(8,128)} async-done(((f32[16,16,1024]{2,1,0:T(8,128)}), f32[16,16,1024]{2,1,0:T(8,128)}, u32[]{:S(2)}, u32[]{:S(2)}) %all-to-all-start.2) | async-done | bytes 1048608 | tf_op jit(solution)/shard_map/primary_rows/all_to_all | solution.py:316
  68.2 5.6 %all-to-all-start.4 = ((f32[16,16,1152]{2,1,0:T(8,128)}), f32[16,16,1152]{2,1,0:T(8,128)}, u32[]{:S(2)}, u32[]{:S(2)}) async-start(f32[16,16,1152]{2,1,0:T(8,128)} %bitcast.18), calls=%async_computation.4 | async-start | bytes 2359296 | tf_op jit(solution)/shard_map/vectors_out/all_to_all | solution.py:316
  73.7 3.0 %send.2 = (f32[32,1024]{1,0:T(8,128)S(1)}, f32[32,1024]{1,0:T(8,128)}, f32[32,1024]{1,0:T(8,128)}, f32[32,1024]{1,0:T(8,128)}, f32[32,1024]{1,0:T(8,128)S(1)}, /...) custom-call(bf16[256,256]{1,0:T(8,128)(2,1)S(1)} %get-tuple-element.71.rest_0_.onehot_ref, ...), custom_call_target="tpu_custom_call" | custom-call | tf_op jit(solution)/shard_map/primary_across/send/pallas_call | solution.py:34
  77.6 4.3 %collective-permute-start.11 = (f32[32,1024]{1,0:T(8,128)S(1)}, f32[32,1024]{1,0:T(8,128)S(1)}, u32[]{:S(2)}, u32[]{:S(2)}) collective-permute-start(f32[32,1024]{1,0:T(8,128)S(1)} %get-tuple-element.80), channel_id=1, source_target_pairs={{0,10},{2,12},{4,14},{6,0},{8,2},{10,4},{12,6},{14,8},{1,11},{3,13... | collective-permute-start | bytes 393224 | tf_op jit(solution)/shard_map/primary_across/ppermute | solution.py:397
  88.0 4.7 %collective-permute-done.11.rest_5_ = f32[32,1024]{1,0:T(8,128)S(1)} collective-permute-done((f32[32,1024]{1,0:T(8,128)S(1)}, f32[32,1024]{1,0:T(8,128)S(1)}, u32[]{:S(2)}, u32[]{:S(2)}) %collective-permute-start.11) | collective-permute-done | bytes 131104 | tf_op jit(solution)/shard_map/primary_across/ppermute | solution.py:397
  93.4 2.6 %collective-permute-start.9 = (f32[32,1024]{1,0:T(8,128)}, f32[32,1024]{1,0:T(8,128)}, u32[]{:S(2)}, u32[]{:S(2)}) collective-permute-start(f32[32,1024]{1,0:T(8,128)} %get-tuple-element.78), channel_id=1, source_target_pairs={{0,6},{2,8},{4,10},{6,12},{8,14},{10,0},{12,2},{14,4},{1,7},{3,9},... | collective-permute-start | bytes 393224 | tf_op jit(solution)/shard_map/primary_across/ppermute | solution.py:397
  98.5 1.9 %collective-permute-done.8.rest_2_ = f32[32,1024]{1,0:T(8,128)} collective-permute-done((f32[32,1024]{1,0:T(8,128)}, f32[32,1024]{1,0:T(8,128)}, u32[]{:S(2)}, u32[]{:S(2)}) %collective-permute-start.8) | collective-permute-done | bytes 131104 | tf_op jit(solution)/shard_map/primary_across/ppermute | solution.py:397
  100.5 5.9 %collective-permute-done.9.rest_3_ = f32[32,1024]{1,0:T(8,128)} collective-permute-done((f32[32,1024]{1,0:T(8,128)}, f32[32,1024]{1,0:T(8,128)}, u32[]{:S(2)}, u32[]{:S(2)}) %collective-permute-start.9) | collective-permute-done | bytes 131104 | tf_op jit(solution)/shard_map/primary_across/ppermute | solution.py:397
  107.2 2.6 %take.2 = f32[256,1024]{1,0:T(8,128)} custom-call(bf16[256,256]{1,0:T(8,128)(2,1)S(1)} %get-tuple-element.70.rest_1_.onehot_ref, f32[32,1024]{1,0:T(8,128)S(1)} %get-tuple-element.75.rest_0_, f32[32,1024]{1,0:T(8,128)} %collective-permute-done.7.rest_1_, f32[32,1024]{1,0:T(8,128)} %collective-permute-done.8.rest_2_, ...), custom_call_target="tpu_custom_call" | custom-call | tf_op jit(solution)/shard_map/primary_across/take/pallas_call | solution.py:34
  109.9 7.3 %all-to-all-start.3 = ((f32[16,16,1024]{2,1,0:T(8,128)}), f32[16,16,1024]{2,1,0:T(8,128)}, u32[]{:S(2)}, u32[]{:S(2)}) async-start(f32[16,16,1024]{2,1,0:T(8,128)} %bitcast.24), calls=%async_computation.3 | async-start | bytes 2097152 | tf_op jit(solution)/shard_map/primaries_out/all_to_all | solution.py:316
  117.2 3.4 %near.1.near_ref = f32[256,128]{1,0:T(8,128)S(1)} custom-call(f32[256,1152]{1,0:T(8,128)} %bitcast.11.x_ref, bf16[3,512,1024]{2,1,0:T(8,128)(2,1)S(1)} %get-tuple-element.73.pieces_ref, f32[8,512]{1,0:T(8,128)S(1)} %get-tuple-element.85.norms_ref), custom_call_target="tpu_custom_call" | custom-call | tf_op jit(solution)/shard_map/near/pallas_call | solution.py:34
  120.6 8.6 %all-to-all-done.3 = f32[16,16,1024]{2,1,0:T(8,128)} async-done(((f32[16,16,1024]{2,1,0:T(8,128)}), f32[16,16,1024]{2,1,0:T(8,128)}, u32[]{:S(2)}, u32[]{:S(2)}) %all-to-all-start.3) | async-done | bytes 1048608 | tf_op jit(solution)/shard_map/primaries_out/all_to_all | solution.py:316
  129.3 4.4 %loss.1 = f32[128,128]{1,0:T(8,128)} custom-call(f32[256,1024]{1,0:T(8,128)} %bitcast.9.p_ref, f32[256,1152]{1,0:T(8,128)} %bitcast.11.x_ref, f32[256,128]{1,0:T(8,128)S(1)} %near.1.near_ref, bf16[3,512,1024]{2,1,0:T(8,128)(2,1)S(1)} %get-tuple-element.73.pieces_ref), custom_call_target="tpu_custom_call" | custom-call | tf_op jit(solution)/shard_map/loss/pallas_call | solution.py:34
  133.7 10.8 %all-to-all-start.5 = ((f32[128,1,128]{2,1,0:T(1,128)}), f32[128,1,128]{2,1,0:T(1,128)S(1)}, u32[]{:S(2)}, u32[]{:S(2)}) async-start(f32[128,1,128]{2,1,0:T(1,128)} %bitcast.13), calls=%async_computation.5 | async-start | bytes 131072 | tf_op jit(solution)/shard_map/losses_back/all_to_all | solution.py:316
  144.6 11.0 %all-to-all-done.5 = f32[128,1,128]{2,1,0:T(1,128)S(1)} async-done(((f32[128,1,128]{2,1,0:T(1,128)}), f32[128,1,128]{2,1,0:T(1,128)S(1)}, u32[]{:S(2)}, u32[]{:S(2)}) %all-to-all-start.5) | async-done | bytes 65568 | tf_op jit(solution)/shard_map/losses_back/all_to_all | solution.py:316
  (50 shorter events, 22.6 us)
Async XLA Ops:
  6.5 47.3 %all-gather.2.cloned.1.call-start = ((), (), s32[]{:S(2)}) async-start(), calls=%async_computation.6 | async-start | bytes 1474560 | tf_op jit(solution)/shard_map/column_vectors/all_gather | solution.py:335
  11.5 16.5 %all-to-all-start = ((s32[8,8,128]{2,1,0:T(8,128)}), s32[8,8,128]{2,1,0:T(8,128)S(1)}, u32[]{:S(2)}, u32[]{:S(2)}) async-start(s32[8,8,128]{2,1,0:T(8,128)} %info.1), calls=%async_computation | async-start | bytes 65536 | tf_op jit(solution)/shard_map/column_info/all_to_all | solution.py:316
  29.8 10.5 %copy-start.16 = (s32[256,128]{1,0:T(8,128)}, s32[256,128]{1,0:T(8,128)S(1)}, u32[]{:S(2)}) copy-start(s32[256,128]{1,0:T(8,128)S(1)} %get-tuple-element.168.info_ref) | copy-start | bytes 393220
  29.8 14.2 %all-to-all-start.1 = ((s32[16,8,128]{2,1,0:T(8,128)}), s32[16,8,128]{2,1,0:T(8,128)S(1)}, u32[]{:S(2)}, u32[]{:S(2)}) async-start(s32[16,8,128]{2,1,0:T(8,128)} %get-tuple-element.72), calls=%async_computation.1 | async-start | bytes 131072 | tf_op jit(solution)/shard_map/requests/all_to_all | solution.py:316
  37.3 1.6 copy-start.3
  41.1 1.0 copy-start.13
  45.6 1.0 copy-start.5
  46.6 10.9 %copy-start.12 = (s32[8,128]{1,0:T(8,128)}, s32[8,128]{1,0:T(8,128)S(1)}, u32[]{:S(2)}) copy-start(s32[8,128]{1,0:T(8,128)S(1)} %get-tuple-element.83) | copy-start | bytes 12292
  46.6 21.6 %all-to-all-start.2 = ((f32[16,16,1024]{2,1,0:T(8,128)}), f32[16,16,1024]{2,1,0:T(8,128)}, u32[]{:S(2)}, u32[]{:S(2)}) async-start(f32[16,16,1024]{2,1,0:T(8,128)} %copy-done.5), calls=%async_computation.2 | async-start | bytes 2097152 | tf_op jit(solution)/shard_map/primary_rows/all_to_all | solution.py:316
  53.8 1.3 copy-start.4
  57.5 1.0 copy-start
  68.2 41.7 %all-to-all-start.4 = ((f32[16,16,1152]{2,1,0:T(8,128)}), f32[16,16,1152]{2,1,0:T(8,128)}, u32[]{:S(2)}, u32[]{:S(2)}) async-start(f32[16,16,1152]{2,1,0:T(8,128)} %bitcast.18), calls=%async_computation.4 | async-start | bytes 2359296 | tf_op jit(solution)/shard_map/vectors_out/all_to_all | solution.py:316
  76.8 9.8 %collective-permute-start.10 = (f32[32,1024]{1,0:T(8,128)S(1)}, f32[32,1024]{1,0:T(8,128)S(1)}, u32[]{:S(2)}, u32[]{:S(2)}) collective-permute-start(f32[32,1024]{1,0:T(8,128)S(1)} %get-tuple-element.79), channel_id=1, source_target_pairs={{0,8},{2,10},{4,12},{6,14},{8,0},{10,2},{12,4},{14,6},{1,9},{3,11}... | collective-permute-start | bytes 393224 | tf_op jit(solution)/shard_map/primary_across/ppermute | solution.py:397
  77.6 15.1 %collective-permute-start.11 = (f32[32,1024]{1,0:T(8,128)S(1)}, f32[32,1024]{1,0:T(8,128)S(1)}, u32[]{:S(2)}, u32[]{:S(2)}) collective-permute-start(f32[32,1024]{1,0:T(8,128)S(1)} %get-tuple-element.80), channel_id=1, source_target_pairs={{0,10},{2,12},{4,14},{6,0},{8,2},{10,4},{12,6},{14,8},{1,11},{3,13... | collective-permute-start | bytes 393224 | tf_op jit(solution)/shard_map/primary_across/ppermute | solution.py:397
  83.1 2.1 %collective-permute-start.14 = (s32[1,1]{1,0:T(1,128)}, s32[1,1]{1,0:T(1,128)}, u32[]{:S(2)}, u32[]{:S(2)}) collective-permute-start(s32[1,1]{1,0:T(1,128)} %slice.3), channel_id=1, source_target_pairs={{0,1},{1,0},{2,3},{3,2},{4,5},{5,4},{6,7},{7,6},{8,9},{9,8},{10,11... | collective-permute-start | bytes 20 | tf_op jit(solution)/shard_map/primary_rows/ppermute | solution.py:383
  83.1 14.4 %collective-permute-start.12 = (f32[32,1024]{1,0:T(8,128)}, f32[32,1024]{1,0:T(8,128)}, u32[]{:S(2)}, u32[]{:S(2)}) collective-permute-start(f32[32,1024]{1,0:T(8,128)} %get-tuple-element.81), channel_id=1, source_target_pairs={{0,12},{2,14},{4,0},{6,2},{8,4},{10,6},{12,8},{14,10},{1,13},{3,15... | collective-permute-start | bytes 393224 | tf_op jit(solution)/shard_map/primary_across/ppermute | solution.py:397
  84.5 14.0 %collective-permute-start.13 = (f32[32,1024]{1,0:T(8,128)}, f32[32,1024]{1,0:T(8,128)}, u32[]{:S(2)}, u32[]{:S(2)}) collective-permute-start(f32[32,1024]{1,0:T(8,128)} %get-tuple-element.82), channel_id=1, source_target_pairs={{0,14},{2,0},{4,2},{6,4},{8,6},{10,8},{12,10},{14,12},{1,15},{3,1}... | collective-permute-start | bytes 393224 | tf_op jit(solution)/shard_map/primary_across/ppermute | solution.py:397
  85.2 13.4 %collective-permute-start.7 = (f32[32,1024]{1,0:T(8,128)}, f32[32,1024]{1,0:T(8,128)}, u32[]{:S(2)}, u32[]{:S(2)}) collective-permute-start(f32[32,1024]{1,0:T(8,128)} %get-tuple-element.76), channel_id=1, source_target_pairs={{0,2},{2,4},{4,6},{6,8},{8,10},{10,12},{12,14},{14,0},{1,3},{3,5},... | collective-permute-start | bytes 393224 | tf_op jit(solution)/shard_map/primary_across/ppermute | solution.py:397
  86.6 13.9 %collective-permute-start.8 = (f32[32,1024]{1,0:T(8,128)}, f32[32,1024]{1,0:T(8,128)}, u32[]{:S(2)}, u32[]{:S(2)}) collective-permute-start(f32[32,1024]{1,0:T(8,128)} %get-tuple-element.77), channel_id=1, source_target_pairs={{0,4},{2,6},{4,8},{6,10},{8,12},{10,14},{12,0},{14,2},{1,5},{3,7},... | collective-permute-start | bytes 393224 | tf_op jit(solution)/shard_map/primary_across/ppermute | solution.py:397
  93.4 12.9 %collective-permute-start.9 = (f32[32,1024]{1,0:T(8,128)}, f32[32,1024]{1,0:T(8,128)}, u32[]{:S(2)}, u32[]{:S(2)}) collective-permute-start(f32[32,1024]{1,0:T(8,128)} %get-tuple-element.78), channel_id=1, source_target_pairs={{0,6},{2,8},{4,10},{6,12},{8,14},{10,0},{12,2},{14,4},{1,7},{3,9},... | collective-permute-start | bytes 393224 | tf_op jit(solution)/shard_map/primary_across/ppermute | solution.py:397
  106.3 0.9 copy-start.7
  109.9 19.3 %all-to-all-start.3 = ((f32[16,16,1024]{2,1,0:T(8,128)}), f32[16,16,1024]{2,1,0:T(8,128)}, u32[]{:S(2)}, u32[]{:S(2)}) async-start(f32[16,16,1024]{2,1,0:T(8,128)} %bitcast.24), calls=%async_computation.3 | async-start | bytes 2097152 | tf_op jit(solution)/shard_map/primaries_out/all_to_all | solution.py:316
  129.2 15.3 %copy-start.9 = (s32[32,4]{0,1:T(4,128)S(1)}, s32[32,4]{0,1:T(4,128)}, u32[]{:S(2)}) copy-start(s32[32,4]{0,1:T(4,128)} %param.12) | copy-start | bytes 1540
  133.7 21.9 %all-to-all-start.5 = ((f32[128,1,128]{2,1,0:T(1,128)}), f32[128,1,128]{2,1,0:T(1,128)S(1)}, u32[]{:S(2)}, u32[]{:S(2)}) async-start(f32[128,1,128]{2,1,0:T(1,128)} %bitcast.13), calls=%async_computation.5 | async-start | bytes 131072 | tf_op jit(solution)/shard_map/losses_back/all_to_all | solution.py:316
  (4 other events, 2.7 us)
Sparse Core Ops, SparseCore 0:
  9.1 42.3 all-gather.1

commit v3 on v1

v3 whole, which is shorter than its diff:
```python
import jax
import jax.numpy as jnp
from jax import lax
from jax.experimental import pallas as pl
from jax.experimental.pallas import tpu as pltpu
from jax.sharding import Mesh, PartitionSpec as P

D = 1024
V = 32
GROUPS = 4
GSIZE = 64
ROWS = 512
NY, NX, NZ = 4, 4, 8
COLS = NY * NX
COLV = NZ * V
SLOTS = COLS * NZ * 2
SHARDS = COLS * NZ
K = 32
PER = 19
amplify = 1.0
tiny = 1e-06

F32, BF16, I32 = jnp.float32, jnp.bfloat16, jnp.int32
VMEM = pl.BlockSpec(memory_space=pltpu.VMEM)
SMEM = pl.BlockSpec(memory_space=pltpu.SMEM)
HBM = pl.BlockSpec(memory_space=pltpu.HBM)
NN = (((1,), (0,)), ((), ()))
NT = (((1,), (1,)), ((), ()))
TN = (((0,), (0,)), ((), ()))


def call(kernel, out_shape, *operands, smem=(), far_in=(), far_out=(), scratch=(), name=None):
    specs = [SMEM if i in smem else HBM if i in far_in else VMEM for i in range(len(operands))]
    operands = [
        pltpu.with_memory_space_constraint(a, pltpu.HBM) if i in far_in else a
        for i, a in enumerate(operands)
    ]
    out_shape = [
        pltpu.HBM(o.shape, o.dtype) if i in far_out else o for i, o in enumerate(out_shape)
    ]
    return pl.pallas_call(
        kernel,
        out_shape=out_shape,
        in_specs=specs,
        out_specs=[HBM if i in far_out else VMEM for i in range(len(out_shape))],
        scratch_shapes=list(scratch),
        compiler_params=pltpu.CompilerParams(vmem_limit_bytes=24 * 2**20),
        name=name,
    )(*operands)


def copies_semaphores(n):
    return pltpu.SemaphoreType.DMA((n,))


def start_all(copies):
    for copy in copies:
        copy.start()


def wait_all(copies):
    for copy in copies:
        copy.wait()


def shape(dims, dtype=F32):
    return jax.ShapeDtypeStruct(dims, dtype)


def split3(a):
    hi = a.astype(BF16)
    rest = a - hi.astype(F32)
    mid = rest.astype(BF16)
    lo = (rest - mid.astype(F32)).astype(BF16)
    return hi, mid, lo


def dot(a, b, dims=NN):
    return lax.dot_general(a, b, dims, preferred_element_type=F32)


def pick(onehot, pieces):
    hi, mid, lo = pieces
    return dot(onehot, hi) + dot(onehot, mid) + dot(onehot, lo)


def bits(mask):
    return jnp.where(mask, 1.0, 0.0)


def iota(dims, axis):
    return lax.broadcasted_iota(I32, dims, axis)


def before_same_block(rows):
    u, w = iota((rows, rows), 0), iota((rows, rows), 1)
    return bits((w < u) & ((u >> 5) == (w >> 5))).astype(BF16)


def before_all(rows):
    return bits(iota((rows, rows), 1) < iota((rows, rows), 0)).astype(BF16)


def prepare_kernel(c_ref, pieces_ref, norms_ref):
    c = c_ref[...]
    for i, piece in enumerate(split3(c)):
        pieces_ref[i] = piece
    squares = split3(c * c)
    ones = jnp.ones((8, D), BF16)
    norms_ref[...] = sum(dot(ones, s, NT) for s in squares)


def request_kernel(owner_ref, row_ref, cand_ref, x_ref, rows_ref, out_ref, owner, row, cand, x, rows, hold, sems):
    copies = [
        pltpu.make_async_copy(a, b, sems.at[i])
        for i, (a, b) in enumerate(
            [(owner_ref, owner), (row_ref, row), (cand_ref, cand), (x_ref, x), (rows_ref, rows)]
        )
    ]
    start_all(copies)
    shard = iota((SHARDS, V), 0)
    earlier = bits(iota((V, V), 0) < iota((V, V), 1)).astype(BF16)
    lane = iota((SHARDS, 128), 1)
    wait_all(copies)
    hit = owner[...] == shard
    rank = dot(bits(hit).astype(BF16), earlier)
    asked = row[...].astype(F32)
    asks = [
        jnp.sum(jnp.where(hit & (rank == float(k)), asked, 0.0), axis=1, keepdims=True)
        for k in range(2)
    ]
    empty = jnp.zeros((1, V), I32)
    owners = jnp.concatenate([empty, owner[...], empty, empty], axis=1).astype(F32)
    line = jnp.where(lane == 0, asks[0], jnp.where(lane == 1, asks[1], 0.0)) + owners
    hold[pl.ds(17, SHARDS, stride=PER), :] = line
    line = jnp.concatenate([cand[g : g + 1, :] for g in range(GROUPS)], axis=1).astype(F32)
    hold[pl.ds(18, SHARDS, stride=PER), :] = jnp.broadcast_to(line, (SHARDS, 128))
    hits = [cand[g : g + 1, :] == shard for g in range(GROUPS)]
    any_hit = hits[0] | hits[1] | hits[2] | hits[3]
    rank = dot(bits(any_hit).astype(BF16), earlier)
    wide = [split3(rows[:, 128 * h : 128 * h + 128].astype(F32))[:2] for h in range(2)]
    lines = []
    for k in range(2):
        sides = [jnp.zeros((SHARDS, 128), F32)] * 2
        for g in range(GROUPS):
            onehot = bits(hits[g] & (rank == float(k))).astype(BF16)
            sides[g % 2] = sides[g % 2] + dot(onehot, wide[g // 2][0]) + dot(onehot, wide[g // 2][1])
        sides[1 - k] = pltpu.roll(sides[1 - k], GSIZE, 1)
        side = even_lanes if k == 0 else odd_lanes
        lines.append(side(sides[0]) + side(sides[1]))
    hold[pl.ds(16, SHARDS, stride=PER), :] = lines[0] + lines[1]
    pieces = split3(x[...])
    for k in range(2):
        sent = pick(bits(any_hit & (rank == float(k))).astype(BF16), pieces)
        for j in range(8):
            hold[pl.ds(8 * k + j, SHARDS, stride=PER), :] = sent[:, 128 * j : 128 * j + 128]
    copy = pltpu.make_async_copy(hold, out_ref, sems.at[5])
    copy.start()
    copy.wait()


def even_lanes(a):
    return jnp.where(iota(a.shape, 1) < GSIZE, a, 0.0)


def odd_lanes(a):
    return jnp.where(iota(a.shape, 1) < GSIZE, 0.0, a)


def slots_kernel(me_ref, got_ref, found_ref, info_ref, slots_ref, most_ref, hold):
    me, column = me_ref[0], me_ref[1]
    owners = got_ref[pl.ds(17, SHARDS, stride=PER), :].astype(I32)
    cands = got_ref[pl.ds(18, SHARDS, stride=PER), :].astype(I32)
    hold[0] = owners
    hold[1] = cands
    at = pl.multiple_of(column * NZ, NZ)
    tile = jnp.concatenate([hold[0, pl.ds(at, NZ), :], hold[1, pl.ds(at, NZ), :]], axis=0)
    turned = jnp.concatenate([tile, jnp.zeros((128 - NZ * 2, 128), I32)], axis=0).T
    block_lane = iota((V, 128), 1)
    for z in range(NZ):
        block = jnp.where(block_lane == 0, turned[V : 2 * V, z : z + 1], 0)
        for g in range(GROUPS):
            cand = turned[g * V : (g + 1) * V, NZ + z : NZ + z + 1]
            block = jnp.where(block_lane == 1 + g, cand, block)
        info_ref[z * V : (z + 1) * V, :] = block
    lane = iota((COLV, 128), 1)
    hit = lane < 0
    for g in range(GROUPS):
        hit = hit | (info_ref[:, 1 + g : 2 + g] == lane * NZ + me)
    hit = hit & (lane < COLS)
    rank = dot(before_same_block(COLV), bits(hit).astype(BF16))
    mine = (iota((NZ, COLV), 1) >> 5) == iota((NZ, COLV), 0)
    for k in range(2):
        turned = bits(hit & (rank == float(k))).T
        for b in range(COLS):
            part = jnp.where(mine, turned[b : b + 1, :], 0.0)
            slots_ref[b * 16 + k * 8 : b * 16 + k * 8 + 8, :] = part
    lane = iota((SHARDS, 128), 1)
    owners = jnp.where((lane >= V) & (lane < 2 * V), owners, 0)
    owners = owners + pltpu.roll(owners, 2 * V, 1)
    owners = (owners + pltpu.roll(owners, V, 1)) & 7
    parts = []
    for b in range(NZ):
        to_plane = bits((cands & 7) == b)
        to_plane = jnp.maximum(to_plane, pltpu.roll(to_plane, 2 * V, 1))
        to_plane = jnp.maximum(to_plane, pltpu.roll(to_plane, V, 1))
        for h in range(2):
            parts.append(jnp.where(owners == (lane >> 5) + 4 * h, to_plane, 0.0).astype(BF16))
    columns = bits((iota((COLS, SHARDS), 1) >> 3) == iota((COLS, SHARDS), 0)).astype(BF16)
    group = bits((iota((128, 128), 0) >> 5) == iota((128, 128), 1)).astype(BF16)
    most = 0.0
    for part in parts:
        most = jnp.maximum(most, jnp.max(dot(dot(columns, part).astype(BF16), group)))
    most_ref[...] = jnp.full((8, 128), most, F32).astype(I32)


def relay_kernel(me_ref, turn_ref, info_ref, slots_ref, send_ref, take_ref):
    me = me_ref[0]
    base = (turn_ref[0] * K).astype(F32)
    lane = iota((COLV, 128), 1)
    u = iota((COLV, 1), 0)
    info = info_ref[...]
    owner = info[:, 0:1]
    hits = bits((owner == lane * NZ + me) & (lane < COLS))
    rank = dot(before_same_block(COLV), hits.astype(BF16))
    rank = jnp.sum(rank * hits, axis=1, keepdims=True)
    here = (owner & 7) == me
    wanted = lane < 0
    to_me = u < 0
    for g in range(GROUPS):
        plane = info[:, 1 + g : 2 + g] & 7
        wanted = wanted | (plane == lane)
        to_me = to_me | (plane == me)
    earlier = before_all(COLV)
    leaves = wanted & (lane < NZ) & here
    order = dot(earlier, bits(leaves).astype(BF16))
    place = jnp.where(leaves, order - base, -1.0).T
    depth = iota((K, COLV), 0).astype(F32)
    rows = jnp.concatenate([bits(place[z : z + 1, :] == depth) for z in range(NZ)], axis=0)
    slot = (owner >> 3) * 16 + rank.astype(I32) * 8 + (u >> 5)
    held = bits((slot == iota((COLV, SLOTS), 1)) & here)
    send_ref[...] = dot(rows.astype(BF16), held.astype(BF16)).astype(BF16)
    comes = ((owner & 7) == lane) & (lane < NZ) & to_me
    order = dot(earlier, bits(comes).astype(BF16)) - base
    fits = comes & (order >= 0.0) & (order < float(K))
    at = jnp.sum(jnp.where(fits, lane.astype(F32) * K + order + 1.0, 0.0), axis=1, keepdims=True)
    found = bits(at == iota((COLV, NZ * K), 1).astype(F32) + 1.0).astype(BF16)
    take_ref[...] = dot(slots_ref[...].astype(BF16), found).astype(BF16)


def fetch_kernel(got_ref, pieces_ref, out_ref, hold, sems):
    column = iota((SHARDS, ROWS), 1)
    asked = got_ref[pl.ds(17, SHARDS, stride=PER), :].astype(I32)
    pieces = [pieces_ref[i] for i in range(3)]
    copies = []
    for k in range(2):
        onehot = bits(asked[:, k : k + 1] == column).astype(BF16)
        hold[k] = pick(onehot, pieces).reshape(COLS, 8, D)
        copies.append(
            pltpu.make_async_copy(hold.at[k], out_ref.at[:, pl.ds(k * 8, 8), :], sems.at[k])
        )
        copies[-1].start()
    wait_all(copies)


def move_kernel(onehot_ref, in_ref, out_ref, hold, sems):
    pieces = split3(in_ref[...])
    half = SLOTS // 2
    copies = []
    for c in range(2):
        hold[c] = pick(onehot_ref[c * half : (c + 1) * half, :], pieces)
        copies.append(
            pltpu.make_async_copy(hold.at[c], out_ref.at[pl.ds(c * half, half), :], sems.at[c])
        )
        copies[-1].start()
    wait_all(copies)


def lookup(table, rows):
    low, high = rows & 127, rows >> 7
    found = jnp.zeros(rows.shape, F32)
    for i in range(ROWS // 128):
        part = jnp.take_along_axis(table[:, 128 * i : 128 * i + 128], low, axis=1)
        found = jnp.where(high == i, part, found)
    return found


def scores(a, pieces_ref):
    hi, mid, lo = split3(a)
    chi, cmid, clo = (pieces_ref[i] for i in range(3))
    small = dot(mid, cmid, NT) + dot(lo, chi, NT) + dot(hi, clo, NT)
    return dot(hi, chi, NT) + (dot(hi, cmid, NT) + dot(mid, chi, NT) + small)


def near_kernel(got_ref, pieces_ref, norms_ref, x_ref, rows_ref, out_ref):
    line = got_ref[pl.ds(16, SHARDS, stride=PER), :]
    for k in range(2):
        at = slice(8 * k, 8 * k + 8)
        for j in range(8):
            part = got_ref[pl.ds(8 * k + j, SHARDS, stride=PER), :]
            x_ref[:, at, 128 * j : 128 * j + 128] = part.reshape(COLS, 8, 128)
        rows_ref[:, at, :] = line.astype(I32).reshape(COLS, 8, 128)
        line = pltpu.roll(line, GSIZE, 1)
    x = x_ref[...].reshape(SLOTS, D)
    square = jnp.sum(x * x, axis=1, keepdims=True)
    table = square - 2.0 * scores(x, pieces_ref) + norms_ref[0:1, :]
    out_ref[...] = lookup(table, rows_ref[...].reshape(SLOTS, 128))


def loss_kernel(p_ref, x_ref, rows_ref, near_ref, pieces_ref, out_ref):
    x = x_ref[...].reshape(SLOTS, D)
    rows = rows_ref[...].reshape(SLOTS, 128)
    r = x - p_ref[...]
    hi = r.astype(BF16)
    mid = (r - hi.astype(F32)).astype(BF16)
    chi, cmid = pieces_ref[0], pieces_ref[1]
    table = dot(hi, chi, NT) + (dot(hi, cmid, NT) + dot(mid, chi, NT))
    rx = jnp.sum(r * x, axis=1, keepdims=True)
    rr = jnp.sum(r * r, axis=1, keepdims=True)
    gap = rx - lookup(table, rows)
    loss = (near_ref[...] + amplify * gap * gap / (rr + tiny)) / D
    loss = loss.reshape(COLS, 2, NZ, 128)
    second = pltpu.roll(loss[:, 1].reshape(COLS * NZ, 128), GSIZE, 1)
    first = loss[:, 0].reshape(COLS * NZ, 128)
    out_ref[...] = jnp.where(iota((COLS * NZ, 128), 1) < GSIZE, first, second)


def collect_kernel(owner_ref, in_ref, out_ref):
    lane = iota((V, 128), 1)
    hits = [owner_ref[:, g : g + 1] == lane for g in range(GROUPS)]
    rank = dot(before_same_block(V), bits(hits[0] | hits[1] | hits[2] | hits[3]).astype(BF16))
    a = in_ref[...]
    plain, rolled = split3(a), split3(pltpu.roll(a, GSIZE, 1))
    for h in range(2):
        halves = []
        for g in (2 * h, 2 * h + 1):
            first = bits(hits[g] & (rank == 0.0)).astype(BF16)
            second = bits(hits[g] & (rank == 1.0)).astype(BF16)
            if g % 2 == 0:
                halves.append(pick(first, plain) + pick(second, rolled))
            else:
                halves.append(pick(first, rolled) + pick(second, plain))
        out_ref[:, 128 * h : 128 * h + 128] = jnp.where(lane < GSIZE, halves[0], halves[1])


def swap(a, axes):
    return lax.all_to_all(a, axes, split_axis=0, concat_axis=0, tiled=True)


def shards(new_vectors, centroids, primary_owner, primary_row, cand_owner, cand_row):
    plane = ("y", "x")
    column = lax.axis_index(("y", "x")).astype(I32)
    me = jnp.stack([lax.axis_index("z").astype(I32), column])
    with jax.named_scope("requests_and_vectors"):
        [sent] = call(
            request_kernel,
            [shape((PER * SHARDS, 128))],
            primary_owner.T,
            primary_row.T,
            cand_owner.T,
            new_vectors,
            cand_row,
            far_in=(0, 1, 2, 3, 4),
            far_out=(0,),
            scratch=[
                pltpu.VMEM((1, V), I32),
                pltpu.VMEM((1, V), I32),
                pltpu.VMEM((GROUPS, V), I32),
                pltpu.VMEM((V, D), F32),
                pltpu.VMEM((V, GROUPS * GSIZE), I32),
                pltpu.VMEM((PER * SHARDS, 128), F32),
                copies_semaphores(6),
            ],
            name="request",
        )
        arrived = swap(sent.reshape(SHARDS, 1, PER * 128), ("y", "x", "z")).reshape(PER * SHARDS, 128)
    pieces, norms = call(
        prepare_kernel, [shape((3, ROWS, D), BF16), shape((8, ROWS))], centroids, name="prepare"
    )
    with jax.named_scope("primary_rows"):
        [found] = call(
            fetch_kernel,
            [shape((COLS, 16, D))],
            arrived,
            pieces,
            far_out=(0,),
            scratch=[pltpu.VMEM((2, COLS, 8, D), F32), copies_semaphores(2)],
            name="fetch",
        )
        fetched = swap(found, plane).reshape(SLOTS, D)
    info, slots, most = call(
        slots_kernel,
        [shape((COLV, 128), I32), shape((SLOTS, COLV)), shape((8, 128), I32)],
        me,
        arrived,
        found,
        smem=(0,),
        far_in=(2,),
        scratch=[pltpu.VMEM((2, SHARDS, 128), I32)],
        name="slots",
    )
    most = most[:1, :1]
    most = jnp.maximum(most, lax.ppermute(most, "rep", [(0, 1), (1, 0)]))[0, 0]

    def relay(turn):
        return call(
            relay_kernel,
            [shape((NZ * K, SLOTS), BF16), shape((SLOTS, NZ * K), BF16)],
            me,
            turn.reshape(1),
            info,
            slots,
            smem=(0, 1),
            name="relay",
        )

    def across(send, take):
        def move(onehot, source, name):
            [moved] = call(
                move_kernel,
                [shape((SLOTS, D))],
                onehot,
                source,
                far_out=(0,),
                scratch=[pltpu.VMEM((2, SLOTS // 2, D), F32), copies_semaphores(2)],
                name=name,
            )
            return moved

        leaving = move(send, fetched, "send")
        got = swap(leaving.reshape(NZ, K, D), "z").reshape(NZ * K, D)
        return move(take, got, "take")

    def more(state):
        turn, total = state
        return turn + 1, total + across(*relay(turn))

    with jax.named_scope("primary_across"):
        primaries = across(*relay(jnp.int32(0)))
        _, primaries = lax.while_loop(lambda s: s[0] * K < most, more, (jnp.int32(1), primaries))
    x, rows, near = call(
        near_kernel,
        [shape((COLS, 16, D)), shape((COLS, 16, 128), I32), shape((SLOTS, 128))],
        arrived,
        pieces,
        norms,
        name="near",
    )
    with jax.named_scope("primaries_out"):
        primaries = swap(primaries.reshape(COLS, 16, D), plane).reshape(SLOTS, D)
    [losses] = call(
        loss_kernel,
        [shape((SHARDS, 128))],
        primaries,
        x,
        rows,
        near,
        pieces,
        name="loss",
    )
    with jax.named_scope("losses_back"):
        back = swap(losses.reshape(SHARDS, 1, 128), ("y", "x", "z")).reshape(SHARDS, 128)
    [result] = call(
        collect_kernel, [shape((V, GROUPS * GSIZE))], cand_owner, back, name="collect"
    )
    return result


def solution(mesh):
    fine = Mesh(mesh.devices.reshape(NY, NX, NZ, 2), ("y", "x", "z", "rep"))
    rows = P(("y", "x", "z", "rep"), None)
    in_specs = (rows, P(("y", "x", "z"), None), rows, rows, rows, rows)
    return jax.shard_map(shards, mesh=fine, in_specs=in_specs, out_specs=rows, check_vma=False)
```

time: 188 us -> 156 us (0.83)
  blocking collectives: 20.9 us -> 0 us
  waiting for transfers between devices: 94.9 us -> 84 us
  Pallas kernels: 17.9 us -> 23.2 us
  local copies, waits for them, and re-layouts: 10.8 us -> 6.3 us
    all_to_all x1 -> x0, blocking collectives: 20.9 us -> none  [swap(): return lax.all_to_all(a, axes, split_axis=0, concat_axis=0, tiled=True)]
    all_to_all x7 -> x5, waiting for transfers between devices: 93.6 us -> 82.9 us  [swap(): return lax.all_to_all(a, axes, split_axis=0, concat_axis=0, tiled=True)]
    pallas_call x11 -> x10, Pallas kernels: 17.9 us -> 23.2 us  [call(): pl.pallas_call(kernel, out_shape=out_shape, in_specs=specs, out_specs=[HB...]
    unnamed x34 -> x15, local copies, waits for them, and re-layouts: 8.29 us -> 5.75 us
    broadcast_in_dim x2 -> x0, local copies, waits for them, and re-layouts: 1.93 us -> none  [the longest x1 1.28 us: shards(): jnp.broadcast_to(wide[None], (NZ,) + wide.shape)]
    all_to_all x7 -> x5, starting transfers between devices: 40.1 us -> 39.5 us  [swap(): return lax.all_to_all(a, axes, split_axis=0, concat_axis=0, tiled=True)]
  transfers between devices with their start and end apart: 8 -> 6, of which waited for: 8 -> 6; matrix products, arithmetic and copies ran while one was open for 0% -> 1% of each run, Pallas kernels for 4% -> 6%
where the time goes in v3:
time: 156 us; the launch traced here: 155 us
  waiting for transfers between devices  84 us (54%)
  starting transfers between devices  39.5 us (25%)
  Pallas kernels  23.2 us (15%)
  local copies, waits for them, and re-layouts  6.3 us (4%)
    all_to_all x5, waiting for transfers between devices, swap(): return lax.all_to_all(a, axes, split_axis=0, concat_axis=0, tiled=True)  82.9 us
    all_to_all x5, starting transfers between devices, swap(): return lax.all_to_all(a, axes, split_axis=0, concat_axis=0, tiled=True)  39.5 us
    pallas_call x10, Pallas kernels, call(): pl.pallas_call(kernel, out_shape=out_shape, in_specs=specs, out_specs=[HB...  23.2 us
    unnamed x15, local copies, waits for them, and re-layouts  5.75 us
  transfers between devices with their start and end apart: 6, of which 6 were waited for; matrix products, arithmetic and copies ran while one was open for 1% of the time, Pallas kernels for 6%

profile of v3, /device:TPU:2, one launch (start us, length us, event | category | flops | bytes accessed | tf_op | source)
XLA Modules:
  0.0 155.1 jit_solution(15714439528008819052)
XLA Ops:
  0.0 2.9 %request.1 = f32[2432,128]{1,0:T(8,128)} custom-call(s32[1,32]{1,0:T(1,128)} %bitcast.36, s32[1,32]{1,0:T(1,128)} %bitcast.37, s32[4,32]{1,0:T(4,128)} %bitcast.35, f32[32,1024]{1,0:T(8,128)} %x_ref.1, s32[32,256]{1,0:T(8,128)} %rows_ref.1), custom_call_target="tpu_custom_call" | custom-call | tf_op jit(solution)/shard_map/requests_and_vectors/request/pallas_call | solution.py:41
  3.0 15.8 %all-to-all-start.1 = ((f32[128,1,2432]{2,1,0:T(1,128)}), f32[128,1,2432]{2,1,0:T(1,128)}, u32[]{:S(2)}, u32[]{:S(2)}) async-start(f32[128,1,2432]{2,1,0:T(1,128)} %bitcast.33), calls=%async_computation.1 | async-start | bytes 2490368 | tf_op jit(solution)/shard_map/requests_and_vectors/all_to_all | solution.py:347
  18.8 1.6 %copy-done.3 = f32[512,1024]{1,0:T(8,128)S(1)} copy-done((f32[512,1024]{1,0:T(8,128)S(1)}, f32[512,1024]{1,0:T(8,128)}, u32[]{:S(2)}) %copy-start.3) | copy-done | bytes 2097176
  20.4 1.5 prepare.1
  21.9 30.1 %all-to-all-done.1 = f32[128,1,2432]{2,1,0:T(1,128)} async-done(((f32[128,1,2432]{2,1,0:T(1,128)}), f32[128,1,2432]{2,1,0:T(1,128)}, u32[]{:S(2)}, u32[]{:S(2)}) %all-to-all-start.1) | async-done | bytes 1245216 | tf_op jit(solution)/shard_map/requests_and_vectors/all_to_all | solution.py:347
  51.9 3.2 %fetch.1.found_ref = f32[16,16,1024]{2,1,0:T(8,128)} custom-call(f32[2432,128]{1,0:T(8,128)} %bitcast.9.got_ref, bf16[3,512,1024]{2,1,0:T(8,128)(2,1)S(1)} %get-tuple-element.55.pieces_ref), custom_call_target="tpu_custom_call" | custom-call | tf_op jit(solution)/shard_map/primary_rows/fetch/pallas_call | solution.py:41
  55.1 7.1 %all-to-all-start.2 = ((f32[16,16,1024]{2,1,0:T(8,128)}), f32[16,16,1024]{2,1,0:T(8,128)S(1)}, u32[]{:S(2)}, u32[]{:S(2)}) async-start(f32[16,16,1024]{2,1,0:T(8,128)} %fetch.1.found_ref), calls=%async_computation.2 | async-start | bytes 2097152 | tf_op jit(solution)/shard_map/primary_rows/all_to_all | solution.py:347
  62.8 2.7 %slots.1 = (s32[256,128]{1,0:T(8,128)}, f32[256,256]{1,0:T(8,128)S(1)}, s32[8,128]{1,0:T(8,128)S(1)}) custom-call(s32[2]{0:T(128)} %pad_add_fusion.me_ref, f32[2432,128]{1,0:T(8,128)} %bitcast.9.got_ref, f32[16,16,1024]{2,1,0:T(8,128)} %fetch.1.found_ref), custom_call_target="tpu_custom_call" | custom-call | tf_op jit(solution)/shard_map/slots/pallas_call | solution.py:41
  65.5 2.0 %relay.2 = (bf16[256,256]{1,0:T(8,128)(2,1)S(1)}, bf16[256,256]{1,0:T(8,128)(2,1)S(1)}) custom-call(s32[2]{0:T(128)} %pad_add_fusion.me_ref, s32[1]{0:T(128)} %constant.25.clone.1.turn_ref, s32[256,128]{1,0:T(8,128)} %get-tuple-element.132.info_ref, f32[256,256]{1,0:T(8,128)S(1)} %get-tuple-element.133.slots_ref), custom_call_target="tpu_custom_call" | custom-call | tf_op jit(solution)/shard_map/primary_across/relay/pallas_call | solution.py:41
  67.5 9.3 %all-to-all-done.2 = f32[16,16,1024]{2,1,0:T(8,128)S(1)} async-done(((f32[16,16,1024]{2,1,0:T(8,128)}), f32[16,16,1024]{2,1,0:T(8,128)S(1)}, u32[]{:S(2)}, u32[]{:S(2)}) %all-to-all-start.2) | async-done | bytes 1048608 | tf_op jit(solution)/shard_map/primary_rows/all_to_all | solution.py:347
  76.9 1.5 send.2
  78.4 3.6 %all-to-all-start.3 = ((f32[8,32,1024]{2,1,0:T(8,128)}), f32[8,32,1024]{2,1,0:T(8,128)S(1)}, u32[]{:S(2)}, u32[]{:S(2)}) async-start(f32[8,32,1024]{2,1,0:T(8,128)} %bitcast.34), calls=%async_computation.3 | async-start | bytes 2097152 | tf_op jit(solution)/shard_map/primary_across/all_to_all | solution.py:347
  82.5 1.2 collective-permute-done
  85.0 22.9 %all-to-all-done.3 = f32[8,32,1024]{2,1,0:T(8,128)S(1)} async-done(((f32[8,32,1024]{2,1,0:T(8,128)}), f32[8,32,1024]{2,1,0:T(8,128)S(1)}, u32[]{:S(2)}, u32[]{:S(2)}) %all-to-all-start.3) | async-done | bytes 1048608 | tf_op jit(solution)/shard_map/primary_across/all_to_all | solution.py:347
  107.9 1.5 take.2
  109.4 5.9 %all-to-all-start.4 = ((f32[16,16,1024]{2,1,0:T(8,128)}), f32[16,16,1024]{2,1,0:T(8,128)}, u32[]{:S(2)}, u32[]{:S(2)}) async-start(f32[16,16,1024]{2,1,0:T(8,128)} %bitcast.30), calls=%async_computation.4 | async-start | bytes 2097152 | tf_op jit(solution)/shard_map/primaries_out/all_to_all | solution.py:347
  115.3 1.9 %copy-done.1 = bf16[3,512,1024]{2,1,0:T(8,128)(2,1)S(1)} copy-done((bf16[3,512,1024]{2,1,0:T(8,128)(2,1)S(1)}, bf16[3,512,1024]{2,1,0:T(8,128)(2,1)}, u32[]{:S(2)}) %copy-start.1) | copy-done | bytes 3145752
  117.2 3.6 %near.1 = (f32[16,16,1024]{2,1,0:T(8,128)S(1)}, s32[16,16,128]{2,1,0:T(8,128)S(1)}, f32[256,128]{1,0:T(8,128)S(1)}) custom-call(f32[2432,128]{1,0:T(8,128)} %bitcast.9.got_ref, bf16[3,512,1024]{2,1,0:T(8,128)(2,1)S(1)} %copy-done.1, f32[8,512]{1,0:T(8,128)S(1)} %get-tuple-element.62.norms_ref), custom_call_target="tpu_custom_call" | custom-call | tf_op jit(solution)/shard_map/near/pallas_call | solution.py:41
  121.7 9.5 %all-to-all-done.4 = f32[16,16,1024]{2,1,0:T(8,128)} async-done(((f32[16,16,1024]{2,1,0:T(8,128)}), f32[16,16,1024]{2,1,0:T(8,128)}, u32[]{:S(2)}, u32[]{:S(2)}) %all-to-all-start.4) | async-done | bytes 1048608 | tf_op jit(solution)/shard_map/primaries_out/all_to_all | solution.py:347
  131.2 1.2 copy-done.5
  132.5 3.2 %loss.1 = f32[128,128]{1,0:T(8,128)} custom-call(f32[256,1024]{1,0:T(8,128)} %bitcast.15.p_ref, f32[16,16,1024]{2,1,0:T(8,128)S(1)} %copy-done.5, s32[16,16,128]{2,1,0:T(8,128)S(1)} %get-tuple-element.64.rows_ref, f32[256,128]{1,0:T(8,128)S(1)} %get-tuple-element.65.near_ref, bf16[3,512,1024]{2,1,0:T(8,128)(2,1)S(1)} %copy-done.2), custom_call_target="tpu_custom_call" | custom-call | tf_op jit(solution)/shard_map/loss/pallas_call | solution.py:41
  135.7 7.2 %all-to-all-start.5 = ((f32[128,1,128]{2,1,0:T(1,128)}), f32[128,1,128]{2,1,0:T(1,128)S(1)}, u32[]{:S(2)}, u32[]{:S(2)}) async-start(f32[128,1,128]{2,1,0:T(1,128)} %bitcast.17), calls=%async_computation.5 | async-start | bytes 131072 | tf_op jit(solution)/shard_map/losses_back/all_to_all | solution.py:347
  143.0 11.0 %all-to-all-done.5 = f32[128,1,128]{2,1,0:T(1,128)S(1)} async-done(((f32[128,1,128]{2,1,0:T(1,128)}), f32[128,1,128]{2,1,0:T(1,128)S(1)}, u32[]{:S(2)}, u32[]{:S(2)}) %all-to-all-start.5) | async-done | bytes 65568 | tf_op jit(solution)/shard_map/losses_back/all_to_all | solution.py:347
  154.0 1.1 collect.1
  (16 shorter events, 2.2 us)
Async XLA Ops:
  3.0 49.0 %all-to-all-start.1 = ((f32[128,1,2432]{2,1,0:T(1,128)}), f32[128,1,2432]{2,1,0:T(1,128)}, u32[]{:S(2)}, u32[]{:S(2)}) async-start(f32[128,1,2432]{2,1,0:T(1,128)} %bitcast.33), calls=%async_computation.1 | async-start | bytes 2490368 | tf_op jit(solution)/shard_map/requests_and_vectors/all_to_all | solution.py:347
  18.8 1.6 %copy-start.3 = (f32[512,1024]{1,0:T(8,128)S(1)}, f32[512,1024]{1,0:T(8,128)}, u32[]{:S(2)}) copy-start(f32[512,1024]{1,0:T(8,128)} %c_ref.1) | copy-start | bytes 6291460
  21.9 33.3 %copy-start = (bf16[3,512,1024]{2,1,0:T(8,128)(2,1)}, bf16[3,512,1024]{2,1,0:T(8,128)(2,1)S(1)}, u32[]{:S(2)}) copy-start(bf16[3,512,1024]{2,1,0:T(8,128)(2,1)S(1)} %get-tuple-element.55.pieces_ref) | copy-start | bytes 9437188
  55.1 21.7 %all-to-all-start.2 = ((f32[16,16,1024]{2,1,0:T(8,128)}), f32[16,16,1024]{2,1,0:T(8,128)S(1)}, u32[]{:S(2)}, u32[]{:S(2)}) async-start(f32[16,16,1024]{2,1,0:T(8,128)} %fetch.1.found_ref), calls=%async_computation.2 | async-start | bytes 2097152 | tf_op jit(solution)/shard_map/primary_rows/all_to_all | solution.py:347
  78.4 29.5 %all-to-all-start.3 = ((f32[8,32,1024]{2,1,0:T(8,128)}), f32[8,32,1024]{2,1,0:T(8,128)S(1)}, u32[]{:S(2)}, u32[]{:S(2)}) async-start(f32[8,32,1024]{2,1,0:T(8,128)} %bitcast.34), calls=%async_computation.3 | async-start | bytes 2097152 | tf_op jit(solution)/shard_map/primary_across/all_to_all | solution.py:347
  82.5 1.2 collective-permute-start
  109.4 21.8 %all-to-all-start.4 = ((f32[16,16,1024]{2,1,0:T(8,128)}), f32[16,16,1024]{2,1,0:T(8,128)}, u32[]{:S(2)}, u32[]{:S(2)}) async-start(f32[16,16,1024]{2,1,0:T(8,128)} %bitcast.30), calls=%async_computation.4 | async-start | bytes 2097152 | tf_op jit(solution)/shard_map/primaries_out/all_to_all | solution.py:347
  115.3 1.9 %copy-start.1 = (bf16[3,512,1024]{2,1,0:T(8,128)(2,1)S(1)}, bf16[3,512,1024]{2,1,0:T(8,128)(2,1)}, u32[]{:S(2)}) copy-start(bf16[3,512,1024]{2,1,0:T(8,128)(2,1)} %copy-done) | copy-start | bytes 9437188
  117.2 14.1 %copy-start.2 = (bf16[3,512,1024]{2,1,0:T(8,128)(2,1)S(1)}, bf16[3,512,1024]{2,1,0:T(8,128)(2,1)}, u32[]{:S(2)}) copy-start(bf16[3,512,1024]{2,1,0:T(8,128)(2,1)} %copy-done) | copy-start | bytes 9437188
  120.7 1.0 copy-start.4
  131.2 1.2 copy-start.5
  132.5 10.4 %copy-start.8 = (s32[32,4]{0,1:T(4,128)S(1)}, s32[32,4]{0,1:T(4,128)}, u32[]{:S(2)}) copy-start(s32[32,4]{0,1:T(4,128)} %param.12) | copy-start | bytes 1540
  135.7 18.3 %all-to-all-start.5 = ((f32[128,1,128]{2,1,0:T(1,128)}), f32[128,1,128]{2,1,0:T(1,128)S(1)}, u32[]{:S(2)}, u32[]{:S(2)}) async-start(f32[128,1,128]{2,1,0:T(1,128)} %bitcast.17), calls=%async_computation.5 | async-start | bytes 131072 | tf_op jit(solution)/shard_map/losses_back/all_to_all | solution.py:347

commit v4 on v3

--- a/solution.py
+++ b/solution.py
@@ -1,3 +1,5 @@
+import functools
+
 import jax
 import jax.numpy as jnp
 from jax import lax
@@ -16,7 +18,8 @@
 SLOTS = COLS * NZ * 2
 SHARDS = COLS * NZ
 K = 32
-PER = 19
+LATER = 16
+PER = 3
 amplify = 1.0
 tiny = 1e-06
 
@@ -29,7 +32,7 @@
 TN = (((0,), (0,)), ((), ()))
 
 
-def call(kernel, out_shape, *operands, smem=(), far_in=(), far_out=(), scratch=(), name=None):
+def call(kernel, out_shape, *operands, smem=(), far_in=(), far_out=(), scratch=(), alias=None, name=None):
     specs = [SMEM if i in smem else HBM if i in far_in else VMEM for i in range(len(operands))]
     operands = [
         pltpu.with_memory_space_constraint(a, pltpu.HBM) if i in far_in else a
@@ -44,6 +47,7 @@
         in_specs=specs,
         out_specs=[HBM if i in far_out else VMEM for i in range(len(out_shape))],
         scratch_shapes=list(scratch),
+        input_output_aliases=alias or {},
         compiler_params=pltpu.CompilerParams(vmem_limit_bytes=24 * 2**20),
         name=name,
     )(*operands)
@@ -110,11 +114,11 @@
     norms_ref[...] = sum(dot(ones, s, NT) for s in squares)
 
 
-def request_kernel(owner_ref, row_ref, cand_ref, x_ref, rows_ref, out_ref, owner, row, cand, x, rows, hold, sems):
+def request_kernel(owner_ref, row_ref, cand_ref, rows_ref, out_ref, owner, row, cand, rows, hold, sems):
     copies = [
         pltpu.make_async_copy(a, b, sems.at[i])
         for i, (a, b) in enumerate(
-            [(owner_ref, owner), (row_ref, row), (cand_ref, cand), (x_ref, x), (rows_ref, rows)]
+            [(owner_ref, owner), (row_ref, row), (cand_ref, cand), (rows_ref, rows)]
         )
     ]
     start_all(copies)
@@ -132,9 +136,9 @@
     empty = jnp.zeros((1, V), I32)
     owners = jnp.concatenate([empty, owner[...], empty, empty], axis=1).astype(F32)
     line = jnp.where(lane == 0, asks[0], jnp.where(lane == 1, asks[1], 0.0)) + owners
-    hold[pl.ds(17, SHARDS, stride=PER), :] = line
+    hold[pl.ds(0, SHARDS, stride=PER), :] = line
     line = jnp.concatenate([cand[g : g + 1, :] for g in range(GROUPS)], axis=1).astype(F32)
-    hold[pl.ds(18, SHARDS, stride=PER), :] = jnp.broadcast_to(line, (SHARDS, 128))
+    hold[pl.ds(1, SHARDS, stride=PER), :] = jnp.broadcast_to(line, (SHARDS, 128))
     hits = [cand[g : g + 1, :] == shard for g in range(GROUPS)]
     any_hit = hits[0] | hits[1] | hits[2] | hits[3]
     rank = dot(bits(any_hit).astype(BF16), earlier)
@@ -148,13 +152,8 @@
         sides[1 - k] = pltpu.roll(sides[1 - k], GSIZE, 1)
         side = even_lanes if k == 0 else odd_lanes
         lines.append(side(sides[0]) + side(sides[1]))
-    hold[pl.ds(16, SHARDS, stride=PER), :] = lines[0] + lines[1]
-    pieces = split3(x[...])
-    for k in range(2):
-        sent = pick(bits(any_hit & (rank == float(k))).astype(BF16), pieces)
-        for j in range(8):
-            hold[pl.ds(8 * k + j, SHARDS, stride=PER), :] = sent[:, 128 * j : 128 * j + 128]
-    copy = pltpu.make_async_copy(hold, out_ref, sems.at[5])
+    hold[pl.ds(2, SHARDS, stride=PER), :] = lines[0] + lines[1]
+    copy = pltpu.make_async_copy(hold, out_ref, sems.at[4])
     copy.start()
     copy.wait()
 
@@ -169,8 +168,8 @@
 
 def slots_kernel(me_ref, got_ref, found_ref, info_ref, slots_ref, most_ref, hold):
     me, column = me_ref[0], me_ref[1]
-    owners = got_ref[pl.ds(17, SHARDS, stride=PER), :].astype(I32)
-    cands = got_ref[pl.ds(18, SHARDS, stride=PER), :].astype(I32)
+    owners = got_ref[pl.ds(0, SHARDS, stride=PER), :].astype(I32)
+    cands = got_ref[pl.ds(1, SHARDS, stride=PER), :].astype(I32)
     hold[0] = owners
     hold[1] = cands
     at = pl.multiple_of(column * NZ, NZ)
@@ -216,7 +215,8 @@
 
 def relay_kernel(me_ref, turn_ref, info_ref, slots_ref, send_ref, take_ref):
     me = me_ref[0]
-    base = (turn_ref[0] * K).astype(F32)
+    base = turn_ref[0].astype(F32)
+    depth_of = send_ref.shape[0] // NZ
     lane = iota((COLV, 128), 1)
     u = iota((COLV, 1), 0)
     info = info_ref[...]
@@ -235,22 +235,22 @@
     leaves = wanted & (lane < NZ) & here
     order = dot(earlier, bits(leaves).astype(BF16))
     place = jnp.where(leaves, order - base, -1.0).T
-    depth = iota((K, COLV), 0).astype(F32)
+    depth = iota((depth_of, COLV), 0).astype(F32)
     rows = jnp.concatenate([bits(place[z : z + 1, :] == depth) for z in range(NZ)], axis=0)
     slot = (owner >> 3) * 16 + rank.astype(I32) * 8 + (u >> 5)
     held = bits((slot == iota((COLV, SLOTS), 1)) & here)
     send_ref[...] = dot(rows.astype(BF16), held.astype(BF16)).astype(BF16)
     comes = ((owner & 7) == lane) & (lane < NZ) & to_me
     order = dot(earlier, bits(comes).astype(BF16)) - base
-    fits = comes & (order >= 0.0) & (order < float(K))
-    at = jnp.sum(jnp.where(fits, lane.astype(F32) * K + order + 1.0, 0.0), axis=1, keepdims=True)
-    found = bits(at == iota((COLV, NZ * K), 1).astype(F32) + 1.0).astype(BF16)
+    fits = comes & (order >= 0.0) & (order < float(depth_of))
+    at = jnp.sum(jnp.where(fits, lane.astype(F32) * depth_of + order + 1.0, 0.0), axis=1, keepdims=True)
+    found = bits(at == iota((COLV, NZ * depth_of), 1).astype(F32) + 1.0).astype(BF16)
     take_ref[...] = dot(slots_ref[...].astype(BF16), found).astype(BF16)
 
 
 def fetch_kernel(got_ref, pieces_ref, out_ref, hold, sems):
     column = iota((SHARDS, ROWS), 1)
-    asked = got_ref[pl.ds(17, SHARDS, stride=PER), :].astype(I32)
+    asked = got_ref[pl.ds(0, SHARDS, stride=PER), :].astype(I32)
     pieces = [pieces_ref[i] for i in range(3)]
     copies = []
     for k in range(2):
@@ -263,15 +263,51 @@
     wait_all(copies)
 
 
-def move_kernel(onehot_ref, in_ref, out_ref, hold, sems):
+def send_kernel(onehot_ref, in_ref, out_ref, hold, sems):
     pieces = split3(in_ref[...])
-    half = SLOTS // 2
+    half = onehot_ref.shape[0] // 2
     copies = []
     for c in range(2):
         hold[c] = pick(onehot_ref[c * half : (c + 1) * half, :], pieces)
         copies.append(
             pltpu.make_async_copy(hold.at[c], out_ref.at[pl.ds(c * half, half), :], sems.at[c])
         )
+        copies[-1].start()
+    wait_all(copies)
+
+
+def put_kernel(first, onehot_ref, in_ref, both_ref, out_ref, hold, sems):
+    pieces = split3(in_ref[...])
+    half = SLOTS // 2
+    at = [out_ref.at[pl.ds(c * half, half), pl.ds(first, D)] for c in range(2)]
+    copies = []
+    for c in range(2):
+        hold[c] = pick(onehot_ref[c * half : (c + 1) * half, :], pieces)
+        copies.append(pltpu.make_async_copy(hold.at[c], at[c], sems.at[c]))
+        copies[-1].start()
+    wait_all(copies)
+
+
+def add_kernel(onehot_ref, in_ref, both_ref, out_ref, hold, sems):
+    at = out_ref.at[:, pl.ds(D, D)]
+    copy = pltpu.make_async_copy(at, hold, sems.at[0])
+    copy.start()
+    copy.wait()
+    hold[...] += pick(onehot_ref[...], split3(in_ref[...]))
+    copy = pltpu.make_async_copy(hold, at, sems.at[1])
+    copy.start()
+    copy.wait()
+
+
+def vectors_kernel(slots_ref, in_ref, out_ref, hold, sems):
+    onehot = slots_ref[...].astype(BF16)
+    pieces = split3(in_ref[...])
+    half = SLOTS // 2
+    copies = []
+    for c in range(2):
+        hold[c] = pick(onehot[c * half : (c + 1) * half, :], pieces)
+        target = out_ref.at[pl.ds(c * half, half), pl.ds(0, D)]
+        copies.append(pltpu.make_async_copy(hold.at[c], target, sems.at[c]))
         copies[-1].start()
     wait_all(copies)
 
@@ -292,33 +328,23 @@
     return dot(hi, chi, NT) + (dot(hi, cmid, NT) + dot(mid, chi, NT) + small)
 
 
-def near_kernel(got_ref, pieces_ref, norms_ref, x_ref, rows_ref, out_ref):
-    line = got_ref[pl.ds(16, SHARDS, stride=PER), :]
-    for k in range(2):
-        at = slice(8 * k, 8 * k + 8)
-        for j in range(8):
-            part = got_ref[pl.ds(8 * k + j, SHARDS, stride=PER), :]
-            x_ref[:, at, 128 * j : 128 * j + 128] = part.reshape(COLS, 8, 128)
-        rows_ref[:, at, :] = line.astype(I32).reshape(COLS, 8, 128)
-        line = pltpu.roll(line, GSIZE, 1)
-    x = x_ref[...].reshape(SLOTS, D)
+def loss_kernel(both_ref, got_ref, pieces_ref, norms_ref, out_ref):
+    line = got_ref[pl.ds(2, SHARDS, stride=PER), :].astype(I32)
+    rows = [line, pltpu.roll(line, GSIZE, 1)]
+    rows = jnp.concatenate([a.reshape(COLS, 1, NZ, 128) for a in rows], axis=1).reshape(SLOTS, 128)
+    rows = rows & (ROWS - 1)
+    x = both_ref[:, :D]
+    r = x - both_ref[:, D:]
     square = jnp.sum(x * x, axis=1, keepdims=True)
-    table = square - 2.0 * scores(x, pieces_ref) + norms_ref[0:1, :]
-    out_ref[...] = lookup(table, rows_ref[...].reshape(SLOTS, 128))
-
-
-def loss_kernel(p_ref, x_ref, rows_ref, near_ref, pieces_ref, out_ref):
-    x = x_ref[...].reshape(SLOTS, D)
-    rows = rows_ref[...].reshape(SLOTS, 128)
-    r = x - p_ref[...]
+    near = square - 2.0 * scores(x, pieces_ref) + norms_ref[0:1, :]
     hi = r.astype(BF16)
     mid = (r - hi.astype(F32)).astype(BF16)
     chi, cmid = pieces_ref[0], pieces_ref[1]
     table = dot(hi, chi, NT) + (dot(hi, cmid, NT) + dot(mid, chi, NT))
     rx = jnp.sum(r * x, axis=1, keepdims=True)
     rr = jnp.sum(r * r, axis=1, keepdims=True)
-    gap = rx - lookup(table, rows)
-    loss = (near_ref[...] + amplify * gap * gap / (rr + tiny)) / D
+    gap = rx - table
+    loss = lookup((near + amplify * gap * gap / (rr + tiny)) / D, rows)
     loss = loss.reshape(COLS, 2, NZ, 128)
     second = pltpu.roll(loss[:, 1].reshape(COLS * NZ, 128), GSIZE, 1)
     first = loss[:, 0].reshape(COLS * NZ, 128)
@@ -351,25 +377,25 @@
     plane = ("y", "x")
     column = lax.axis_index(("y", "x")).astype(I32)
     me = jnp.stack([lax.axis_index("z").astype(I32), column])
-    with jax.named_scope("requests_and_vectors"):
+    with jax.named_scope("column_vectors"):
+        vectors = lax.all_gather(new_vectors, "z", axis=0, tiled=True)
+    with jax.named_scope("requests"):
         [sent] = call(
             request_kernel,
             [shape((PER * SHARDS, 128))],
             primary_owner.T,
             primary_row.T,
             cand_owner.T,
-            new_vectors,
             cand_row,
-            far_in=(0, 1, 2, 3, 4),
+            far_in=(0, 1, 2, 3),
             far_out=(0,),
             scratch=[
                 pltpu.VMEM((1, V), I32),
                 pltpu.VMEM((1, V), I32),
                 pltpu.VMEM((GROUPS, V), I32),
-                pltpu.VMEM((V, D), F32),
                 pltpu.VMEM((V, GROUPS * GSIZE), I32),
                 pltpu.VMEM((PER * SHARDS, 128), F32),
-                copies_semaphores(6),
+                copies_semaphores(5),
             ],
             name="request",
         )
@@ -402,61 +428,71 @@
     most = most[:1, :1]
     most = jnp.maximum(most, lax.ppermute(most, "rep", [(0, 1), (1, 0)]))[0, 0]
 
-    def relay(turn):
-        return call(
+    halves = [pltpu.VMEM((2, SLOTS // 2, D), F32), copies_semaphores(2)]
+    pair = [shape((SLOTS, 2 * D))]
+
+    def across(base, depth):
+        send, take = call(
             relay_kernel,
-            [shape((NZ * K, SLOTS), BF16), shape((SLOTS, NZ * K), BF16)],
+            [shape((NZ * depth, SLOTS), BF16), shape((SLOTS, NZ * depth), BF16)],
             me,
-            turn.reshape(1),
+            base.reshape(1),
             info,
             slots,
             smem=(0, 1),
             name="relay",
         )
-
-    def across(send, take):
-        def move(onehot, source, name):
-            [moved] = call(
-                move_kernel,
-                [shape((SLOTS, D))],
-                onehot,
-                source,
-                far_out=(0,),
-                scratch=[pltpu.VMEM((2, SLOTS // 2, D), F32), copies_semaphores(2)],
-                name=name,
-            )
-            return moved
-
-        leaving = move(send, fetched, "send")
-        got = swap(leaving.reshape(NZ, K, D), "z").reshape(NZ * K, D)
-        return move(take, got, "take")
+        [leaving] = call(
+            send_kernel,
+            [shape((NZ * depth, D))],
+            send,
+            fetched,
+            far_out=(0,),
+            scratch=[pltpu.VMEM((2, NZ * depth // 2, D), F32), copies_semaphores(2)],
+            name="send",
+        )
+        return take, swap(leaving.reshape(NZ, depth, D), "z").reshape(NZ * depth, D)
 
     def more(state):
-        turn, total = state
-        return turn + 1, total + across(*relay(turn))
-
+        base, both = state
+        take, got = across(base, LATER)
+        [both] = call(
+            add_kernel,
+            pair,
+            take,
+            got,
+            both,
+            far_in=(2,),
+            far_out=(0,),
+            alias={2: 0},
+            scratch=[pltpu.VMEM((SLOTS, D), F32), copies_semaphores(2)],
+            name="add",
+        )
+        return base + LATER, both
+
+    with jax.named_scope("vectors_out"):
+        [both] = call(
+            vectors_kernel, pair, slots, vectors, far_out=(0,), scratch=halves, name="vectors"
+        )
     with jax.named_scope("primary_across"):
-        primaries = across(*relay(jnp.int32(0)))
-        _, primaries = lax.while_loop(lambda s: s[0] * K < most, more, (jnp.int32(1), primaries))
-    x, rows, near = call(
-        near_kernel,
-        [shape((COLS, 16, D)), shape((COLS, 16, 128), I32), shape((SLOTS, 128))],
-        arrived,
-        pieces,
-        norms,
-        name="near",
-    )
-    with jax.named_scope("primaries_out"):
-        primaries = swap(primaries.reshape(COLS, 16, D), plane).reshape(SLOTS, D)
+        take, got = across(jnp.int32(0), K)
+        [both] = call(
+            functools.partial(put_kernel, D),
+            pair,
+            take,
+            got,
+            both,
+            far_in=(2,),
+            far_out=(0,),
+            alias={2: 0},
+            scratch=halves,
+            name="put",
+        )
+        _, both = lax.while_loop(lambda s: s[0] < most, more, (jnp.int32(K), both))
+    with jax.named_scope("out_to_owners"):
+        both = swap(both.reshape(COLS, 16, 2 * D), plane).reshape(SLOTS, 2 * D)
     [losses] = call(
-        loss_kernel,
-        [shape((SHARDS, 128))],
-        primaries,
-        x,
-        rows,
-        near,
-        pieces,
-        name="loss",
+        loss_kernel, [shape((SHARDS, 128))], both, arrived, pieces, norms, name="loss"
     )
     with jax.named_scope("losses_back"):
         back = swap(losses.reshape(SHARDS, 1, 128), ("y", "x", "z")).reshape(SHARDS, 128)

time: 156 us -> 161 us (1.032)
  blocking collectives: 0 us -> 33.5 us
  waiting for transfers between devices: 84 us -> 58.3 us
  between operations: 1.44 us -> 14.8 us
  starting transfers between devices: 39.5 us -> 32 us
  Pallas kernels: 23.2 us -> 18.2 us
  local copies, waits for them, and re-layouts: 6.3 us -> 3.5 us
    all_to_all x5 -> x4, waiting for transfers between devices: 82.9 us -> 34.8 us  [swap(): return lax.all_to_all(a, axes, split_axis=0, concat_axis=0, tiled=True)]
    all_to_all x0 -> x1, blocking collectives: none -> 33.5 us  [swap(): return lax.all_to_all(a, axes, split_axis=0, concat_axis=0, tiled=True)]
    all_gather x0 -> x1, waiting for transfers between devices: none -> 21.5 us  [shards(): vectors = lax.all_gather(new_vectors, 'z', axis=0, tiled=True)]
    all_to_all x5 -> x4, starting transfers between devices: 39.5 us -> 32 us  [swap(): return lax.all_to_all(a, axes, split_axis=0, concat_axis=0, tiled=True)]
    pallas_call x10, Pallas kernels: 23.2 us -> 18.2 us  [call(): pl.pallas_call(kernel, out_shape=out_shape, in_specs=specs, out_specs=[HB...]
    unnamed x15 -> x11, local copies, waits for them, and re-layouts: 5.75 us -> 2.91 us
  transfers between devices with their start and end apart: 6 -> 6, of which waited for: 6 -> 6; matrix products, arithmetic and copies ran while one was open for 1% -> 0% of each run, Pallas kernels for 6% -> 4%
where the time goes in v4:
time: 161 us; the launch traced here: 160 us
  waiting for transfers between devices  58.3 us (36%)
  blocking collectives  33.5 us (21%)
  starting transfers between devices  32 us (20%)
  Pallas kernels  18.2 us (11%)
  between operations  14.8 us (9%)
  local copies, waits for them, and re-layouts  3.5 us (2%)
    all_to_all x4, waiting for transfers between devices, swap(): return lax.all_to_all(a, axes, split_axis=0, concat_axis=0, tiled=True)  34.8 us
    all_to_all x1, blocking collectives, swap(): return lax.all_to_all(a, axes, split_axis=0, concat_axis=0, tiled=True)  33.5 us
    all_to_all x4, starting transfers between devices, swap(): return lax.all_to_all(a, axes, split_axis=0, concat_axis=0, tiled=True)  32 us
    all_gather x1, waiting for transfers between devices, shards(): vectors = lax.all_gather(new_vectors, 'z', axis=0, tiled=True)  21.5 us
    pallas_call x10, Pallas kernels, call(): pl.pallas_call(kernel, out_shape=out_shape, in_specs=specs, out_specs=[HB...  18.2 us
  transfers between devices with their start and end apart: 6, of which 6 were waited for; matrix products, arithmetic and copies ran while one was open for 0% of the time, Pallas kernels for 4%

profile of v4, /device:TPU:2, one launch (start us, length us, event | category | flops | bytes accessed | tf_op | source)
XLA Modules:
  0.0 160.4 jit_solution(8868701092748967508)
XLA Ops:
  6.5 2.0 %request.1 = f32[384,128]{1,0:T(8,128)} custom-call(s32[1,32]{1,0:T(1,128)} %bitcast.40, s32[1,32]{1,0:T(1,128)} %bitcast.41, s32[4,32]{1,0:T(4,128)} %bitcast.39, s32[32,256]{1,0:T(8,128)} %rows_ref.1), custom_call_target="tpu_custom_call" | custom-call | tf_op jit(solution)/shard_map/requests/request/pallas_call | solution.py:44
  8.6 15.4 %all-to-all-start.1 = ((f32[128,1,384]{2,1,0:T(1,128)}), f32[128,1,384]{2,1,0:T(1,128)S(1)}, u32[]{:S(2)}, u32[]{:S(2)}) async-start(f32[128,1,384]{2,1,0:T(1,128)} %bitcast.38), calls=%async_computation.1 | async-start | bytes 393216 | tf_op jit(solution)/shard_map/requests/all_to_all | solution.py:373
  24.0 1.6 copy-done.2
  25.6 1.5 prepare.1
  27.1 9.3 %all-to-all-done.1 = f32[128,1,384]{2,1,0:T(1,128)S(1)} async-done(((f32[128,1,384]{2,1,0:T(1,128)}), f32[128,1,384]{2,1,0:T(1,128)S(1)}, u32[]{:S(2)}, u32[]{:S(2)}) %all-to-all-start.1) | async-done | bytes 196640 | tf_op jit(solution)/shard_map/requests/all_to_all | solution.py:373
  36.4 1.9 %fetch.1.found_ref = f32[16,16,1024]{2,1,0:T(8,128)} custom-call(f32[384,128]{1,0:T(8,128)S(1)} %bitcast.29, bf16[3,512,1024]{2,1,0:T(8,128)(2,1)S(1)} %get-tuple-element.52.pieces_ref), custom_call_target="tpu_custom_call" | custom-call | tf_op jit(solution)/shard_map/primary_rows/fetch/pallas_call | solution.py:44
  38.3 5.7 %all-to-all-start.2 = ((f32[16,16,1024]{2,1,0:T(8,128)}), f32[16,16,1024]{2,1,0:T(8,128)S(1)}, u32[]{:S(2)}, u32[]{:S(2)}) async-start(f32[16,16,1024]{2,1,0:T(8,128)} %fetch.1.found_ref), calls=%async_computation.2 | async-start | bytes 2097152 | tf_op jit(solution)/shard_map/primary_rows/all_to_all | solution.py:373
  44.0 0.7 all-gather.2.cloned.1.call-update
  44.7 1.9 %slots.1 = (s32[256,128]{1,0:T(8,128)S(1)}, f32[256,256]{1,0:T(8,128)S(1)}, s32[8,128]{1,0:T(8,128)S(1)}) custom-call(s32[2]{0:T(128)S(1)} %pad_add_fusion.me_ref, f32[384,128]{1,0:T(8,128)S(1)} %bitcast.30, f32[16,16,1024]{2,1,0:T(8,128)} %fetch.1.found_ref), custom_call_target="tpu_custom_call" | custom-call | tf_op jit(solution)/shard_map/slots/pallas_call | solution.py:44
  46.7 1.7 %relay.2 = (bf16[256,256]{1,0:T(8,128)(2,1)S(1)}, bf16[256,256]{1,0:T(8,128)(2,1)S(1)}) custom-call(s32[2]{0:T(128)S(1)} %pad_add_fusion.me_ref, s32[1]{0:T(128)} %constant.23.clone.1.turn_ref, s32[256,128]{1,0:T(8,128)S(1)} %get-tuple-element.126.info_ref, f32[256,256]{1,0:T(8,128)S(1)} %get-tuple-element.127.slots_ref), custom_call_target="tpu_custom_call" | custom-call | tf_op jit(solution)/shard_map/primary_across/relay/pallas_call | solution.py:44
  48.3 10.4 %all-to-all-done.2 = f32[16,16,1024]{2,1,0:T(8,128)S(1)} async-done(((f32[16,16,1024]{2,1,0:T(8,128)}), f32[16,16,1024]{2,1,0:T(8,128)S(1)}, u32[]{:S(2)}, u32[]{:S(2)}) %all-to-all-start.2) | async-done | bytes 1048608 | tf_op jit(solution)/shard_map/primary_rows/all_to_all | solution.py:373
  58.8 1.5 send.2
  60.3 3.6 %all-to-all-start.3 = ((f32[8,32,1024]{2,1,0:T(8,128)}), f32[8,32,1024]{2,1,0:T(8,128)S(1)}, u32[]{:S(2)}, u32[]{:S(2)}) async-start(f32[8,32,1024]{2,1,0:T(8,128)} %bitcast.37), calls=%async_computation.3 | async-start | bytes 2097152 | tf_op jit(solution)/shard_map/primary_across/all_to_all | solution.py:373
  64.5 1.3 collective-permute-done
  67.1 21.5 %all-gather.2.cloned.1.call-done.in_ref = f32[256,1024]{1,0:T(8,128)} async-done(((f32[32,1024]{1,0:T(8,128)}), f32[256,1024]{1,0:T(8,128)}) %all-gather.2.cloned.1.call-update) | async-done | bytes 1048592 | tf_op jit(solution)/shard_map/column_vectors/all_gather | solution.py:381
  88.6 1.2 copy-done.3
  89.8 1.5 vectors.1.both_ref
  91.3 4.1 %all-to-all-done.3 = f32[8,32,1024]{2,1,0:T(8,128)S(1)} async-done(((f32[8,32,1024]{2,1,0:T(8,128)}), f32[8,32,1024]{2,1,0:T(8,128)S(1)}, u32[]{:S(2)}, u32[]{:S(2)}) %all-to-all-start.3) | async-done | bytes 1048608 | tf_op jit(solution)/shard_map/primary_across/all_to_all | solution.py:373
  95.4 1.5 put.1
  96.9 33.5 %all_to_all.31 = f32[16,16,2048]{2,1,0:T(8,128)S(1)} all-to-all(f32[16,16,2048]{2,1,0:T(8,128)} %bitcast.33), channel_id=1, replica_groups=mesh['y'=4,'x'=4,'z'=8,'rep'=2] {'y','x'}, dimensions={0} | all-to-all | bytes 4194304 | tf_op jit(solution)/shard_map/out_to_owners/all_to_all | solution.py:373
  130.4 3.6 %loss.1 = f32[128,128]{1,0:T(8,128)} custom-call(f32[256,2048]{1,0:T(8,128)S(1)} %bitcast.27, f32[384,128]{1,0:T(8,128)S(1)} %bitcast.31, bf16[3,512,1024]{2,1,0:T(8,128)(2,1)S(1)} %copy-done.1, f32[8,512]{1,0:T(8,128)S(1)} %get-tuple-element.59.norms_ref), custom_call_target="tpu_custom_call" | custom-call | tf_op jit(solution)/shard_map/loss/pallas_call | solution.py:44
  134.1 7.3 %all-to-all-start.5 = ((f32[128,1,128]{2,1,0:T(1,128)}), f32[128,1,128]{2,1,0:T(1,128)S(1)}, u32[]{:S(2)}, u32[]{:S(2)}) async-start(f32[128,1,128]{2,1,0:T(1,128)} %bitcast.17), calls=%async_computation.5 | async-start | bytes 131072 | tf_op jit(solution)/shard_map/losses_back/all_to_all | solution.py:373
  141.5 11.0 %all-to-all-done.5 = f32[128,1,128]{2,1,0:T(1,128)S(1)} async-done(((f32[128,1,128]{2,1,0:T(1,128)}), f32[128,1,128]{2,1,0:T(1,128)S(1)}, u32[]{:S(2)}, u32[]{:S(2)}) %all-to-all-start.5) | async-done | bytes 65568 | tf_op jit(solution)/shard_map/losses_back/all_to_all | solution.py:373
  152.4 1.1 collect.1
  (14 shorter events, 0.8 us)
Async XLA Ops:
  8.6 27.8 %all-to-all-start.1 = ((f32[128,1,384]{2,1,0:T(1,128)}), f32[128,1,384]{2,1,0:T(1,128)S(1)}, u32[]{:S(2)}, u32[]{:S(2)}) async-start(f32[128,1,384]{2,1,0:T(1,128)} %bitcast.38), calls=%async_computation.1 | async-start | bytes 393216 | tf_op jit(solution)/shard_map/requests/all_to_all | solution.py:373
  24.0 1.6 copy-start.2
  27.1 11.2 %copy-start = (bf16[3,512,1024]{2,1,0:T(8,128)(2,1)}, bf16[3,512,1024]{2,1,0:T(8,128)(2,1)S(1)}, u32[]{:S(2)}) copy-start(bf16[3,512,1024]{2,1,0:T(8,128)(2,1)S(1)} %get-tuple-element.52.pieces_ref) | copy-start | bytes 9437188
  38.3 20.5 %all-to-all-start.2 = ((f32[16,16,1024]{2,1,0:T(8,128)}), f32[16,16,1024]{2,1,0:T(8,128)S(1)}, u32[]{:S(2)}, u32[]{:S(2)}) async-start(f32[16,16,1024]{2,1,0:T(8,128)} %fetch.1.found_ref), calls=%async_computation.2 | async-start | bytes 2097152 | tf_op jit(solution)/shard_map/primary_rows/all_to_all | solution.py:373
  43.9 44.7 %all-gather.2.cloned.1.call-start = ((), (), s32[]{:S(2)}) async-start(), calls=%async_computation.6 | async-start | bytes 1179648 | tf_op jit(solution)/shard_map/column_vectors/all_gather | solution.py:381
  60.3 35.0 %all-to-all-start.3 = ((f32[8,32,1024]{2,1,0:T(8,128)}), f32[8,32,1024]{2,1,0:T(8,128)S(1)}, u32[]{:S(2)}, u32[]{:S(2)}) async-start(f32[8,32,1024]{2,1,0:T(8,128)} %bitcast.37), calls=%async_computation.3 | async-start | bytes 2097152 | tf_op jit(solution)/shard_map/primary_across/all_to_all | solution.py:373
  64.5 1.3 collective-permute-start
  88.6 1.2 copy-start.3
  96.9 33.5 %copy-start.1 = (bf16[3,512,1024]{2,1,0:T(8,128)(2,1)S(1)}, bf16[3,512,1024]{2,1,0:T(8,128)(2,1)}, u32[]{:S(2)}) copy-start(bf16[3,512,1024]{2,1,0:T(8,128)(2,1)} %copy-done) | copy-start | bytes 9437188
  130.4 11.0 %copy-start.4 = (s32[32,4]{0,1:T(4,128)S(1)}, s32[32,4]{0,1:T(4,128)}, u32[]{:S(2)}) copy-start(s32[32,4]{0,1:T(4,128)} %param.12) | copy-start | bytes 1540
  134.1 18.4 %all-to-all-start.5 = ((f32[128,1,128]{2,1,0:T(1,128)}), f32[128,1,128]{2,1,0:T(1,128)S(1)}, u32[]{:S(2)}, u32[]{:S(2)}) async-start(f32[128,1,128]{2,1,0:T(1,128)} %bitcast.17), calls=%async_computation.5 | async-start | bytes 131072 | tf_op jit(solution)/shard_map/losses_back/all_to_all | solution.py:373
Sparse Core Ops, SparseCore 0:
  46.5 41.9 all-gather.1

commit v5 on v4

--- a/solution.py
+++ b/solution.py
@@ -20,6 +20,7 @@
 K = 32
 LATER = 16
 PER = 3
+FIRST = (2, -2, 1, -1)
 amplify = 1.0
 tiny = 1e-06
 
@@ -248,7 +249,8 @@
     take_ref[...] = dot(slots_ref[...].astype(BF16), found).astype(BF16)
 
 
-def fetch_kernel(got_ref, pieces_ref, out_ref, hold, sems):
+def fetch_kernel(got_ref, pieces_ref, *rest):
+    out_ref, hold, sems = rest[-3:]
     column = iota((SHARDS, ROWS), 1)
     asked = got_ref[pl.ds(0, SHARDS, stride=PER), :].astype(I32)
     pieces = [pieces_ref[i] for i in range(3)]
@@ -263,7 +265,8 @@
     wait_all(copies)
 
 
-def send_kernel(onehot_ref, in_ref, out_ref, hold, sems):
+def send_kernel(onehot_ref, in_ref, *rest):
+    out_ref, hold, sems = rest[-3:]
     pieces = split3(in_ref[...])
     half = onehot_ref.shape[0] // 2
     copies = []
@@ -299,15 +302,23 @@
     copy.wait()
 
 
-def vectors_kernel(slots_ref, in_ref, out_ref, hold, sems):
+def vectors_kernel(me_ref, slots_ref, *rest):
+    parts, out_ref, column, hold, sems = rest[:NZ], rest[-4], rest[-3], rest[-2], rest[-1]
+    me = me_ref[0]
+    copies = []
+    for i, part in enumerate(parts):
+        at = pl.multiple_of(((me + i) & 7) * V, V)
+        copies.append(pltpu.make_async_copy(part, column.at[pl.ds(at, V), :], sems.at[i]))
+    start_all(copies)
     onehot = slots_ref[...].astype(BF16)
-    pieces = split3(in_ref[...])
+    wait_all(copies)
+    pieces = split3(column[...])
     half = SLOTS // 2
     copies = []
     for c in range(2):
         hold[c] = pick(onehot[c * half : (c + 1) * half, :], pieces)
         target = out_ref.at[pl.ds(c * half, half), pl.ds(0, D)]
-        copies.append(pltpu.make_async_copy(hold.at[c], target, sems.at[c]))
+        copies.append(pltpu.make_async_copy(hold.at[c], target, sems.at[NZ + c]))
         copies[-1].start()
     wait_all(copies)
 
@@ -377,8 +388,15 @@
     plane = ("y", "x")
     column = lax.axis_index(("y", "x")).astype(I32)
     me = jnp.stack([lax.axis_index("z").astype(I32), column])
+    def along_z(block, step):
+        return lax.ppermute(block, "z", [(z, (z - step) % NZ) for z in range(NZ)])
+
     with jax.named_scope("column_vectors"):
-        vectors = lax.all_gather(new_vectors, "z", axis=0, tiled=True)
+        blocks = {0: new_vectors}
+        for step in (2, -2, 1, -1, 4):
+            blocks[step] = along_z(new_vectors, step)
+        blocks[3] = along_z(blocks[2], 1)
+        blocks[-3] = along_z(blocks[-2], -1)
     with jax.named_scope("requests"):
         [sent] = call(
             request_kernel,
@@ -409,6 +427,8 @@
             [shape((COLS, 16, D))],
             arrived,
             pieces,
+            *[blocks[o] for o in FIRST],
+            far_in=tuple(range(2, 2 + len(FIRST))),
             far_out=(0,),
             scratch=[pltpu.VMEM((2, COLS, 8, D), F32), copies_semaphores(2)],
             name="fetch",
@@ -431,7 +451,7 @@
     halves = [pltpu.VMEM((2, SLOTS // 2, D), F32), copies_semaphores(2)]
     pair = [shape((SLOTS, 2 * D))]
 
-    def across(base, depth):
+    def across(base, depth, *after):
         send, take = call(
             relay_kernel,
             [shape((NZ * depth, SLOTS), BF16), shape((SLOTS, NZ * depth), BF16)],
@@ -447,6 +467,8 @@
             [shape((NZ * depth, D))],
             send,
             fetched,
+            *after,
+            far_in=tuple(range(2, 2 + len(after))),
             far_out=(0,),
             scratch=[pltpu.VMEM((2, NZ * depth // 2, D), F32), copies_semaphores(2)],
             name="send",
@@ -472,10 +494,19 @@
 
     with jax.named_scope("vectors_out"):
         [both] = call(
-            vectors_kernel, pair, slots, vectors, far_out=(0,), scratch=halves, name="vectors"
+            vectors_kernel,
+            pair,
+            me,
+            slots,
+            *[blocks[o] for o in (0, 1, 2, 3, 4, -3, -2, -1)],
+            smem=(0,),
+            far_in=tuple(range(2, 2 + NZ)),
+            far_out=(0,),
+            scratch=[pltpu.VMEM((COLV, D), F32), halves[0], copies_semaphores(NZ + 2)],
+            name="vectors",
         )
     with jax.named_scope("primary_across"):
-        take, got = across(jnp.int32(0), K)
+        take, got = across(jnp.int32(0), K, blocks[4], blocks[3], blocks[-3])
         [both] = call(
             functools.partial(put_kernel, D),
             pair,

time: 161 us -> 150 us (0.932)
  waiting for transfers between devices: 58.3 us -> 43 us
  starting transfers between devices: 32 us -> 47 us
  between operations: 14.8 us -> 1.38 us
  Pallas kernels: 18.2 us -> 20.2 us
    all_gather x1 -> x0, waiting for transfers between devices: 21.5 us -> none  [shards(): vectors = lax.all_gather(new_vectors, 'z', axis=0, tiled=True)]
    ppermute x0 -> x7, starting transfers between devices: none -> 12.3 us  [along_z(): return lax.ppermute(block, 'z', [(z, (z - step) % NZ) for z in range(NZ)])]
    ppermute x0 -> x7, waiting for transfers between devices: none -> 8.25 us  [along_z(): return lax.ppermute(block, 'z', [(z, (z - step) % NZ) for z in range(NZ)])]
    all_to_all x4, starting transfers between devices: 32 us -> 34.7 us  [swap(): return lax.all_to_all(a, axes, split_axis=0, concat_axis=0, tiled=True)]
    pallas_call x10, Pallas kernels: 18.2 us -> 20.2 us  [call(): pl.pallas_call(kernel, out_shape=out_shape, in_specs=specs, out_specs=[HB...]
  transfers between devices with their start and end apart: 6 -> 12, of which waited for: 6 -> 8; matrix products, arithmetic and copies ran while one was open for 0% -> 0% of each run, Pallas kernels for 4% -> 6%
where the time goes in v5:
time: 150 us; the launch traced here: 149 us
  starting transfers between devices  47 us (31%)
  waiting for transfers between devices  43 us (29%)
  blocking collectives  34 us (23%)
  Pallas kernels  20.2 us (13%)
  local copies, waits for them, and re-layouts  3.55 us (2%)
    all_to_all x4, waiting for transfers between devices, swap(): return lax.all_to_all(a, axes, split_axis=0, concat_axis=0, tiled=True)  34.7 us
    all_to_all x4, starting transfers between devices, swap(): return lax.all_to_all(a, axes, split_axis=0, concat_axis=0, tiled=True)  34.7 us
    all_to_all x1, blocking collectives, swap(): return lax.all_to_all(a, axes, split_axis=0, concat_axis=0, tiled=True)  34 us
    pallas_call x10, Pallas kernels, call(): pl.pallas_call(kernel, out_shape=out_shape, in_specs=specs, out_specs=[HB...  20.2 us
    ppermute x7, starting transfers between devices, along_z(): return lax.ppermute(block, 'z', [(z, (z - step) % NZ) for z in range(NZ)])  12.3 us
    ppermute x7, waiting for transfers between devices, along_z(): return lax.ppermute(block, 'z', [(z, (z - step) % NZ) for z in range(NZ)])  8.25 us
    unnamed x21, local copies, waits for them, and re-layouts  3.02 us
  transfers between devices with their start and end apart: 12, of which 8 were waited for; matrix products, arithmetic and copies ran while one was open for 0% of the time, Pallas kernels for 6%

profile of v5, /device:TPU:2, one launch (start us, length us, event | category | flops | bytes accessed | tf_op | source)
XLA Modules:
  0.0 149.2 jit_solution(15505983498912065097)
XLA Ops:
  0.0 2.0 %request.1 = f32[384,128]{1,0:T(8,128)} custom-call(s32[1,32]{1,0:T(1,128)} %bitcast.40, s32[1,32]{1,0:T(1,128)} %bitcast.41, s32[4,32]{1,0:T(4,128)} %bitcast.39, s32[32,256]{1,0:T(8,128)} %rows_ref.1), custom_call_target="tpu_custom_call" | custom-call | tf_op jit(solution)/shard_map/requests/request/pallas_call | solution.py:45
  2.0 15.4 %all-to-all-start.1 = ((f32[128,1,384]{2,1,0:T(1,128)}), f32[128,1,384]{2,1,0:T(1,128)S(1)}, u32[]{:S(2)}, u32[]{:S(2)}) async-start(f32[128,1,384]{2,1,0:T(1,128)} %bitcast.38), calls=%async_computation.1 | async-start | bytes 393216 | tf_op jit(solution)/shard_map/requests/all_to_all | solution.py:384
  17.5 3.7 %collective-permute-start = (f32[32,1024]{1,0:T(8,128)}, f32[32,1024]{1,0:T(8,128)S(1)}, u32[]{:S(2)}, u32[]{:S(2)}) collective-permute-start(f32[32,1024]{1,0:T(8,128)} %rest_0_.1), channel_id=1, source_target_pairs={{0,12},{2,14},{4,0},{6,2},{8,4},{10,6},{12,8},{14,10},{1,13},{3,15... | collective-permute-start | bytes 393224 | tf_op jit(solution)/shard_map/column_vectors/ppermute | solution.py:392
  21.1 3.2 %collective-permute-start.2 = (f32[32,1024]{1,0:T(8,128)}, f32[32,1024]{1,0:T(8,128)S(1)}, u32[]{:S(2)}, u32[]{:S(2)}) collective-permute-start(f32[32,1024]{1,0:T(8,128)} %rest_0_.1), channel_id=1, source_target_pairs={{0,14},{2,0},{4,2},{6,4},{8,6},{10,8},{12,10},{14,12},{1,15},{3,1}... | collective-permute-start | bytes 393224 | tf_op jit(solution)/shard_map/column_vectors/ppermute | solution.py:392
  24.4 1.6 %copy-done.2 = f32[512,1024]{1,0:T(8,128)S(1)} copy-done((f32[512,1024]{1,0:T(8,128)S(1)}, f32[512,1024]{1,0:T(8,128)}, u32[]{:S(2)}) %copy-start.2) | copy-done | bytes 2097176
  27.4 2.8 %collective-permute-done.rest_0_.rest_2_ = f32[32,1024]{1,0:T(8,128)S(1)} collective-permute-done((f32[32,1024]{1,0:T(8,128)}, f32[32,1024]{1,0:T(8,128)S(1)}, u32[]{:S(2)}, u32[]{:S(2)}) %collective-permute-start) | collective-permute-done | bytes 131104 | tf_op jit(solution)/shard_map/column_vectors/ppermute | solution.py:392
  30.2 1.9 %collective-permute-done.1.rest_1_.rest_6_ = f32[32,1024]{1,0:T(8,128)S(1)} collective-permute-done((f32[32,1024]{1,0:T(8,128)}, f32[32,1024]{1,0:T(8,128)S(1)}, u32[]{:S(2)}, u32[]{:S(2)}) %collective-permute-start.1) | collective-permute-done | bytes 131104 | tf_op jit(solution)/shard_map/column_vectors/ppermute | solution.py:392
  33.4 1.9 %fetch.1.found_ref = f32[16,16,1024]{2,1,0:T(8,128)} custom-call(f32[384,128]{1,0:T(8,128)S(1)} %bitcast.29, bf16[3,512,1024]{2,1,0:T(8,128)(2,1)S(1)} %get-tuple-element.52.pieces_ref, f32[32,1024]{1,0:T(8,128)} %copy-done.3, f32[32,1024]{1,0:T(8,128)} %copy-done.4, f32[32,1024]{1,0:T(8,128)} %copy-done.5, f32[32,1024]{1,0:T(8,128)} %collective-permute-done.3.rest_3_.rest_7_), custom_call_target="tpu_custom_call" | custom-call | tf_op jit(solution)/shard_map/primary_rows/fetch/pallas_call | solution.py:45
  35.3 7.7 %all-to-all-start.2 = ((f32[16,16,1024]{2,1,0:T(8,128)}), f32[16,16,1024]{2,1,0:T(8,128)S(1)}, u32[]{:S(2)}, u32[]{:S(2)}) async-start(f32[16,16,1024]{2,1,0:T(8,128)} %fetch.1.found_ref), calls=%async_computation.2 | async-start | bytes 2097152 | tf_op jit(solution)/shard_map/primary_rows/all_to_all | solution.py:384
  43.0 2.8 %collective-permute-start.4 = (f32[32,1024]{1,0:T(8,128)}, f32[32,1024]{1,0:T(8,128)S(1)}, u32[]{:S(2)}, u32[]{:S(2)}) collective-permute-start(f32[32,1024]{1,0:T(8,128)} %rest_0_.1), channel_id=1, source_target_pairs={{0,8},{2,10},{4,12},{6,14},{8,0},{10,2},{12,4},{14,6},{1,9},{3,11}... | collective-permute-start | bytes 393224 | tf_op jit(solution)/shard_map/column_vectors/ppermute | solution.py:392
  45.8 2.7 %collective-permute-start.5 = (f32[32,1024]{1,0:T(8,128)}, f32[32,1024]{1,0:T(8,128)S(1)}, u32[]{:S(2)}, u32[]{:S(2)}) collective-permute-start(f32[32,1024]{1,0:T(8,128)} %copy-done.3), channel_id=1, source_target_pairs={{0,14},{2,0},{4,2},{6,4},{8,6},{10,8},{12,10},{14,12},{1,15},{3,1}... | collective-permute-start | bytes 393224 | tf_op jit(solution)/shard_map/column_vectors/ppermute | solution.py:392
  48.5 1.9 %slots.1 = (s32[256,128]{1,0:T(8,128)S(1)}, f32[256,256]{1,0:T(8,128)S(1)}, s32[8,128]{1,0:T(8,128)S(1)}) custom-call(s32[2]{0:T(128)S(1)} %pad_add_fusion.me_ref, f32[384,128]{1,0:T(8,128)S(1)} %bitcast.30, f32[16,16,1024]{2,1,0:T(8,128)} %fetch.1.found_ref), custom_call_target="tpu_custom_call" | custom-call | tf_op jit(solution)/shard_map/slots/pallas_call | solution.py:45
  50.5 1.7 %relay.2 = (bf16[256,256]{1,0:T(8,128)(2,1)S(1)}, bf16[256,256]{1,0:T(8,128)(2,1)S(1)}) custom-call(s32[2]{0:T(128)S(1)} %pad_add_fusion.me_ref, s32[1]{0:T(128)} %constant.23.clone.1.turn_ref, s32[256,128]{1,0:T(8,128)S(1)} %get-tuple-element.126.info_ref, f32[256,256]{1,0:T(8,128)S(1)} %get-tuple-element.127.slots_ref), custom_call_target="tpu_custom_call" | custom-call | tf_op jit(solution)/shard_map/primary_across/relay/pallas_call | solution.py:45
  52.2 1.8 %collective-permute-done.4.rest_0_.rest_4_ = f32[32,1024]{1,0:T(8,128)S(1)} collective-permute-done((f32[32,1024]{1,0:T(8,128)}, f32[32,1024]{1,0:T(8,128)S(1)}, u32[]{:S(2)}, u32[]{:S(2)}) %collective-permute-start.4) | collective-permute-done | bytes 131104 | tf_op jit(solution)/shard_map/column_vectors/ppermute | solution.py:392
  55.8 1.9 %all-to-all-done.2 = f32[16,16,1024]{2,1,0:T(8,128)S(1)} async-done(((f32[16,16,1024]{2,1,0:T(8,128)}), f32[16,16,1024]{2,1,0:T(8,128)S(1)}, u32[]{:S(2)}, u32[]{:S(2)}) %all-to-all-start.2) | async-done | bytes 1048608 | tf_op jit(solution)/shard_map/primary_rows/all_to_all | solution.py:384
  57.7 1.5 %send.2 = f32[256,1024]{1,0:T(8,128)} custom-call(bf16[256,256]{1,0:T(8,128)(2,1)S(1)} %get-tuple-element.56.onehot_ref, f32[256,1024]{1,0:T(8,128)S(1)} %bitcast.35, f32[32,1024]{1,0:T(8,128)} %copy-done.6, f32[32,1024]{1,0:T(8,128)} %copy-done.7, f32[32,1024]{1,0:T(8,128)} %copy-done.8), custom_call_target="tpu_custom_call" | custom-call | tf_op jit(solution)/shard_map/primary_across/send/pallas_call | solution.py:45
  59.2 4.9 %all-to-all-start.3 = ((f32[8,32,1024]{2,1,0:T(8,128)}), f32[8,32,1024]{2,1,0:T(8,128)S(1)}, u32[]{:S(2)}, u32[]{:S(2)}) async-start(f32[8,32,1024]{2,1,0:T(8,128)} %bitcast.37), calls=%async_computation.3 | async-start | bytes 2097152 | tf_op jit(solution)/shard_map/primary_across/all_to_all | solution.py:384
  64.7 3.4 %vectors.1.both_ref = f32[256,2048]{1,0:T(8,128)} custom-call(s32[2]{0:T(128)S(1)} %pad_add_fusion.me_ref, f32[256,256]{1,0:T(8,128)S(1)} %get-tuple-element.127.slots_ref, f32[32,1024]{1,0:T(8,128)} %rest_0_.1, f32[32,1024]{1,0:T(8,128)} %copy-done.5, f32[32,1024]{1,0:T(8,128)} %copy-done.3, f32[32,1024]{1,0:T(8,128)} %copy-done.7, f32[32,1024]{1,0:T(8,128)} %copy-done.6, ...), custom_call_target="tpu_custom_call" | custom-call | tf_op jit(solution)/shard_map/vectors_out/vectors/pallas_call | solution.py:45
  69.3 21.8 %all-to-all-done.3 = f32[8,32,1024]{2,1,0:T(8,128)S(1)} async-done(((f32[8,32,1024]{2,1,0:T(8,128)}), f32[8,32,1024]{2,1,0:T(8,128)S(1)}, u32[]{:S(2)}, u32[]{:S(2)}) %all-to-all-start.3) | async-done | bytes 1048608 | tf_op jit(solution)/shard_map/primary_across/all_to_all | solution.py:384
  91.1 1.6 %put.1 = f32[256,2048]{1,0:T(8,128)} custom-call(bf16[256,256]{1,0:T(8,128)(2,1)S(1)} %get-tuple-element.55.onehot_ref, f32[256,1024]{1,0:T(8,128)S(1)} %bitcast.28, f32[256,2048]{1,0:T(8,128)} %vectors.1.both_ref), custom_call_target="tpu_custom_call", output_to_operand_aliasing={{}: (2, {})} | custom-call | tf_op jit(solution)/shard_map/primary_across/put/pallas_call | solution.py:45
  92.7 34.0 %all_to_all.31 = f32[16,16,2048]{2,1,0:T(8,128)S(1)} all-to-all(f32[16,16,2048]{2,1,0:T(8,128)} %bitcast.33), channel_id=1, replica_groups=mesh['y'=4,'x'=4,'z'=8,'rep'=2] {'y','x'}, dimensions={0} | all-to-all | bytes 4194304 | tf_op jit(solution)/shard_map/out_to_owners/all_to_all | solution.py:384
  126.7 3.7 %loss.1 = f32[128,128]{1,0:T(8,128)} custom-call(f32[256,2048]{1,0:T(8,128)S(1)} %bitcast.27, f32[384,128]{1,0:T(8,128)S(1)} %bitcast.31, bf16[3,512,1024]{2,1,0:T(8,128)(2,1)S(1)} %copy-done.1, f32[8,512]{1,0:T(8,128)S(1)} %get-tuple-element.59.norms_ref), custom_call_target="tpu_custom_call" | custom-call | tf_op jit(solution)/shard_map/loss/pallas_call | solution.py:45
  130.3 6.6 %all-to-all-start.5 = ((f32[128,1,128]{2,1,0:T(1,128)}), f32[128,1,128]{2,1,0:T(1,128)S(1)}, u32[]{:S(2)}, u32[]{:S(2)}) async-start(f32[128,1,128]{2,1,0:T(1,128)} %bitcast.17), calls=%async_computation.5 | async-start | bytes 131072 | tf_op jit(solution)/shard_map/losses_back/all_to_all | solution.py:384
  137.0 11.0 %all-to-all-done.5 = f32[128,1,128]{2,1,0:T(1,128)S(1)} async-done(((f32[128,1,128]{2,1,0:T(1,128)}), f32[128,1,128]{2,1,0:T(1,128)S(1)}, u32[]{:S(2)}, u32[]{:S(2)}) %all-to-all-start.5) | async-done | bytes 65568 | tf_op jit(solution)/shard_map/losses_back/all_to_all | solution.py:384
  (35 shorter events, 6.5 us)
Async XLA Ops:
  2.0 31.4 %all-to-all-start.1 = ((f32[128,1,384]{2,1,0:T(1,128)}), f32[128,1,384]{2,1,0:T(1,128)S(1)}, u32[]{:S(2)}, u32[]{:S(2)}) async-start(f32[128,1,384]{2,1,0:T(1,128)} %bitcast.38), calls=%async_computation.1 | async-start | bytes 393216 | tf_op jit(solution)/shard_map/requests/all_to_all | solution.py:384
  17.5 12.7 %collective-permute-start = (f32[32,1024]{1,0:T(8,128)}, f32[32,1024]{1,0:T(8,128)S(1)}, u32[]{:S(2)}, u32[]{:S(2)}) collective-permute-start(f32[32,1024]{1,0:T(8,128)} %rest_0_.1), channel_id=1, source_target_pairs={{0,12},{2,14},{4,0},{6,2},{8,4},{10,6},{12,8},{14,10},{1,13},{3,15... | collective-permute-start | bytes 393224 | tf_op jit(solution)/shard_map/column_vectors/ppermute | solution.py:392
  21.1 10.9 %collective-permute-start.1 = (f32[32,1024]{1,0:T(8,128)}, f32[32,1024]{1,0:T(8,128)S(1)}, u32[]{:S(2)}, u32[]{:S(2)}) collective-permute-start(f32[32,1024]{1,0:T(8,128)} %rest_0_.1), channel_id=1, source_target_pairs={{0,4},{2,6},{4,8},{6,10},{8,12},{10,14},{12,0},{14,2},{1,5},{3,7},... | collective-permute-start | bytes 393224 | tf_op jit(solution)/shard_map/column_vectors/ppermute | solution.py:392
  21.1 10.9 %collective-permute-start.2 = (f32[32,1024]{1,0:T(8,128)}, f32[32,1024]{1,0:T(8,128)S(1)}, u32[]{:S(2)}, u32[]{:S(2)}) collective-permute-start(f32[32,1024]{1,0:T(8,128)} %rest_0_.1), channel_id=1, source_target_pairs={{0,14},{2,0},{4,2},{6,4},{8,6},{10,8},{12,10},{14,12},{1,15},{3,1}... | collective-permute-start | bytes 393224 | tf_op jit(solution)/shard_map/column_vectors/ppermute | solution.py:392
  24.4 9.0 %collective-permute-start.3 = (f32[32,1024]{1,0:T(8,128)}, f32[32,1024]{1,0:T(8,128)}, u32[]{:S(2)}, u32[]{:S(2)}) collective-permute-start(f32[32,1024]{1,0:T(8,128)} %rest_0_.1), channel_id=1, source_target_pairs={{0,2},{2,4},{4,6},{6,8},{8,10},{10,12},{12,14},{14,0},{1,3},{3,5},... | collective-permute-start | bytes 393224 | tf_op jit(solution)/shard_map/column_vectors/ppermute | solution.py:392
  24.4 1.6 %copy-start.2 = (f32[512,1024]{1,0:T(8,128)S(1)}, f32[512,1024]{1,0:T(8,128)}, u32[]{:S(2)}) copy-start(f32[512,1024]{1,0:T(8,128)} %c_ref.1) | copy-start | bytes 6291460
  27.4 7.9 %copy-start = (bf16[3,512,1024]{2,1,0:T(8,128)(2,1)}, bf16[3,512,1024]{2,1,0:T(8,128)(2,1)S(1)}, u32[]{:S(2)}) copy-start(bf16[3,512,1024]{2,1,0:T(8,128)(2,1)S(1)} %get-tuple-element.52.pieces_ref) | copy-start | bytes 9437188
  30.2 3.2 %copy-start.3 = (f32[32,1024]{1,0:T(8,128)}, f32[32,1024]{1,0:T(8,128)S(1)}, u32[]{:S(2)}) copy-start(f32[32,1024]{1,0:T(8,128)S(1)} %collective-permute-done.rest_0_.rest_2_) | copy-start | bytes 393220
  32.1 0.7 copy-start.4
  32.7 0.7 copy-start.5
  35.3 22.4 %all-to-all-start.2 = ((f32[16,16,1024]{2,1,0:T(8,128)}), f32[16,16,1024]{2,1,0:T(8,128)S(1)}, u32[]{:S(2)}, u32[]{:S(2)}) async-start(f32[16,16,1024]{2,1,0:T(8,128)} %fetch.1.found_ref), calls=%async_computation.2 | async-start | bytes 2097152 | tf_op jit(solution)/shard_map/primary_rows/all_to_all | solution.py:384
  43.0 10.9 %collective-permute-start.4 = (f32[32,1024]{1,0:T(8,128)}, f32[32,1024]{1,0:T(8,128)S(1)}, u32[]{:S(2)}, u32[]{:S(2)}) collective-permute-start(f32[32,1024]{1,0:T(8,128)} %rest_0_.1), channel_id=1, source_target_pairs={{0,8},{2,10},{4,12},{6,14},{8,0},{10,2},{12,4},{14,6},{1,9},{3,11}... | collective-permute-start | bytes 393224 | tf_op jit(solution)/shard_map/column_vectors/ppermute | solution.py:392
  45.8 9.1 %collective-permute-start.5 = (f32[32,1024]{1,0:T(8,128)}, f32[32,1024]{1,0:T(8,128)S(1)}, u32[]{:S(2)}, u32[]{:S(2)}) collective-permute-start(f32[32,1024]{1,0:T(8,128)} %copy-done.3), channel_id=1, source_target_pairs={{0,14},{2,0},{4,2},{6,4},{8,6},{10,8},{12,10},{14,12},{1,15},{3,1}... | collective-permute-start | bytes 393224 | tf_op jit(solution)/shard_map/column_vectors/ppermute | solution.py:392
  48.5 7.3 %collective-permute-start.6 = (f32[32,1024]{1,0:T(8,128)}, f32[32,1024]{1,0:T(8,128)S(1)}, u32[]{:S(2)}, u32[]{:S(2)}) collective-permute-start(f32[32,1024]{1,0:T(8,128)} %copy-done.4), channel_id=1, source_target_pairs={{0,2},{2,4},{4,6},{6,8},{8,10},{10,12},{12,14},{14,0},{1,3},{3,5},... | collective-permute-start | bytes 393224 | tf_op jit(solution)/shard_map/column_vectors/ppermute | solution.py:392
  53.9 3.8 %copy-start.6 = (f32[32,1024]{1,0:T(8,128)}, f32[32,1024]{1,0:T(8,128)S(1)}, u32[]{:S(2)}) copy-start(f32[32,1024]{1,0:T(8,128)S(1)} %collective-permute-done.4.rest_0_.rest_4_) | copy-start | bytes 393220
  54.9 2.8 %copy-start.7 = (f32[32,1024]{1,0:T(8,128)}, f32[32,1024]{1,0:T(8,128)S(1)}, u32[]{:S(2)}) copy-start(f32[32,1024]{1,0:T(8,128)S(1)} %collective-permute-done.5.rest_1_.rest_3_) | copy-start | bytes 393220
  55.8 1.9 %copy-start.8 = (f32[32,1024]{1,0:T(8,128)}, f32[32,1024]{1,0:T(8,128)S(1)}, u32[]{:S(2)}) copy-start(f32[32,1024]{1,0:T(8,128)S(1)} %collective-permute-done.6.rest_2_.rest_5_) | copy-start | bytes 393220
  59.2 31.9 %all-to-all-start.3 = ((f32[8,32,1024]{2,1,0:T(8,128)}), f32[8,32,1024]{2,1,0:T(8,128)S(1)}, u32[]{:S(2)}, u32[]{:S(2)}) async-start(f32[8,32,1024]{2,1,0:T(8,128)} %bitcast.37), calls=%async_computation.3 | async-start | bytes 2097152 | tf_op jit(solution)/shard_map/primary_across/all_to_all | solution.py:384
  64.7 3.4 %collective-permute-start.7 = (s32[1,1]{1,0:T(1,128)}, s32[1,1]{1,0:T(1,128)}, u32[]{:S(2)}, u32[]{:S(2)}) collective-permute-start(s32[1,1]{1,0:T(1,128)} %slice.3), channel_id=1, source_target_pairs={{0,1},{1,0},{2,3},{3,2},{4,5},{5,4},{6,7},{7,6},{8,9},{9,8},{10,11... | collective-permute-start | bytes 20 | tf_op jit(solution)/shard_map/ppermute | solution.py:449
  92.7 34.0 %copy-start.1 = (bf16[3,512,1024]{2,1,0:T(8,128)(2,1)S(1)}, bf16[3,512,1024]{2,1,0:T(8,128)(2,1)}, u32[]{:S(2)}) copy-start(bf16[3,512,1024]{2,1,0:T(8,128)(2,1)} %copy-done) | copy-start | bytes 9437188
  126.7 10.3 %copy-start.9 = (s32[32,4]{0,1:T(4,128)S(1)}, s32[32,4]{0,1:T(4,128)}, u32[]{:S(2)}) copy-start(s32[32,4]{0,1:T(4,128)} %param.12) | copy-start | bytes 1540
  130.3 17.7 %all-to-all-start.5 = ((f32[128,1,128]{2,1,0:T(1,128)}), f32[128,1,128]{2,1,0:T(1,128)S(1)}, u32[]{:S(2)}, u32[]{:S(2)}) async-start(f32[128,1,128]{2,1,0:T(1,128)} %bitcast.17), calls=%async_computation.5 | async-start | bytes 131072 | tf_op jit(solution)/shard_map/losses_back/all_to_all | solution.py:384

commit v6 on v5

--- a/solution.py
+++ b/solution.py
@@ -18,7 +18,7 @@
 SLOTS = COLS * NZ * 2
 SHARDS = COLS * NZ
 K = 32
-LATER = 16
+NEXT = 8
 PER = 3
 FIRST = (2, -2, 1, -1)
 amplify = 1.0
@@ -265,7 +265,7 @@
     wait_all(copies)
 
 
-def send_kernel(onehot_ref, in_ref, *rest):
+def send_kernel(base_ref, onehot_ref, in_ref, *rest):
     out_ref, hold, sems = rest[-3:]
     pieces = split3(in_ref[...])
     half = onehot_ref.shape[0] // 2
@@ -451,8 +451,8 @@
     halves = [pltpu.VMEM((2, SLOTS // 2, D), F32), copies_semaphores(2)]
     pair = [shape((SLOTS, 2 * D))]
 
-    def across(base, depth, *after):
-        send, take = call(
+    def relay(base, depth):
+        return call(
             relay_kernel,
             [shape((NZ * depth, SLOTS), BF16), shape((SLOTS, NZ * depth), BF16)],
             me,
@@ -462,22 +462,25 @@
             smem=(0, 1),
             name="relay",
         )
+
+    def across(base, send, *after):
+        depth = send.shape[0] // NZ
         [leaving] = call(
             send_kernel,
             [shape((NZ * depth, D))],
+            base.reshape(1),
             send,
             fetched,
             *after,
-            far_in=tuple(range(2, 2 + len(after))),
+            smem=(0,),
+            far_in=tuple(range(3, 3 + len(after))),
             far_out=(0,),
             scratch=[pltpu.VMEM((2, NZ * depth // 2, D), F32), copies_semaphores(2)],
             name="send",
         )
-        return take, swap(leaving.reshape(NZ, depth, D), "z").reshape(NZ * depth, D)
-
-    def more(state):
-        base, both = state
-        take, got = across(base, LATER)
+        return swap(leaving.reshape(NZ, depth, D), "z").reshape(NZ * depth, D)
+
+    def add(take, got, both):
         [both] = call(
             add_kernel,
             pair,
@@ -490,7 +493,16 @@
             scratch=[pltpu.VMEM((SLOTS, D), F32), copies_semaphores(2)],
             name="add",
         )
-        return base + LATER, both
+        return both
+
+    def second(state):
+        base, both = state
+        return base + NEXT, add(next_take, across(base, next_send), both)
+
+    def more(state):
+        base, both = state
+        send, take = relay(base, K)
+        return base + K, add(take, across(base, send), both)
 
     with jax.named_scope("vectors_out"):
         [both] = call(
@@ -506,7 +518,9 @@
             name="vectors",
         )
     with jax.named_scope("primary_across"):
-        take, got = across(jnp.int32(0), K, blocks[4], blocks[3], blocks[-3])
+        send, take = relay(jnp.int32(0), K)
+        got = across(jnp.int32(0), send, blocks[4], blocks[3], blocks[-3])
+        next_send, next_take = relay(jnp.int32(K), NEXT)
         [both] = call(
             functools.partial(put_kernel, D),
             pair,
@@ -519,7 +533,9 @@
             scratch=halves,
             name="put",
         )
-        _, both = lax.while_loop(lambda s: s[0] < most, more, (jnp.int32(K), both))
+        state = (jnp.int32(K), both)
+        state = lax.while_loop(lambda s: (s[0] == K) & (K < most), second, state)
+        _, both = lax.while_loop(lambda s: s[0] < most, more, state)
     with jax.named_scope("out_to_owners"):
         both = swap(both.reshape(COLS, 16, 2 * D), plane).reshape(SLOTS, 2 * D)
     [losses] = call(

time: 150 us -> 150 us (level)
  Pallas kernels: 20.2 us -> 22.3 us
  waiting for transfers between devices: 43 us -> 41 us
    pallas_call x10 -> x11, Pallas kernels: 20.2 us -> 22.3 us  [call(): pl.pallas_call(kernel, out_shape=out_shape, in_specs=specs, out_specs=[HB...]
    all_to_all x4, waiting for transfers between devices: 34.7 us -> 32.8 us  [swap(): return lax.all_to_all(a, axes, split_axis=0, concat_axis=0, tiled=True)]
  transfers between devices with their start and end apart: 12 -> 12, of which waited for: 8 -> 8; matrix products, arithmetic and copies ran while one was open for 0% -> 0% of each run, Pallas kernels for 6% -> 7%
where the time goes in v6:
time: 150 us; the launch traced here: 149 us
  starting transfers between devices  47 us (31%)
  waiting for transfers between devices  41 us (27%)
  blocking collectives  34 us (23%)
  Pallas kernels  22.3 us (15%)
  local copies, waits for them, and re-layouts  3.55 us (2%)
    all_to_all x4, starting transfers between devices, swap(): return lax.all_to_all(a, axes, split_axis=0, concat_axis=0, tiled=True)  34.7 us
    all_to_all x1, blocking collectives, swap(): return lax.all_to_all(a, axes, split_axis=0, concat_axis=0, tiled=True)  34 us
    all_to_all x4, waiting for transfers between devices, swap(): return lax.all_to_all(a, axes, split_axis=0, concat_axis=0, tiled=True)  32.8 us
    pallas_call x11, Pallas kernels, call(): pl.pallas_call(kernel, out_shape=out_shape, in_specs=specs, out_specs=[HB...  22.3 us
    ppermute x7, starting transfers between devices, along_z(): return lax.ppermute(block, 'z', [(z, (z - step) % NZ) for z in range(NZ)])  12.4 us
    ppermute x7, waiting for transfers between devices, along_z(): return lax.ppermute(block, 'z', [(z, (z - step) % NZ) for z in range(NZ)])  8.25 us
    unnamed x21, local copies, waits for them, and re-layouts  3.01 us
  transfers between devices with their start and end apart: 12, of which 8 were waited for; matrix products, arithmetic and copies ran while one was open for 0% of the time, Pallas kernels for 7%

profile of v6, /device:TPU:2, one launch (start us, length us, event | category | flops | bytes accessed | tf_op | source)
XLA Modules:
  0.0 149.3 jit_solution(15167325654184755477)
XLA Ops:
  0.0 2.0 %request.1 = f32[384,128]{1,0:T(8,128)} custom-call(s32[1,32]{1,0:T(1,128)} %bitcast.51, s32[1,32]{1,0:T(1,128)} %bitcast.52, s32[4,32]{1,0:T(4,128)} %bitcast.50, s32[32,256]{1,0:T(8,128)} %rows_ref.1), custom_call_target="tpu_custom_call" | custom-call | tf_op jit(solution)/shard_map/requests/request/pallas_call | solution.py:45
  2.0 15.4 %all-to-all-start.2 = ((f32[128,1,384]{2,1,0:T(1,128)}), f32[128,1,384]{2,1,0:T(1,128)S(1)}, u32[]{:S(2)}, u32[]{:S(2)}) async-start(f32[128,1,384]{2,1,0:T(1,128)} %bitcast.49), calls=%async_computation.2 | async-start | bytes 393216 | tf_op jit(solution)/shard_map/requests/all_to_all | solution.py:384
  17.5 3.7 %collective-permute-start = (f32[32,1024]{1,0:T(8,128)}, f32[32,1024]{1,0:T(8,128)S(1)}, u32[]{:S(2)}, u32[]{:S(2)}) collective-permute-start(f32[32,1024]{1,0:T(8,128)} %rest_0_.1), channel_id=1, source_target_pairs={{0,12},{2,14},{4,0},{6,2},{8,4},{10,6},{12,8},{14,10},{1,13},{3,15... | collective-permute-start | bytes 393224 | tf_op jit(solution)/shard_map/column_vectors/ppermute | solution.py:392
  21.1 3.2 %collective-permute-start.2 = (f32[32,1024]{1,0:T(8,128)}, f32[32,1024]{1,0:T(8,128)S(1)}, u32[]{:S(2)}, u32[]{:S(2)}) collective-permute-start(f32[32,1024]{1,0:T(8,128)} %rest_0_.1), channel_id=1, source_target_pairs={{0,14},{2,0},{4,2},{6,4},{8,6},{10,8},{12,10},{14,12},{1,15},{3,1}... | collective-permute-start | bytes 393224 | tf_op jit(solution)/shard_map/column_vectors/ppermute | solution.py:392
  24.4 1.6 %copy-done.2 = f32[512,1024]{1,0:T(8,128)S(1)} copy-done((f32[512,1024]{1,0:T(8,128)S(1)}, f32[512,1024]{1,0:T(8,128)}, u32[]{:S(2)}) %copy-start.2) | copy-done | bytes 2097176
  27.4 2.7 %collective-permute-done.rest_0_.rest_2_ = f32[32,1024]{1,0:T(8,128)S(1)} collective-permute-done((f32[32,1024]{1,0:T(8,128)}, f32[32,1024]{1,0:T(8,128)S(1)}, u32[]{:S(2)}, u32[]{:S(2)}) %collective-permute-start) | collective-permute-done | bytes 131104 | tf_op jit(solution)/shard_map/column_vectors/ppermute | solution.py:392
  30.2 1.9 %collective-permute-done.1.rest_1_.rest_6_ = f32[32,1024]{1,0:T(8,128)S(1)} collective-permute-done((f32[32,1024]{1,0:T(8,128)}, f32[32,1024]{1,0:T(8,128)S(1)}, u32[]{:S(2)}, u32[]{:S(2)}) %collective-permute-start.1) | collective-permute-done | bytes 131104 | tf_op jit(solution)/shard_map/column_vectors/ppermute | solution.py:392
  33.4 1.9 %fetch.1.found_ref = f32[16,16,1024]{2,1,0:T(8,128)} custom-call(f32[384,128]{1,0:T(8,128)S(1)} %bitcast.39, bf16[3,512,1024]{2,1,0:T(8,128)(2,1)S(1)} %get-tuple-element.88.pieces_ref, f32[32,1024]{1,0:T(8,128)} %copy-done.3, f32[32,1024]{1,0:T(8,128)} %copy-done.4, f32[32,1024]{1,0:T(8,128)} %copy-done.5, f32[32,1024]{1,0:T(8,128)} %collective-permute-done.3.rest_3_.rest_7_), custom_call_target="tpu_custom_call" | custom-call | tf_op jit(solution)/shard_map/primary_rows/fetch/pallas_call | solution.py:45
  35.4 7.7 %all-to-all-start.3 = ((f32[16,16,1024]{2,1,0:T(8,128)}), f32[16,16,1024]{2,1,0:T(8,128)S(1)}, u32[]{:S(2)}, u32[]{:S(2)}) async-start(f32[16,16,1024]{2,1,0:T(8,128)} %fetch.1.found_ref), calls=%async_computation.3 | async-start | bytes 2097152 | tf_op jit(solution)/shard_map/primary_rows/all_to_all | solution.py:384
  43.0 2.8 %collective-permute-start.4 = (f32[32,1024]{1,0:T(8,128)}, f32[32,1024]{1,0:T(8,128)S(1)}, u32[]{:S(2)}, u32[]{:S(2)}) collective-permute-start(f32[32,1024]{1,0:T(8,128)} %rest_0_.1), channel_id=1, source_target_pairs={{0,8},{2,10},{4,12},{6,14},{8,0},{10,2},{12,4},{14,6},{1,9},{3,11}... | collective-permute-start | bytes 393224 | tf_op jit(solution)/shard_map/column_vectors/ppermute | solution.py:392
  45.8 2.7 %collective-permute-start.5 = (f32[32,1024]{1,0:T(8,128)}, f32[32,1024]{1,0:T(8,128)S(1)}, u32[]{:S(2)}, u32[]{:S(2)}) collective-permute-start(f32[32,1024]{1,0:T(8,128)} %copy-done.3), channel_id=1, source_target_pairs={{0,14},{2,0},{4,2},{6,4},{8,6},{10,8},{12,10},{14,12},{1,15},{3,1}... | collective-permute-start | bytes 393224 | tf_op jit(solution)/shard_map/column_vectors/ppermute | solution.py:392
  48.6 1.9 %slots.1 = (s32[256,128]{1,0:T(8,128)S(1)}, f32[256,256]{1,0:T(8,128)S(1)}, s32[8,128]{1,0:T(8,128)S(1)}) custom-call(s32[2]{0:T(128)S(1)} %pad_add_fusion.me_ref, f32[384,128]{1,0:T(8,128)S(1)} %bitcast.40, f32[16,16,1024]{2,1,0:T(8,128)} %fetch.1.found_ref), custom_call_target="tpu_custom_call" | custom-call | tf_op jit(solution)/shard_map/slots/pallas_call | solution.py:45
  50.5 1.7 %relay.3 = (bf16[256,256]{1,0:T(8,128)(2,1)S(1)}, bf16[256,256]{1,0:T(8,128)(2,1)S(1)}) custom-call(s32[2]{0:T(128)S(1)} %pad_add_fusion.me_ref, s32[1]{0:T(128)} %constant.28.clone.1.turn_ref.base_ref, s32[256,128]{1,0:T(8,128)S(1)} %get-tuple-element.237.info_ref, f32[256,256]{1,0:T(8,128)S(1)} %get-tuple-element.238.slots_ref), custom_call_target="tpu_custom_call" | custom-call | tf_op jit(solution)/shard_map/primary_across/relay/pallas_call | solution.py:45
  52.2 1.7 %collective-permute-done.4.rest_0_.rest_4_ = f32[32,1024]{1,0:T(8,128)S(1)} collective-permute-done((f32[32,1024]{1,0:T(8,128)}, f32[32,1024]{1,0:T(8,128)S(1)}, u32[]{:S(2)}, u32[]{:S(2)}) %collective-permute-start.4) | collective-permute-done | bytes 131104 | tf_op jit(solution)/shard_map/column_vectors/ppermute | solution.py:392
  55.8 1.9 %all-to-all-done.3 = f32[16,16,1024]{2,1,0:T(8,128)S(1)} async-done(((f32[16,16,1024]{2,1,0:T(8,128)}), f32[16,16,1024]{2,1,0:T(8,128)S(1)}, u32[]{:S(2)}, u32[]{:S(2)}) %all-to-all-start.3) | async-done | bytes 1048608 | tf_op jit(solution)/shard_map/primary_rows/all_to_all | solution.py:384
  59.2 4.9 %all-to-all-start.4 = ((f32[8,32,1024]{2,1,0:T(8,128)}), f32[8,32,1024]{2,1,0:T(8,128)S(1)}, u32[]{:S(2)}, u32[]{:S(2)}) async-start(f32[8,32,1024]{2,1,0:T(8,128)} %bitcast.48), calls=%async_computation.4 | async-start | bytes 2097152 | tf_op jit(solution)/shard_map/primary_across/all_to_all | solution.py:384
  64.1 2.0 %relay.4 = (bf16[64,256]{1,0:T(8,128)(2,1)S(1)}, bf16[256,64]{1,0:T(8,128)(2,1)S(1)}) custom-call(s32[2]{0:T(128)S(1)} %pad_add_fusion.me_ref, s32[1]{0:T(128)} %constant.29.clone.1.turn_ref, s32[256,128]{1,0:T(8,128)S(1)} %get-tuple-element.237.info_ref, f32[256,256]{1,0:T(8,128)S(1)} %get-tuple-element.238.slots_ref), custom_call_target="tpu_custom_call" | custom-call | tf_op jit(solution)/shard_map/primary_across/relay/pallas_call | solution.py:45
  66.7 3.4 %vectors.1.both_ref = f32[256,2048]{1,0:T(8,128)} custom-call(s32[2]{0:T(128)S(1)} %pad_add_fusion.me_ref, f32[256,256]{1,0:T(8,128)S(1)} %get-tuple-element.238.slots_ref, f32[32,1024]{1,0:T(8,128)} %rest_0_.1, f32[32,1024]{1,0:T(8,128)} %copy-done.5, f32[32,1024]{1,0:T(8,128)} %copy-done.3, f32[32,1024]{1,0:T(8,128)} %copy-done.7, f32[32,1024]{1,0:T(8,128)} %copy-done.6, ...), custom_call_target="tpu_custom_call" | custom-call | tf_op jit(solution)/shard_map/vectors_out/vectors/pallas_call | solution.py:45
  71.3 19.8 %all-to-all-done.4 = f32[8,32,1024]{2,1,0:T(8,128)S(1)} async-done(((f32[8,32,1024]{2,1,0:T(8,128)}), f32[8,32,1024]{2,1,0:T(8,128)S(1)}, u32[]{:S(2)}, u32[]{:S(2)}) %all-to-all-start.4) | async-done | bytes 1048608 | tf_op jit(solution)/shard_map/primary_across/all_to_all | solution.py:384
  91.1 1.6 %put.1 = f32[256,2048]{1,0:T(8,128)} custom-call(bf16[256,256]{1,0:T(8,128)(2,1)S(1)} %get-tuple-element.91.onehot_ref, f32[256,1024]{1,0:T(8,128)S(1)} %bitcast.38, f32[256,2048]{1,0:T(8,128)} %vectors.1.both_ref), custom_call_target="tpu_custom_call", output_to_operand_aliasing={{}: (2, {})} | custom-call | tf_op jit(solution)/shard_map/primary_across/put/pallas_call | solution.py:45
  92.7 34.0 %all_to_all.37 = f32[16,16,2048]{2,1,0:T(8,128)S(1)} all-to-all(f32[16,16,2048]{2,1,0:T(8,128)} %bitcast.43), channel_id=1, replica_groups=mesh['y'=4,'x'=4,'z'=8,'rep'=2] {'y','x'}, dimensions={0} | all-to-all | bytes 4194304 | tf_op jit(solution)/shard_map/out_to_owners/all_to_all | solution.py:384
  126.8 3.6 %loss.1 = f32[128,128]{1,0:T(8,128)} custom-call(f32[256,2048]{1,0:T(8,128)S(1)} %bitcast.37, f32[384,128]{1,0:T(8,128)S(1)} %bitcast.41, bf16[3,512,1024]{2,1,0:T(8,128)(2,1)S(1)} %copy-done.1, f32[8,512]{1,0:T(8,128)S(1)} %get-tuple-element.99.norms_ref), custom_call_target="tpu_custom_call" | custom-call | tf_op jit(solution)/shard_map/loss/pallas_call | solution.py:45
  130.4 6.6 %all-to-all-start.6 = ((f32[128,1,128]{2,1,0:T(1,128)}), f32[128,1,128]{2,1,0:T(1,128)S(1)}, u32[]{:S(2)}, u32[]{:S(2)}) async-start(f32[128,1,128]{2,1,0:T(1,128)} %bitcast.20), calls=%async_computation.6 | async-start | bytes 131072 | tf_op jit(solution)/shard_map/losses_back/all_to_all | solution.py:384
  137.2 11.0 %all-to-all-done.6 = f32[128,1,128]{2,1,0:T(1,128)S(1)} async-done(((f32[128,1,128]{2,1,0:T(1,128)}), f32[128,1,128]{2,1,0:T(1,128)S(1)}, u32[]{:S(2)}, u32[]{:S(2)}) %all-to-all-start.6) | async-done | bytes 65568 | tf_op jit(solution)/shard_map/losses_back/all_to_all | solution.py:384
  (37 shorter events, 8.0 us)
Async XLA Ops:
  2.0 31.4 %all-to-all-start.2 = ((f32[128,1,384]{2,1,0:T(1,128)}), f32[128,1,384]{2,1,0:T(1,128)S(1)}, u32[]{:S(2)}, u32[]{:S(2)}) async-start(f32[128,1,384]{2,1,0:T(1,128)} %bitcast.49), calls=%async_computation.2 | async-start | bytes 393216 | tf_op jit(solution)/shard_map/requests/all_to_all | solution.py:384
  17.5 12.7 %collective-permute-start = (f32[32,1024]{1,0:T(8,128)}, f32[32,1024]{1,0:T(8,128)S(1)}, u32[]{:S(2)}, u32[]{:S(2)}) collective-permute-start(f32[32,1024]{1,0:T(8,128)} %rest_0_.1), channel_id=1, source_target_pairs={{0,12},{2,14},{4,0},{6,2},{8,4},{10,6},{12,8},{14,10},{1,13},{3,15... | collective-permute-start | bytes 393224 | tf_op jit(solution)/shard_map/column_vectors/ppermute | solution.py:392
  21.1 11.0 %collective-permute-start.1 = (f32[32,1024]{1,0:T(8,128)}, f32[32,1024]{1,0:T(8,128)S(1)}, u32[]{:S(2)}, u32[]{:S(2)}) collective-permute-start(f32[32,1024]{1,0:T(8,128)} %rest_0_.1), channel_id=1, source_target_pairs={{0,4},{2,6},{4,8},{6,10},{8,12},{10,14},{12,0},{14,2},{1,5},{3,7},... | collective-permute-start | bytes 393224 | tf_op jit(solution)/shard_map/column_vectors/ppermute | solution.py:392
  21.1 11.0 %collective-permute-start.2 = (f32[32,1024]{1,0:T(8,128)}, f32[32,1024]{1,0:T(8,128)S(1)}, u32[]{:S(2)}, u32[]{:S(2)}) collective-permute-start(f32[32,1024]{1,0:T(8,128)} %rest_0_.1), channel_id=1, source_target_pairs={{0,14},{2,0},{4,2},{6,4},{8,6},{10,8},{12,10},{14,12},{1,15},{3,1}... | collective-permute-start | bytes 393224 | tf_op jit(solution)/shard_map/column_vectors/ppermute | solution.py:392
  24.4 9.0 %collective-permute-start.3 = (f32[32,1024]{1,0:T(8,128)}, f32[32,1024]{1,0:T(8,128)}, u32[]{:S(2)}, u32[]{:S(2)}) collective-permute-start(f32[32,1024]{1,0:T(8,128)} %rest_0_.1), channel_id=1, source_target_pairs={{0,2},{2,4},{4,6},{6,8},{8,10},{10,12},{12,14},{14,0},{1,3},{3,5},... | collective-permute-start | bytes 393224 | tf_op jit(solution)/shard_map/column_vectors/ppermute | solution.py:392
  24.4 1.6 %copy-start.2 = (f32[512,1024]{1,0:T(8,128)S(1)}, f32[512,1024]{1,0:T(8,128)}, u32[]{:S(2)}) copy-start(f32[512,1024]{1,0:T(8,128)} %c_ref.1) | copy-start | bytes 6291460
  27.4 7.9 %copy-start = (bf16[3,512,1024]{2,1,0:T(8,128)(2,1)}, bf16[3,512,1024]{2,1,0:T(8,128)(2,1)S(1)}, u32[]{:S(2)}) copy-start(bf16[3,512,1024]{2,1,0:T(8,128)(2,1)S(1)} %get-tuple-element.88.pieces_ref) | copy-start | bytes 9437188
  30.2 3.2 %copy-start.3 = (f32[32,1024]{1,0:T(8,128)}, f32[32,1024]{1,0:T(8,128)S(1)}, u32[]{:S(2)}) copy-start(f32[32,1024]{1,0:T(8,128)S(1)} %collective-permute-done.rest_0_.rest_2_) | copy-start | bytes 393220
  32.1 0.7 copy-start.4
  32.8 0.7 copy-start.5
  35.4 22.3 %all-to-all-start.3 = ((f32[16,16,1024]{2,1,0:T(8,128)}), f32[16,16,1024]{2,1,0:T(8,128)S(1)}, u32[]{:S(2)}, u32[]{:S(2)}) async-start(f32[16,16,1024]{2,1,0:T(8,128)} %fetch.1.found_ref), calls=%async_computation.3 | async-start | bytes 2097152 | tf_op jit(solution)/shard_map/primary_rows/all_to_all | solution.py:384
  43.0 10.9 %collective-permute-start.4 = (f32[32,1024]{1,0:T(8,128)}, f32[32,1024]{1,0:T(8,128)S(1)}, u32[]{:S(2)}, u32[]{:S(2)}) collective-permute-start(f32[32,1024]{1,0:T(8,128)} %rest_0_.1), channel_id=1, source_target_pairs={{0,8},{2,10},{4,12},{6,14},{8,0},{10,2},{12,4},{14,6},{1,9},{3,11}... | collective-permute-start | bytes 393224 | tf_op jit(solution)/shard_map/column_vectors/ppermute | solution.py:392
  45.8 9.1 %collective-permute-start.5 = (f32[32,1024]{1,0:T(8,128)}, f32[32,1024]{1,0:T(8,128)S(1)}, u32[]{:S(2)}, u32[]{:S(2)}) collective-permute-start(f32[32,1024]{1,0:T(8,128)} %copy-done.3), channel_id=1, source_target_pairs={{0,14},{2,0},{4,2},{6,4},{8,6},{10,8},{12,10},{14,12},{1,15},{3,1}... | collective-permute-start | bytes 393224 | tf_op jit(solution)/shard_map/column_vectors/ppermute | solution.py:392
  48.5 7.3 %collective-permute-start.6 = (f32[32,1024]{1,0:T(8,128)}, f32[32,1024]{1,0:T(8,128)S(1)}, u32[]{:S(2)}, u32[]{:S(2)}) collective-permute-start(f32[32,1024]{1,0:T(8,128)} %copy-done.4), channel_id=1, source_target_pairs={{0,2},{2,4},{4,6},{6,8},{8,10},{10,12},{12,14},{14,0},{1,3},{3,5},... | collective-permute-start | bytes 393224 | tf_op jit(solution)/shard_map/column_vectors/ppermute | solution.py:392
  53.9 3.8 %copy-start.6 = (f32[32,1024]{1,0:T(8,128)}, f32[32,1024]{1,0:T(8,128)S(1)}, u32[]{:S(2)}) copy-start(f32[32,1024]{1,0:T(8,128)S(1)} %collective-permute-done.4.rest_0_.rest_4_) | copy-start | bytes 393220
  54.9 2.8 %copy-start.7 = (f32[32,1024]{1,0:T(8,128)}, f32[32,1024]{1,0:T(8,128)S(1)}, u32[]{:S(2)}) copy-start(f32[32,1024]{1,0:T(8,128)S(1)} %collective-permute-done.5.rest_1_.rest_3_) | copy-start | bytes 393220
  55.8 1.9 %copy-start.8 = (f32[32,1024]{1,0:T(8,128)}, f32[32,1024]{1,0:T(8,128)S(1)}, u32[]{:S(2)}) copy-start(f32[32,1024]{1,0:T(8,128)S(1)} %collective-permute-done.6.rest_2_.rest_5_) | copy-start | bytes 393220
  59.2 31.9 %all-to-all-start.4 = ((f32[8,32,1024]{2,1,0:T(8,128)}), f32[8,32,1024]{2,1,0:T(8,128)S(1)}, u32[]{:S(2)}, u32[]{:S(2)}) async-start(f32[8,32,1024]{2,1,0:T(8,128)} %bitcast.48), calls=%async_computation.4 | async-start | bytes 2097152 | tf_op jit(solution)/shard_map/primary_across/all_to_all | solution.py:384
  66.7 3.4 %collective-permute-start.7 = (s32[1,1]{1,0:T(1,128)}, s32[1,1]{1,0:T(1,128)}, u32[]{:S(2)}, u32[]{:S(2)}) collective-permute-start(s32[1,1]{1,0:T(1,128)} %slice.3), channel_id=1, source_target_pairs={{0,1},{1,0},{2,3},{3,2},{4,5},{5,4},{6,7},{7,6},{8,9},{9,8},{10,11... | collective-permute-start | bytes 20 | tf_op jit(solution)/shard_map/ppermute | solution.py:449
  92.7 34.1 %copy-start.1 = (bf16[3,512,1024]{2,1,0:T(8,128)(2,1)S(1)}, bf16[3,512,1024]{2,1,0:T(8,128)(2,1)}, u32[]{:S(2)}) copy-start(bf16[3,512,1024]{2,1,0:T(8,128)(2,1)} %copy-done) | copy-start | bytes 9437188
  126.8 10.3 %copy-start.9 = (s32[32,4]{0,1:T(4,128)S(1)}, s32[32,4]{0,1:T(4,128)}, u32[]{:S(2)}) copy-start(s32[32,4]{0,1:T(4,128)} %param.14) | copy-start | bytes 1540
  130.4 17.8 %all-to-all-start.6 = ((f32[128,1,128]{2,1,0:T(1,128)}), f32[128,1,128]{2,1,0:T(1,128)S(1)}, u32[]{:S(2)}, u32[]{:S(2)}) async-start(f32[128,1,128]{2,1,0:T(1,128)} %bitcast.20), calls=%async_computation.6 | async-start | bytes 131072 | tf_op jit(solution)/shard_map/losses_back/all_to_all | solution.py:384

commit v7 on v6

--- a/solution.py
+++ b/solution.py
@@ -1,5 +1,3 @@
-import functools
-
 import jax
 import jax.numpy as jnp
 from jax import lax
@@ -17,6 +15,7 @@
 COLV = NZ * V
 SLOTS = COLS * NZ * 2
 SHARDS = COLS * NZ
+QUARTER = SLOTS // 4
 K = 32
 NEXT = 8
 PER = 3
@@ -214,7 +213,8 @@
     most_ref[...] = jnp.full((8, 128), most, F32).astype(I32)
 
 
-def relay_kernel(me_ref, turn_ref, info_ref, slots_ref, send_ref, take_ref):
+def relay_kernel(me_ref, turn_ref, info_ref, slots_ref, *rest):
+    send_ref, take_ref = rest[-2:]
     me = me_ref[0]
     base = turn_ref[0].astype(F32)
     depth_of = send_ref.shape[0] // NZ
@@ -279,32 +279,19 @@
     wait_all(copies)
 
 
-def put_kernel(first, onehot_ref, in_ref, both_ref, out_ref, hold, sems):
-    pieces = split3(in_ref[...])
-    half = SLOTS // 2
-    at = [out_ref.at[pl.ds(c * half, half), pl.ds(first, D)] for c in range(2)]
-    copies = []
-    for c in range(2):
-        hold[c] = pick(onehot_ref[c * half : (c + 1) * half, :], pieces)
-        copies.append(pltpu.make_async_copy(hold.at[c], at[c], sems.at[c]))
-        copies[-1].start()
-    wait_all(copies)
-
-
-def add_kernel(onehot_ref, in_ref, both_ref, out_ref, hold, sems):
-    at = out_ref.at[:, pl.ds(D, D)]
-    copy = pltpu.make_async_copy(at, hold, sems.at[0])
+def add_kernel(onehot_ref, in_ref, total_ref, out_ref, hold, sems):
+    copy = pltpu.make_async_copy(out_ref, hold, sems.at[0])
     copy.start()
     copy.wait()
     hold[...] += pick(onehot_ref[...], split3(in_ref[...]))
-    copy = pltpu.make_async_copy(hold, at, sems.at[1])
+    copy = pltpu.make_async_copy(hold, out_ref, sems.at[1])
     copy.start()
     copy.wait()
 
 
-def vectors_kernel(me_ref, slots_ref, *rest):
-    parts, out_ref, column, hold, sems = rest[:NZ], rest[-4], rest[-3], rest[-2], rest[-1]
-    me = me_ref[0]
+def vectors_kernel(here_ref, slots_ref, *rest):
+    parts, outs, column, hold, sems = rest[:NZ], rest[-NY - 3 : -3], rest[-3], rest[-2], rest[-1]
+    me, y = here_ref[0], here_ref[1]
     copies = []
     for i, part in enumerate(parts):
         at = pl.multiple_of(((me + i) & 7) * V, V)
@@ -312,14 +299,36 @@
     start_all(copies)
     onehot = slots_ref[...].astype(BF16)
     wait_all(copies)
-    pieces = split3(column[...])
-    half = SLOTS // 2
+    hold[...] = pick(onehot, split3(column[...]))
     copies = []
-    for c in range(2):
-        hold[c] = pick(onehot[c * half : (c + 1) * half, :], pieces)
-        target = out_ref.at[pl.ds(c * half, half), pl.ds(0, D)]
-        copies.append(pltpu.make_async_copy(hold.at[c], target, sems.at[NZ + c]))
-        copies[-1].start()
+    for d in range(NY):
+        at = pl.multiple_of(((y + d) & 3) * QUARTER, QUARTER)
+        copies.append(
+            pltpu.make_async_copy(hold.at[pl.ds(at, QUARTER), :], outs[d], sems.at[NZ + d])
+        )
+    start_all(copies)
+    wait_all(copies)
+
+
+def regroup_kernel(here_ref, *rest):
+    parts, outs, hold, sems = rest[:NY], rest[NY : NY + NX], rest[-2], rest[-1]
+    y, x = here_ref[1], here_ref[2]
+    copies = [pltpu.make_async_copy(parts[d], hold.at[d], sems.at[d]) for d in range(NY)]
+    start_all(copies)
+    wait_all(copies)
+    copies = []
+    for e in range(NX):
+        source = pl.multiple_of(((x + e) & 3) * 16, 16)
+        for d in range(NY):
+            target = pl.multiple_of(((y - d) & 3) * 16, 16)
+            copies.append(
+                pltpu.make_async_copy(
+                    hold.at[d, pl.ds(source, 16), :],
+                    outs[e].at[pl.ds(target, 16), :],
+                    sems.at[NY + e * NY + d],
+                )
+            )
+    start_all(copies)
     wait_all(copies)
 
 
@@ -339,23 +348,43 @@
     return dot(hi, chi, NT) + (dot(hi, cmid, NT) + dot(mid, chi, NT) + small)
 
 
-def loss_kernel(both_ref, got_ref, pieces_ref, norms_ref, out_ref):
+def near_kernel(here_ref, got_ref, pieces_ref, norms_ref, *rest):
+    parts, x_ref, rows_ref, out_ref, sems = rest[:NX], rest[-4], rest[-3], rest[-2], rest[-1]
+    x = here_ref[2]
+    copies = []
+    for e in range(NX):
+        for y in range(NY):
+            target = pl.multiple_of(y * QUARTER + ((x - e) & 3) * 16, 16)
+            copies.append(
+                pltpu.make_async_copy(
+                    parts[e].at[pl.ds(y * 16, 16), :],
+                    x_ref.at[pl.ds(target, 16), :],
+                    sems.at[e * NY + y],
+                )
+            )
+    start_all(copies)
     line = got_ref[pl.ds(2, SHARDS, stride=PER), :].astype(I32)
     rows = [line, pltpu.roll(line, GSIZE, 1)]
     rows = jnp.concatenate([a.reshape(COLS, 1, NZ, 128) for a in rows], axis=1).reshape(SLOTS, 128)
     rows = rows & (ROWS - 1)
-    x = both_ref[:, :D]
-    r = x - both_ref[:, D:]
+    rows_ref[...] = rows
+    wait_all(copies)
+    x = x_ref[...]
     square = jnp.sum(x * x, axis=1, keepdims=True)
-    near = square - 2.0 * scores(x, pieces_ref) + norms_ref[0:1, :]
+    out_ref[...] = lookup(square - 2.0 * scores(x, pieces_ref) + norms_ref[0:1, :], rows)
+
+
+def loss_kernel(p_ref, x_ref, rows_ref, near_ref, pieces_ref, out_ref):
+    x = x_ref[...]
+    r = x - p_ref[...]
     hi = r.astype(BF16)
     mid = (r - hi.astype(F32)).astype(BF16)
     chi, cmid = pieces_ref[0], pieces_ref[1]
     table = dot(hi, chi, NT) + (dot(hi, cmid, NT) + dot(mid, chi, NT))
     rx = jnp.sum(r * x, axis=1, keepdims=True)
     rr = jnp.sum(r * r, axis=1, keepdims=True)
-    gap = rx - table
-    loss = lookup((near + amplify * gap * gap / (rr + tiny)) / D, rows)
+    gap = rx - lookup(table, rows_ref[...])
+    loss = (near_ref[...] + amplify * gap * gap / (rr + tiny)) / D
     loss = loss.reshape(COLS, 2, NZ, 128)
     second = pltpu.roll(loss[:, 1].reshape(COLS * NZ, 128), GSIZE, 1)
     first = loss[:, 0].reshape(COLS * NZ, 128)
@@ -388,6 +417,7 @@
     plane = ("y", "x")
     column = lax.axis_index(("y", "x")).astype(I32)
     me = jnp.stack([lax.axis_index("z").astype(I32), column])
+    here = jnp.stack([lax.axis_index(n).astype(I32) for n in ("z", "y", "x")])
     def along_z(block, step):
         return lax.ppermute(block, "z", [(z, (z - step) % NZ) for z in range(NZ)])
 
@@ -448,10 +478,7 @@
     most = most[:1, :1]
     most = jnp.maximum(most, lax.ppermute(most, "rep", [(0, 1), (1, 0)]))[0, 0]
 
-    halves = [pltpu.VMEM((2, SLOTS // 2, D), F32), copies_semaphores(2)]
-    pair = [shape((SLOTS, 2 * D))]
-
-    def relay(base, depth):
+    def relay(base, depth, *after):
         return call(
             relay_kernel,
             [shape((NZ * depth, SLOTS), BF16), shape((SLOTS, NZ * depth), BF16)],
@@ -459,87 +486,115 @@
             base.reshape(1),
             info,
             slots,
+            *after,
             smem=(0, 1),
+            far_in=tuple(range(4, 4 + len(after))),
             name="relay",
         )
 
-    def across(base, send, *after):
-        depth = send.shape[0] // NZ
-        [leaving] = call(
+    def move(base, onehot, source, name, *after):
+        count = onehot.shape[0]
+        [moved] = call(
             send_kernel,
-            [shape((NZ * depth, D))],
+            [shape((count, D))],
             base.reshape(1),
-            send,
-            fetched,
+            onehot,
+            source,
             *after,
             smem=(0,),
             far_in=tuple(range(3, 3 + len(after))),
             far_out=(0,),
-            scratch=[pltpu.VMEM((2, NZ * depth // 2, D), F32), copies_semaphores(2)],
-            name="send",
-        )
-        return swap(leaving.reshape(NZ, depth, D), "z").reshape(NZ * depth, D)
-
-    def add(take, got, both):
-        [both] = call(
+            scratch=[pltpu.VMEM((2, count // 2, D), F32), copies_semaphores(2)],
+            name=name,
+        )
+        return moved
+
+    def across(leaving):
+        return swap(leaving.reshape(NZ, -1, D), "z").reshape(-1, D)
+
+    def add(take, got, total):
+        [total] = call(
             add_kernel,
-            pair,
+            [shape((SLOTS, D))],
             take,
             got,
-            both,
+            total,
             far_in=(2,),
             far_out=(0,),
             alias={2: 0},
             scratch=[pltpu.VMEM((SLOTS, D), F32), copies_semaphores(2)],
             name="add",
         )
-        return both
+        return total
 
     def second(state):
-        base, both = state
-        return base + NEXT, add(next_take, across(base, next_send), both)
+        base, total = state
+        return base + NEXT, add(next_take, across(move(base, next_send, fetched, "send")), total)
 
     def more(state):
-        base, both = state
+        base, total = state
         send, take = relay(base, K)
-        return base + K, add(take, across(base, send), both)
-
+        return base + K, add(take, across(move(base, send, fetched, "send")), total)
+
+    def around(block, axis, step, size):
+        return lax.ppermute(block, axis, [(i, (i + step) % size) for i in range(size)])
+
+    zero = jnp.int32(0)
+    with jax.named_scope("primary_across"):
+        send, take = relay(zero, K)
+        leaving = move(zero, send, fetched, "send", blocks[4], blocks[3], blocks[-3])
+        got = across(leaving)
     with jax.named_scope("vectors_out"):
-        [both] = call(
+        quarters = call(
             vectors_kernel,
-            pair,
-            me,
+            [shape((QUARTER, D))] * NY,
+            here,
             slots,
             *[blocks[o] for o in (0, 1, 2, 3, 4, -3, -2, -1)],
+            leaving,
             smem=(0,),
-            far_in=tuple(range(2, 2 + NZ)),
-            far_out=(0,),
-            scratch=[pltpu.VMEM((COLV, D), F32), halves[0], copies_semaphores(NZ + 2)],
+            far_in=tuple(range(2, 3 + NZ)),
+            far_out=tuple(range(NY)),
+            scratch=[pltpu.VMEM((COLV, D), F32), pltpu.VMEM((SLOTS, D), F32), copies_semaphores(NZ + NY)],
             name="vectors",
         )
+        quarters = [quarters[0]] + [around(quarters[d], "y", d, NY) for d in range(1, NY)]
+        quarters = call(
+            regroup_kernel,
+            [shape((QUARTER, D))] * NX,
+            here,
+            *quarters,
+            smem=(0,),
+            far_in=tuple(range(1, 1 + NY)),
+            far_out=tuple(range(NX)),
+            scratch=[pltpu.VMEM((NY, QUARTER, D), F32), copies_semaphores(NY + NY * NX)],
+            name="regroup",
+        )
+        mine = quarters[0]
+        quarters = [mine] + [around(quarters[e], "x", e, NX) for e in range(1, NX)]
     with jax.named_scope("primary_across"):
-        send, take = relay(jnp.int32(0), K)
-        got = across(jnp.int32(0), send, blocks[4], blocks[3], blocks[-3])
-        next_send, next_take = relay(jnp.int32(K), NEXT)
-        [both] = call(
-            functools.partial(put_kernel, D),
-            pair,
-            take,
-            got,
-            both,
-            far_in=(2,),
-            far_out=(0,),
-            alias={2: 0},
-            scratch=halves,
-            name="put",
-        )
-        state = (jnp.int32(K), both)
+        next_send, next_take = relay(jnp.int32(K), NEXT, mine)
+        total = move(zero, take, got, "take", mine)
+        state = (jnp.int32(K), total)
         state = lax.while_loop(lambda s: (s[0] == K) & (K < most), second, state)
-        _, both = lax.while_loop(lambda s: s[0] < most, more, state)
-    with jax.named_scope("out_to_owners"):
-        both = swap(both.reshape(COLS, 16, 2 * D), plane).reshape(SLOTS, 2 * D)
+        _, total = lax.while_loop(lambda s: s[0] < most, more, state)
+    x, rows, near = call(
+        near_kernel,
+        [shape((SLOTS, D)), shape((SLOTS, 128), I32), shape((SLOTS, 128))],
+        here,
+        arrived,
+        pieces,
+        norms,
+        *quarters,
+        smem=(0,),
+        far_in=tuple(range(4, 4 + NX)),
+        scratch=[copies_semaphores(NX * NY)],
+        name="near",
+    )
+    with jax.named_scope("primaries_out"):
+        primaries = swap(total.reshape(COLS, 16, D), plane).reshape(SLOTS, D)
     [losses] = call(
-        loss_kernel, [shape((SHARDS, 128))], both, arrived, pieces, norms, name="loss"
+        loss_kernel, [shape((SHARDS, 128))], primaries, x, rows, near, pieces, name="loss"
     )
     with jax.named_scope("losses_back"):
         back = swap(losses.reshape(SHARDS, 1, 128), ("y", "x", "z")).reshape(SHARDS, 128)

time: 150 us -> 163 us (1.087)
  blocking collectives: 34 us -> 0 us
  starting transfers between devices: 47 us -> 68.7 us
  waiting for transfers between devices: 41 us -> 50.9 us
  Pallas kernels: 22.3 us -> 30.3 us
  local copies, waits for them, and re-layouts: 3.55 us -> 10 us
    all_to_all x1 -> x0, blocking collectives: 34 us -> none  [swap(): return lax.all_to_all(a, axes, split_axis=0, concat_axis=0, tiled=True)]
    ppermute x0 -> x6, waiting for transfers between devices: none -> 26.4 us  [around(): lax.ppermute(block, axis, [(i, (i + step) % size) for i in range(size)])]
    all_to_all x4 -> x5, waiting for transfers between devices: 32.8 us -> 16.9 us  [swap(): return lax.all_to_all(a, axes, split_axis=0, concat_axis=0, tiled=True)]
    all_to_all x4 -> x5, starting transfers between devices: 34.7 us -> 45.9 us  [swap(): return lax.all_to_all(a, axes, split_axis=0, concat_axis=0, tiled=True)]
    ppermute x0 -> x6, starting transfers between devices: none -> 8.34 us  [around(): lax.ppermute(block, axis, [(i, (i + step) % size) for i in range(size)])]
    pallas_call x11 -> x13, Pallas kernels: 22.3 us -> 30.3 us  [call(): pl.pallas_call(kernel, out_shape=out_shape, in_specs=specs, out_specs=[HB...]
    unnamed x21 -> x49, local copies, waits for them, and re-layouts: 3.01 us -> 9.45 us
    ppermute x7, starting transfers between devices: 12.4 us -> 14.4 us  [along_z(): return lax.ppermute(block, 'z', [(z, (z - step) % NZ) for z in range(NZ)])]
  transfers between devices with their start and end apart: 12 -> 19, of which waited for: 8 -> 11; matrix products, arithmetic and copies ran while one was open for 0% -> 1% of each run, Pallas kernels for 7% -> 11%
where the time goes in v7:
time: 163 us; the launch traced here: 162 us
  starting transfers between devices  68.7 us (42%)
  waiting for transfers between devices  50.9 us (31%)
  Pallas kernels  30.3 us (19%)
  local copies, waits for them, and re-layouts  10 us (6%)
    all_to_all x5, starting transfers between devices, swap(): return lax.all_to_all(a, axes, split_axis=0, concat_axis=0, tiled=True)  45.9 us
    pallas_call x13, Pallas kernels, call(): pl.pallas_call(kernel, out_shape=out_shape, in_specs=specs, out_specs=[HB...  30.3 us
    ppermute x6, waiting for transfers between devices, around(): lax.ppermute(block, axis, [(i, (i + step) % size) for i in range(size)])  26.4 us
    all_to_all x5, waiting for transfers between devices, swap(): return lax.all_to_all(a, axes, split_axis=0, concat_axis=0, tiled=True)  16.9 us
    ppermute x7, starting transfers between devices, along_z(): return lax.ppermute(block, 'z', [(z, (z - step) % NZ) for z in range(NZ)])  14.4 us
    unnamed x49, local copies, waits for them, and re-layouts  9.45 us
    ppermute x6, starting transfers between devices, around(): lax.ppermute(block, axis, [(i, (i + step) % size) for i in range(size)])  8.34 us
    ppermute x7, waiting for transfers between devices, along_z(): return lax.ppermute(block, 'z', [(z, (z - step) % NZ) for z in range(NZ)])  6.35 us
  transfers between devices with their start and end apart: 19, of which 11 were waited for; matrix products, arithmetic and copies ran while one was open for 1% of the time, Pallas kernels for 11%

profile of v7, /device:TPU:2, one launch (start us, length us, event | category | flops | bytes accessed | tf_op | source)
XLA Modules:
  0.0 161.6 jit_solution(8897995489435159518)
XLA Ops:
  0.0 2.0 %request.1 = f32[384,128]{1,0:T(8,128)} custom-call(s32[1,32]{1,0:T(1,128)} %bitcast.50, s32[1,32]{1,0:T(1,128)} %bitcast.51, s32[4,32]{1,0:T(4,128)} %bitcast.49, s32[32,256]{1,0:T(8,128)} %rows_ref.1), custom_call_target="tpu_custom_call" | custom-call | tf_op jit(solution)/shard_map/requests/request/pallas_call | solution.py:44
  2.0 15.4 %all-to-all-start.2 = ((f32[128,1,384]{2,1,0:T(1,128)}), f32[128,1,384]{2,1,0:T(1,128)S(1)}, u32[]{:S(2)}, u32[]{:S(2)}) async-start(f32[128,1,384]{2,1,0:T(1,128)} %bitcast.48), calls=%async_computation.2 | async-start | bytes 393216 | tf_op jit(solution)/shard_map/requests/all_to_all | solution.py:413
  22.0 3.0 %collective-permute-start = (f32[32,1024]{1,0:T(8,128)}, f32[32,1024]{1,0:T(8,128)}, u32[]{:S(2)}, u32[]{:S(2)}) collective-permute-start(f32[32,1024]{1,0:T(8,128)} %rest_0_.1), channel_id=1, source_target_pairs={{0,12},{2,14},{4,0},{6,2},{8,4},{10,6},{12,8},{14,10},{1,13},{3,15... | collective-permute-start | bytes 393224 | tf_op jit(solution)/shard_map/column_vectors/ppermute | solution.py:422
  28.6 3.3 %collective-permute-done.1.rest_1_.rest_6_ = f32[32,1024]{1,0:T(8,128)S(1)} collective-permute-done((f32[32,1024]{1,0:T(8,128)}, f32[32,1024]{1,0:T(8,128)S(1)}, u32[]{:S(2)}, u32[]{:S(2)}) %collective-permute-start.1) | collective-permute-done | bytes 131104 | tf_op jit(solution)/shard_map/column_vectors/ppermute | solution.py:422
  34.4 7.7 %all-to-all-start.3 = ((f32[16,16,1024]{2,1,0:T(8,128)}), f32[16,16,1024]{2,1,0:T(8,128)}, u32[]{:S(2)}, u32[]{:S(2)}) async-start(f32[16,16,1024]{2,1,0:T(8,128)} %fetch.1.found_ref), calls=%async_computation.3 | async-start | bytes 2097152 | tf_op jit(solution)/shard_map/primary_rows/all_to_all | solution.py:413
  42.1 3.7 %collective-permute-start.4 = (f32[32,1024]{1,0:T(8,128)}, f32[32,1024]{1,0:T(8,128)S(1)}, u32[]{:S(2)}, u32[]{:S(2)}) collective-permute-start(f32[32,1024]{1,0:T(8,128)} %rest_0_.1), channel_id=1, source_target_pairs={{0,8},{2,10},{4,12},{6,14},{8,0},{10,2},{12,4},{14,6},{1,9},{3,11}... | collective-permute-start | bytes 393224 | tf_op jit(solution)/shard_map/column_vectors/ppermute | solution.py:422
  47.2 1.9 %collective-permute-start.5 = (f32[32,1024]{1,0:T(8,128)}, f32[32,1024]{1,0:T(8,128)S(1)}, u32[]{:S(2)}, u32[]{:S(2)}) collective-permute-start(f32[32,1024]{1,0:T(8,128)} %collective-permute-done.rest_0_.rest_2_), channel_id=1, source_target_pairs={{0,14},{2,0},{4,2},{6,4},{8,6},{10,8},{12,10},{14,12},{1,15},{3,1}... | collective-permute-start | bytes 393224 | tf_op jit(solution)/shard_map/column_vectors/ppermute | solution.py:422
  49.1 1.9 %slots.1 = (s32[256,128]{1,0:T(8,128)S(1)}, f32[256,256]{1,0:T(8,128)S(1)}, s32[8,128]{1,0:T(8,128)S(1)}) custom-call(s32[2]{0:T(128)S(1)} %pad_add_fusion.me_ref, f32[384,128]{1,0:T(8,128)S(1)} %bitcast.41, f32[16,16,1024]{2,1,0:T(8,128)} %fetch.1.found_ref), custom_call_target="tpu_custom_call" | custom-call | tf_op jit(solution)/shard_map/slots/pallas_call | solution.py:44
  52.8 2.5 %collective-permute-done.6.rest_2_.rest_5_ = f32[32,1024]{1,0:T(8,128)S(1)} collective-permute-done((f32[32,1024]{1,0:T(8,128)}, f32[32,1024]{1,0:T(8,128)S(1)}, u32[]{:S(2)}, u32[]{:S(2)}) %collective-permute-start.6) | collective-permute-done | bytes 131104 | tf_op jit(solution)/shard_map/column_vectors/ppermute | solution.py:422
  57.1 2.7 %send.3.rest_8_ = f32[256,1024]{1,0:T(8,128)} custom-call(s32[1]{0:T(128)} %constant.11.clone.1.turn_ref.base_ref, bf16[256,256]{1,0:T(8,128)(2,1)S(1)} %get-tuple-element.103.onehot_ref, f32[256,1024]{1,0:T(8,128)} %bitcast.13.in_ref, f32[32,1024]{1,0:T(8,128)} %copy-done.11, f32[32,1024]{1,0:T(8,128)} %copy-done.13, f32[32,1024]{1,0:T(8,128)} %copy-done.12), custom_call_target="tpu_custom_call" | custom-call | tf_op jit(solution)/shard_map/primary_across/send/pallas_call | solution.py:44
  59.9 5.2 %all-to-all-start.4 = ((f32[8,32,1024]{2,1,0:T(8,128)}), f32[8,32,1024]{2,1,0:T(8,128)S(1)}, u32[]{:S(2)}, u32[]{:S(2)}) async-start(f32[8,32,1024]{2,1,0:T(8,128)} %bitcast.47), calls=%async_computation.4 | async-start | bytes 2097152 | tf_op jit(solution)/shard_map/primary_across/all_to_all | solution.py:413
  65.2 3.5 %vectors.1 = (f32[64,1024]{1,0:T(8,128)}, f32[64,1024]{1,0:T(8,128)}, f32[64,1024]{1,0:T(8,128)}, f32[64,1024]{1,0:T(8,128)}) custom-call(s32[3]{0:T(128)S(1)} %pad_add_fusion.1.here_ref, f32[256,256]{1,0:T(8,128)S(1)} %get-tuple-element.260.slots_ref, f32[32,1024]{1,0:T(8,128)} %rest_0_.1, f32[32,1024]{1,0:T(8,128)} %copy-done.9, ...), custom_call_target="tpu_custom_call" | custom-call | tf_op jit(solution)/shard_map/vectors_out/vectors/pallas_call | solution.py:44
  68.8 2.3 %collective-permute-start.8 = (f32[64,1024]{1,0:T(8,128)}, f32[64,1024]{1,0:T(8,128)S(1)}, u32[]{:S(2)}, u32[]{:S(2)}) collective-permute-start(f32[64,1024]{1,0:T(8,128)} %get-tuple-element.106), channel_id=1, source_target_pairs={{0,128},{64,192},{128,0},{192,64},{1,129},{65,193},{129,1},{193,65... | collective-permute-start | bytes 786440 | tf_op jit(solution)/shard_map/vectors_out/ppermute | solution.py:540
  75.5 6.4 %collective-permute-done.7.rest_1_ = f32[64,1024]{1,0:T(8,128)S(1)} collective-permute-done((f32[64,1024]{1,0:T(8,128)}, f32[64,1024]{1,0:T(8,128)S(1)}, u32[]{:S(2)}, u32[]{:S(2)}) %collective-permute-start.7) | collective-permute-done | bytes 262176 | tf_op jit(solution)/shard_map/vectors_out/ppermute | solution.py:540
  82.9 2.9 %regroup.1 = (f32[64,1024]{1,0:T(8,128)}, f32[64,1024]{1,0:T(8,128)}, f32[64,1024]{1,0:T(8,128)}, f32[64,1024]{1,0:T(8,128)}) custom-call(s32[3]{0:T(128)S(1)} %pad_add_fusion.1.here_ref, f32[64,1024]{1,0:T(8,128)} %get-tuple-element.104.rest_0_, f32[64,1024]{1,0:T(8,128)} %copy-done.17, f32[64,1024]{1,0:T(8,128)} %copy-done.18, f32[64,1024]{1,0:T(8,128)} %copy-done.19), custom_call_target="tpu_custom_call" | custom-call | tf_op jit(solution)/shard_map/vectors_out/regroup/pallas_call | solution.py:44
  85.8 2.0 %relay.4 = (bf16[64,256]{1,0:T(8,128)(2,1)S(1)}, bf16[256,64]{1,0:T(8,128)(2,1)S(1)}) custom-call(s32[2]{0:T(128)S(1)} %pad_add_fusion.me_ref, s32[1]{0:T(128)} %constant.29.clone.1.turn_ref, s32[256,128]{1,0:T(8,128)S(1)} %get-tuple-element.259.info_ref, f32[256,256]{1,0:T(8,128)S(1)} %get-tuple-element.260.slots_ref, f32[64,1024]{1,0:T(8,128)} %get-tuple-element.108.rest_0_), custom_call_target="tpu_custom_call" | custom-call | tf_op jit(solution)/shard_map/primary_across/relay/pallas_call | solution.py:44
  87.8 4.0 %all-to-all-done.4 = f32[8,32,1024]{2,1,0:T(8,128)S(1)} async-done(((f32[8,32,1024]{2,1,0:T(8,128)}), f32[8,32,1024]{2,1,0:T(8,128)S(1)}, u32[]{:S(2)}, u32[]{:S(2)}) %all-to-all-start.4) | async-done | bytes 1048608 | tf_op jit(solution)/shard_map/primary_across/all_to_all | solution.py:413
  93.4 6.3 %all-to-all-start.5 = ((f32[16,16,1024]{2,1,0:T(8,128)}), f32[16,16,1024]{2,1,0:T(8,128)}, u32[]{:S(2)}, u32[]{:S(2)}) async-start(f32[16,16,1024]{2,1,0:T(8,128)} %bitcast.44), calls=%async_computation.5 | async-start | bytes 2097152 | tf_op jit(solution)/shard_map/primaries_out/all_to_all | solution.py:413
  102.2 2.3 %collective-permute-start.13 = (f32[64,1024]{1,0:T(8,128)S(1)}, f32[64,1024]{1,0:T(8,128)S(1)}, u32[]{:S(2)}, u32[]{:S(2)}) collective-permute-start(f32[64,1024]{1,0:T(8,128)S(1)} %copy-done.21), channel_id=1, source_target_pairs={{0,48},{16,0},{32,16},{48,32},{1,49},{17,1},{33,17},{49,33},{2,50}... | collective-permute-start | bytes 786440 | tf_op jit(solution)/shard_map/vectors_out/ppermute | solution.py:540
  104.5 18.8 %collective-permute-done.11.rest_1_ = f32[64,1024]{1,0:T(8,128)S(1)} collective-permute-done((f32[64,1024]{1,0:T(8,128)S(1)}, f32[64,1024]{1,0:T(8,128)S(1)}, u32[]{:S(2)}, u32[]{:S(2)}) %collective-permute-start.11) | collective-permute-done | bytes 262176 | tf_op jit(solution)/shard_map/vectors_out/ppermute | solution.py:540
  126.8 4.3 %near.1 = (f32[256,1024]{1,0:T(8,128)S(1)}, s32[256,128]{1,0:T(8,128)S(1)}, f32[256,128]{1,0:T(8,128)S(1)}) custom-call(s32[3]{0:T(128)S(1)} %pad_add_fusion.1.here_ref, f32[384,128]{1,0:T(8,128)S(1)} %bitcast.42, bf16[3,512,1024]{2,1,0:T(8,128)(2,1)S(1)} %copy-done.1, f32[8,512]{1,0:T(8,128)S(1)} %get-tuple-element.115.norms_ref, ...), custom_call_target="tpu_custom_call" | custom-call | tf_op jit(solution)/shard_map/near/pallas_call | solution.py:44
  134.9 3.2 %loss.1 = f32[128,128]{1,0:T(8,128)} custom-call(f32[256,1024]{1,0:T(8,128)} %bitcast.20.p_ref, f32[256,1024]{1,0:T(8,128)S(1)} %copy-done.5, s32[256,128]{1,0:T(8,128)S(1)} %get-tuple-element.120.rows_ref, f32[256,128]{1,0:T(8,128)S(1)} %copy-done.7, bf16[3,512,1024]{2,1,0:T(8,128)(2,1)S(1)} %copy-done.2), custom_call_target="tpu_custom_call" | custom-call | tf_op jit(solution)/shard_map/loss/pallas_call | solution.py:44
  138.1 11.2 %all-to-all-start.6 = ((f32[128,1,128]{2,1,0:T(1,128)}), f32[128,1,128]{2,1,0:T(1,128)S(1)}, u32[]{:S(2)}, u32[]{:S(2)}) async-start(f32[128,1,128]{2,1,0:T(1,128)} %bitcast.22), calls=%async_computation.6 | async-start | bytes 131072 | tf_op jit(solution)/shard_map/losses_back/all_to_all | solution.py:413
  149.5 11.0 %all-to-all-done.6 = f32[128,1,128]{2,1,0:T(1,128)S(1)} async-done(((f32[128,1,128]{2,1,0:T(1,128)}), f32[128,1,128]{2,1,0:T(1,128)S(1)}, u32[]{:S(2)}, u32[]{:S(2)}) %all-to-all-start.6) | async-done | bytes 65568 | tf_op jit(solution)/shard_map/losses_back/all_to_all | solution.py:413
  (81 shorter events, 32.4 us)
Async XLA Ops:
  2.0 30.5 %all-to-all-start.2 = ((f32[128,1,384]{2,1,0:T(1,128)}), f32[128,1,384]{2,1,0:T(1,128)S(1)}, u32[]{:S(2)}, u32[]{:S(2)}) async-start(f32[128,1,384]{2,1,0:T(1,128)} %bitcast.48), calls=%async_computation.2 | async-start | bytes 393216 | tf_op jit(solution)/shard_map/requests/all_to_all | solution.py:413
  17.5 11.1 %collective-permute-start.3 = (f32[32,1024]{1,0:T(8,128)}, f32[32,1024]{1,0:T(8,128)S(1)}, u32[]{:S(2)}, u32[]{:S(2)}) collective-permute-start(f32[32,1024]{1,0:T(8,128)} %rest_0_.1), channel_id=1, source_target_pairs={{0,2},{2,4},{4,6},{6,8},{8,10},{10,12},{12,14},{14,0},{1,3},{3,5},... | collective-permute-start | bytes 393224 | tf_op jit(solution)/shard_map/column_vectors/ppermute | solution.py:422
  19.0 9.5 %collective-permute-start.2 = (f32[32,1024]{1,0:T(8,128)}, f32[32,1024]{1,0:T(8,128)S(1)}, u32[]{:S(2)}, u32[]{:S(2)}) collective-permute-start(f32[32,1024]{1,0:T(8,128)} %rest_0_.1), channel_id=1, source_target_pairs={{0,14},{2,0},{4,2},{6,4},{8,6},{10,8},{12,10},{14,12},{1,15},{3,1}... | collective-permute-start | bytes 393224 | tf_op jit(solution)/shard_map/column_vectors/ppermute | solution.py:422
  20.8 11.1 %collective-permute-start.1 = (f32[32,1024]{1,0:T(8,128)}, f32[32,1024]{1,0:T(8,128)S(1)}, u32[]{:S(2)}, u32[]{:S(2)}) collective-permute-start(f32[32,1024]{1,0:T(8,128)} %rest_0_.1), channel_id=1, source_target_pairs={{0,4},{2,6},{4,8},{6,10},{8,12},{10,14},{12,0},{14,2},{1,5},{3,7},... | collective-permute-start | bytes 393224 | tf_op jit(solution)/shard_map/column_vectors/ppermute | solution.py:422
  22.0 10.6 %collective-permute-start = (f32[32,1024]{1,0:T(8,128)}, f32[32,1024]{1,0:T(8,128)}, u32[]{:S(2)}, u32[]{:S(2)}) collective-permute-start(f32[32,1024]{1,0:T(8,128)} %rest_0_.1), channel_id=1, source_target_pairs={{0,12},{2,14},{4,0},{6,2},{8,4},{10,6},{12,8},{14,10},{1,13},{3,15... | collective-permute-start | bytes 393224 | tf_op jit(solution)/shard_map/column_vectors/ppermute | solution.py:422
  28.0 6.4 %copy-start = (bf16[3,512,1024]{2,1,0:T(8,128)(2,1)}, bf16[3,512,1024]{2,1,0:T(8,128)(2,1)S(1)}, u32[]{:S(2)}) copy-start(bf16[3,512,1024]{2,1,0:T(8,128)(2,1)S(1)} %get-tuple-element.99.pieces_ref) | copy-start | bytes 9437188
  34.4 22.7 %all-to-all-start.3 = ((f32[16,16,1024]{2,1,0:T(8,128)}), f32[16,16,1024]{2,1,0:T(8,128)}, u32[]{:S(2)}, u32[]{:S(2)}) async-start(f32[16,16,1024]{2,1,0:T(8,128)} %fetch.1.found_ref), calls=%async_computation.3 | async-start | bytes 2097152 | tf_op jit(solution)/shard_map/primary_rows/all_to_all | solution.py:413
  42.1 10.6 %collective-permute-start.4 = (f32[32,1024]{1,0:T(8,128)}, f32[32,1024]{1,0:T(8,128)S(1)}, u32[]{:S(2)}, u32[]{:S(2)}) collective-permute-start(f32[32,1024]{1,0:T(8,128)} %rest_0_.1), channel_id=1, source_target_pairs={{0,8},{2,10},{4,12},{6,14},{8,0},{10,2},{12,4},{14,6},{1,9},{3,11}... | collective-permute-start | bytes 393224 | tf_op jit(solution)/shard_map/column_vectors/ppermute | solution.py:422
  45.8 9.4 %collective-permute-start.6 = (f32[32,1024]{1,0:T(8,128)}, f32[32,1024]{1,0:T(8,128)S(1)}, u32[]{:S(2)}, u32[]{:S(2)}) collective-permute-start(f32[32,1024]{1,0:T(8,128)} %copy-done.10), channel_id=1, source_target_pairs={{0,2},{2,4},{4,6},{6,8},{8,10},{10,12},{12,14},{14,0},{1,3},{3,5},... | collective-permute-start | bytes 393224 | tf_op jit(solution)/shard_map/column_vectors/ppermute | solution.py:422
  47.2 8.1 %collective-permute-start.5 = (f32[32,1024]{1,0:T(8,128)}, f32[32,1024]{1,0:T(8,128)S(1)}, u32[]{:S(2)}, u32[]{:S(2)}) collective-permute-start(f32[32,1024]{1,0:T(8,128)} %collective-permute-done.rest_0_.rest_2_), channel_id=1, source_target_pairs={{0,14},{2,0},{4,2},{6,4},{8,6},{10,8},{12,10},{14,12},{1,15},{3,1}... | collective-permute-start | bytes 393224 | tf_op jit(solution)/shard_map/column_vectors/ppermute | solution.py:422
  59.9 32.0 %all-to-all-start.4 = ((f32[8,32,1024]{2,1,0:T(8,128)}), f32[8,32,1024]{2,1,0:T(8,128)S(1)}, u32[]{:S(2)}, u32[]{:S(2)}) async-start(f32[8,32,1024]{2,1,0:T(8,128)} %bitcast.47), calls=%async_computation.4 | async-start | bytes 2097152 | tf_op jit(solution)/shard_map/primary_across/all_to_all | solution.py:413
  68.7 13.2 %collective-permute-start.7 = (f32[64,1024]{1,0:T(8,128)}, f32[64,1024]{1,0:T(8,128)S(1)}, u32[]{:S(2)}, u32[]{:S(2)}) collective-permute-start(f32[64,1024]{1,0:T(8,128)} %get-tuple-element.105), channel_id=1, source_target_pairs={{0,64},{64,128},{128,192},{192,0},{1,65},{65,129},{129,193},{193,1... | collective-permute-start | bytes 786440 | tf_op jit(solution)/shard_map/vectors_out/ppermute | solution.py:540
  68.8 13.1 %collective-permute-start.8 = (f32[64,1024]{1,0:T(8,128)}, f32[64,1024]{1,0:T(8,128)S(1)}, u32[]{:S(2)}, u32[]{:S(2)}) collective-permute-start(f32[64,1024]{1,0:T(8,128)} %get-tuple-element.106), channel_id=1, source_target_pairs={{0,128},{64,192},{128,0},{192,64},{1,129},{65,193},{129,1},{193,65... | collective-permute-start | bytes 786440 | tf_op jit(solution)/shard_map/vectors_out/ppermute | solution.py:540
  71.1 11.1 %collective-permute-start.9 = (f32[64,1024]{1,0:T(8,128)}, f32[64,1024]{1,0:T(8,128)S(1)}, u32[]{:S(2)}, u32[]{:S(2)}) collective-permute-start(f32[64,1024]{1,0:T(8,128)} %get-tuple-element.107), channel_id=1, source_target_pairs={{0,192},{64,0},{128,64},{192,128},{1,193},{65,1},{129,65},{193,129... | collective-permute-start | bytes 786440 | tf_op jit(solution)/shard_map/vectors_out/ppermute | solution.py:540
  72.9 1.3 collective-permute-start.10
  93.4 6.4 %copy-start.23 = (f32[64,1024]{1,0:T(8,128)S(1)}, f32[64,1024]{1,0:T(8,128)}, u32[]{:S(2)}) copy-start(f32[64,1024]{1,0:T(8,128)} %get-tuple-element.116) | copy-start | bytes 786436
  93.4 7.9 %copy-start.22 = (f32[64,1024]{1,0:T(8,128)S(1)}, f32[64,1024]{1,0:T(8,128)}, u32[]{:S(2)}) copy-start(f32[64,1024]{1,0:T(8,128)} %get-tuple-element.117) | copy-start | bytes 786436
  93.4 8.8 %copy-start.21 = (f32[64,1024]{1,0:T(8,128)S(1)}, f32[64,1024]{1,0:T(8,128)}, u32[]{:S(2)}) copy-start(f32[64,1024]{1,0:T(8,128)} %get-tuple-element.118) | copy-start | bytes 786436
  93.4 39.3 %all-to-all-start.5 = ((f32[16,16,1024]{2,1,0:T(8,128)}), f32[16,16,1024]{2,1,0:T(8,128)}, u32[]{:S(2)}, u32[]{:S(2)}) async-start(f32[16,16,1024]{2,1,0:T(8,128)} %bitcast.44), calls=%async_computation.5 | async-start | bytes 2097152 | tf_op jit(solution)/shard_map/primaries_out/all_to_all | solution.py:413
  99.8 23.5 %collective-permute-start.11 = (f32[64,1024]{1,0:T(8,128)S(1)}, f32[64,1024]{1,0:T(8,128)S(1)}, u32[]{:S(2)}, u32[]{:S(2)}) collective-permute-start(f32[64,1024]{1,0:T(8,128)S(1)} %copy-done.23), channel_id=1, source_target_pairs={{0,16},{16,32},{32,48},{48,0},{1,17},{17,33},{33,49},{49,1},{2,18}... | collective-permute-start | bytes 786440 | tf_op jit(solution)/shard_map/vectors_out/ppermute | solution.py:540
  101.3 22.0 %collective-permute-start.12 = (f32[64,1024]{1,0:T(8,128)S(1)}, f32[64,1024]{1,0:T(8,128)S(1)}, u32[]{:S(2)}, u32[]{:S(2)}) collective-permute-start(f32[64,1024]{1,0:T(8,128)S(1)} %copy-done.22), channel_id=1, source_target_pairs={{0,32},{16,48},{32,0},{48,16},{1,33},{17,49},{33,1},{49,17},{2,34}... | collective-permute-start | bytes 786440 | tf_op jit(solution)/shard_map/vectors_out/ppermute | solution.py:540
  102.2 22.0 %collective-permute-start.13 = (f32[64,1024]{1,0:T(8,128)S(1)}, f32[64,1024]{1,0:T(8,128)S(1)}, u32[]{:S(2)}, u32[]{:S(2)}) collective-permute-start(f32[64,1024]{1,0:T(8,128)S(1)} %copy-done.21), channel_id=1, source_target_pairs={{0,48},{16,0},{32,16},{48,32},{1,49},{17,1},{33,17},{49,33},{2,50}... | collective-permute-start | bytes 786440 | tf_op jit(solution)/shard_map/vectors_out/ppermute | solution.py:540
  132.8 16.6 %copy-start.20 = (s32[32,4]{0,1:T(4,128)S(1)}, s32[32,4]{0,1:T(4,128)}, u32[]{:S(2)}) copy-start(s32[32,4]{0,1:T(4,128)} %param.14) | copy-start | bytes 1540
  138.1 22.3 %all-to-all-start.6 = ((f32[128,1,128]{2,1,0:T(1,128)}), f32[128,1,128]{2,1,0:T(1,128)S(1)}, u32[]{:S(2)}, u32[]{:S(2)}) async-start(f32[128,1,128]{2,1,0:T(1,128)} %bitcast.22), calls=%async_computation.6 | async-start | bytes 131072 | tf_op jit(solution)/shard_map/losses_back/all_to_all | solution.py:413
  (19 other events, 34.0 us)

commit v8 on v7

--- a/solution.py
+++ b/solution.py
@@ -27,13 +27,17 @@
 VMEM = pl.BlockSpec(memory_space=pltpu.VMEM)
 SMEM = pl.BlockSpec(memory_space=pltpu.SMEM)
 HBM = pl.BlockSpec(memory_space=pltpu.HBM)
+ANY = pl.BlockSpec(memory_space=pl.ANY)
 NN = (((1,), (0,)), ((), ()))
 NT = (((1,), (1,)), ((), ()))
 TN = (((0,), (0,)), ((), ()))
 
 
-def call(kernel, out_shape, *operands, smem=(), far_in=(), far_out=(), scratch=(), alias=None, name=None):
-    specs = [SMEM if i in smem else HBM if i in far_in else VMEM for i in range(len(operands))]
+def call(kernel, out_shape, *operands, smem=(), any_in=(), far_in=(), far_out=(), scratch=(), alias=None, name=None):
+    specs = [
+        SMEM if i in smem else ANY if i in any_in else HBM if i in far_in else VMEM
+        for i in range(len(operands))
+    ]
     operands = [
         pltpu.with_memory_space_constraint(a, pltpu.HBM) if i in far_in else a
         for i, a in enumerate(operands)
@@ -349,7 +353,7 @@
 
 
 def near_kernel(here_ref, got_ref, pieces_ref, norms_ref, *rest):
-    parts, x_ref, rows_ref, out_ref, sems = rest[:NX], rest[-4], rest[-3], rest[-2], rest[-1]
+    parts, out_ref, near_ref, x_all, near, sems = rest[:NX], *rest[-5:]
     x = here_ref[2]
     copies = []
     for e in range(NX):
@@ -358,7 +362,7 @@
             copies.append(
                 pltpu.make_async_copy(
                     parts[e].at[pl.ds(y * 16, 16), :],
-                    x_ref.at[pl.ds(target, 16), :],
+                    x_all.at[pl.ds(target, 16), :],
                     sems.at[e * NY + y],
                 )
             )
@@ -367,24 +371,41 @@
     rows = [line, pltpu.roll(line, GSIZE, 1)]
     rows = jnp.concatenate([a.reshape(COLS, 1, NZ, 128) for a in rows], axis=1).reshape(SLOTS, 128)
     rows = rows & (ROWS - 1)
-    rows_ref[...] = rows
-    wait_all(copies)
-    x = x_ref[...]
+    near[:, 128:] = rows.astype(F32)
+    wait_all(copies)
+    ends = [pltpu.make_async_copy(x_all, out_ref, sems.at[NX * NY])]
+    ends[0].start()
+    x = x_all[...]
     square = jnp.sum(x * x, axis=1, keepdims=True)
-    out_ref[...] = lookup(square - 2.0 * scores(x, pieces_ref) + norms_ref[0:1, :], rows)
-
-
-def loss_kernel(p_ref, x_ref, rows_ref, near_ref, pieces_ref, out_ref):
-    x = x_ref[...]
-    r = x - p_ref[...]
-    hi = r.astype(BF16)
-    mid = (r - hi.astype(F32)).astype(BF16)
-    chi, cmid = pieces_ref[0], pieces_ref[1]
-    table = dot(hi, chi, NT) + (dot(hi, cmid, NT) + dot(mid, chi, NT))
-    rx = jnp.sum(r * x, axis=1, keepdims=True)
-    rr = jnp.sum(r * r, axis=1, keepdims=True)
-    gap = rx - lookup(table, rows_ref[...])
-    loss = (near_ref[...] + amplify * gap * gap / (rr + tiny)) / D
+    near[:, :128] = lookup(square - 2.0 * scores(x, pieces_ref) + norms_ref[0:1, :], rows)
+    ends.append(pltpu.make_async_copy(near, near_ref, sems.at[NX * NY + 1]))
+    ends[1].start()
+    wait_all(ends)
+
+
+def loss_kernel(p_ref, x_ref, near_ref, pieces_ref, out_ref, p_half, x_half, near, sems):
+    copies = []
+    for c in range(2):
+        cut = pl.ds(c * D // 2, D // 2)
+        copies.append(pltpu.make_async_copy(p_ref.at[:, cut], p_half.at[c], sems.at[2 * c]))
+        copies.append(pltpu.make_async_copy(x_ref.at[:, cut], x_half.at[c], sems.at[2 * c + 1]))
+    copies.append(pltpu.make_async_copy(near_ref, near, sems.at[4]))
+    start_all(copies)
+    table, rx, rr = 0.0, 0.0, 0.0
+    for c in range(2):
+        wait_all(copies[2 * c : 2 * c + 2])
+        x = x_half[c]
+        r = x - p_half[c]
+        hi = r.astype(BF16)
+        mid = (r - hi.astype(F32)).astype(BF16)
+        cut = slice(c * D // 2, (c + 1) * D // 2)
+        chi, cmid = pieces_ref[0, :, cut], pieces_ref[1, :, cut]
+        table = table + (dot(hi, chi, NT) + (dot(hi, cmid, NT) + dot(mid, chi, NT)))
+        rx = rx + jnp.sum(r * x, axis=1, keepdims=True)
+        rr = rr + jnp.sum(r * r, axis=1, keepdims=True)
+    copies[4].wait()
+    gap = rx - lookup(table, near[:, 128:].astype(I32))
+    loss = (near[:, :128] + amplify * gap * gap / (rr + tiny)) / D
     loss = loss.reshape(COLS, 2, NZ, 128)
     second = pltpu.roll(loss[:, 1].reshape(COLS * NZ, 128), GSIZE, 1)
     first = loss[:, 0].reshape(COLS * NZ, 128)
@@ -458,7 +479,7 @@
             arrived,
             pieces,
             *[blocks[o] for o in FIRST],
-            far_in=tuple(range(2, 2 + len(FIRST))),
+            any_in=tuple(range(2, 2 + len(FIRST))),
             far_out=(0,),
             scratch=[pltpu.VMEM((2, COLS, 8, D), F32), copies_semaphores(2)],
             name="fetch",
@@ -488,7 +509,7 @@
             slots,
             *after,
             smem=(0, 1),
-            far_in=tuple(range(4, 4 + len(after))),
+            any_in=tuple(range(4, 4 + len(after))),
             name="relay",
         )
 
@@ -502,7 +523,7 @@
             source,
             *after,
             smem=(0,),
-            far_in=tuple(range(3, 3 + len(after))),
+            any_in=tuple(range(3, 3 + len(after))),
             far_out=(0,),
             scratch=[pltpu.VMEM((2, count // 2, D), F32), copies_semaphores(2)],
             name=name,
@@ -529,7 +550,8 @@
 
     def second(state):
         base, total = state
-        return base + NEXT, add(next_take, across(move(base, next_send, fetched, "send")), total)
+        send, take = relay(base, NEXT)
+        return base + NEXT, add(take, across(move(base, send, fetched, "send")), total)
 
     def more(state):
         base, total = state
@@ -553,7 +575,7 @@
             *[blocks[o] for o in (0, 1, 2, 3, 4, -3, -2, -1)],
             leaving,
             smem=(0,),
-            far_in=tuple(range(2, 3 + NZ)),
+            any_in=tuple(range(2, 3 + NZ)),
             far_out=tuple(range(NY)),
             scratch=[pltpu.VMEM((COLV, D), F32), pltpu.VMEM((SLOTS, D), F32), copies_semaphores(NZ + NY)],
             name="vectors",
@@ -565,36 +587,53 @@
             here,
             *quarters,
             smem=(0,),
-            far_in=tuple(range(1, 1 + NY)),
+            any_in=tuple(range(1, 1 + NY)),
             far_out=tuple(range(NX)),
             scratch=[pltpu.VMEM((NY, QUARTER, D), F32), copies_semaphores(NY + NY * NX)],
             name="regroup",
         )
-        mine = quarters[0]
-        quarters = [mine] + [around(quarters[e], "x", e, NX) for e in range(1, NX)]
+        quarters = [quarters[0]] + [around(quarters[e], "x", e, NX) for e in range(1, NX)]
     with jax.named_scope("primary_across"):
-        next_send, next_take = relay(jnp.int32(K), NEXT, mine)
-        total = move(zero, take, got, "take", mine)
+        total = move(zero, take, got, "take", *quarters)
         state = (jnp.int32(K), total)
         state = lax.while_loop(lambda s: (s[0] == K) & (K < most), second, state)
         _, total = lax.while_loop(lambda s: s[0] < most, more, state)
-    x, rows, near = call(
+    x, near = call(
         near_kernel,
-        [shape((SLOTS, D)), shape((SLOTS, 128), I32), shape((SLOTS, 128))],
+        [shape((SLOTS, D)), shape((SLOTS, 256))],
         here,
         arrived,
         pieces,
         norms,
         *quarters,
         smem=(0,),
-        far_in=tuple(range(4, 4 + NX)),
-        scratch=[copies_semaphores(NX * NY)],
+        any_in=tuple(range(4, 4 + NX)),
+        far_out=(0, 1),
+        scratch=[
+            pltpu.VMEM((SLOTS, D), F32),
+            pltpu.VMEM((SLOTS, 256), F32),
+            copies_semaphores(NX * NY + 2),
+        ],
         name="near",
     )
     with jax.named_scope("primaries_out"):
         primaries = swap(total.reshape(COLS, 16, D), plane).reshape(SLOTS, D)
     [losses] = call(
-        loss_kernel, [shape((SHARDS, 128))], primaries, x, rows, near, pieces, name="loss"
+        loss_kernel,
+        [shape((SHARDS, 128))],
+        primaries,
+        x,
+        near,
+        pieces,
+        any_in=(0,),
+        far_in=(1, 2),
+        scratch=[
+            pltpu.VMEM((2, SLOTS, D // 2), F32),
+            pltpu.VMEM((2, SLOTS, D // 2), F32),
+            pltpu.VMEM((SLOTS, 256), F32),
+            copies_semaphores(5),
+        ],
+        name="loss",
     )
     with jax.named_scope("losses_back"):
         back = swap(losses.reshape(SHARDS, 1, 128), ("y", "x", "z")).reshape(SHARDS, 128)

time: 163 us -> 158 us (0.969)
  waiting for transfers between devices: 50.9 us -> 40.6 us
  local copies, waits for them, and re-layouts: 10 us -> 16.2 us
  Pallas kernels: 30.3 us -> 28.5 us
    ppermute x6, waiting for transfers between devices: 26.4 us -> 17.1 us  [around(): lax.ppermute(block, axis, [(i, (i + step) % size) for i in range(size)])]
    unnamed x49 -> x51, local copies, waits for them, and re-layouts: 9.45 us -> 15.7 us
    pallas_call x13 -> x12, Pallas kernels: 30.3 us -> 28.5 us  [call(): pl.pallas_call(kernel, out_shape=out_shape, in_specs=specs, out_specs=[HB...]
  transfers between devices with their start and end apart: 19 -> 19, of which waited for: 11 -> 12; matrix products, arithmetic and copies ran while one was open for 1% -> 1% of each run, Pallas kernels for 11% -> 10%
where the time goes in v8:
time: 158 us; the launch traced here: 157 us
  starting transfers between devices  70.2 us (44%)
  waiting for transfers between devices  40.6 us (26%)
  Pallas kernels  28.5 us (18%)
  local copies, waits for them, and re-layouts  16.2 us (10%)
    all_to_all x5, starting transfers between devices, swap(): return lax.all_to_all(a, axes, split_axis=0, concat_axis=0, tiled=True)  47.5 us
    pallas_call x12, Pallas kernels, call(): pl.pallas_call(kernel, out_shape=out_shape, in_specs=specs, out_specs=[HB...  28.5 us
    ppermute x6, waiting for transfers between devices, around(): lax.ppermute(block, axis, [(i, (i + step) % size) for i in range(size)])  17.1 us
    all_to_all x5, waiting for transfers between devices, swap(): return lax.all_to_all(a, axes, split_axis=0, concat_axis=0, tiled=True)  17 us
    unnamed x51, local copies, waits for them, and re-layouts  15.7 us
    ppermute x7, starting transfers between devices, along_z(): return lax.ppermute(block, 'z', [(z, (z - step) % NZ) for z in range(NZ)])  14.4 us
    ppermute x6, starting transfers between devices, around(): lax.ppermute(block, axis, [(i, (i + step) % size) for i in range(size)])  8.27 us
    ppermute x7, waiting for transfers between devices, along_z(): return lax.ppermute(block, 'z', [(z, (z - step) % NZ) for z in range(NZ)])  5.3 us
  transfers between devices with their start and end apart: 19, of which 12 were waited for; matrix products, arithmetic and copies ran while one was open for 1% of the time, Pallas kernels for 10%

profile of v8, /device:TPU:2, one launch (start us, length us, event | category | flops | bytes accessed | tf_op | source)
XLA Modules:
  0.0 157.5 jit_solution(15665242292923111512)
XLA Ops:
  0.0 2.0 %request.1 = f32[384,128]{1,0:T(8,128)} custom-call(s32[1,32]{1,0:T(1,128)} %bitcast.50, s32[1,32]{1,0:T(1,128)} %bitcast.51, s32[4,32]{1,0:T(4,128)} %bitcast.49, s32[32,256]{1,0:T(8,128)} %rows_ref.1), custom_call_target="tpu_custom_call" | custom-call | tf_op jit(solution)/shard_map/requests/request/pallas_call | solution.py:48
  2.0 15.4 %all-to-all-start.2 = ((f32[128,1,384]{2,1,0:T(1,128)}), f32[128,1,384]{2,1,0:T(1,128)S(1)}, u32[]{:S(2)}, u32[]{:S(2)}) async-start(f32[128,1,384]{2,1,0:T(1,128)} %bitcast.48), calls=%async_computation.2 | async-start | bytes 393216 | tf_op jit(solution)/shard_map/requests/all_to_all | solution.py:434
  22.0 3.0 %collective-permute-start = (f32[32,1024]{1,0:T(8,128)}, f32[32,1024]{1,0:T(8,128)S(1)}, u32[]{:S(2)}, u32[]{:S(2)}) collective-permute-start(f32[32,1024]{1,0:T(8,128)} %rest_0_.1), channel_id=1, source_target_pairs={{0,12},{2,14},{4,0},{6,2},{8,4},{10,6},{12,8},{14,10},{1,13},{3,15... | collective-permute-start | bytes 393224 | tf_op jit(solution)/shard_map/column_vectors/ppermute | solution.py:443
  29.6 2.3 %collective-permute-done.1.rest_1_.rest_6_ = f32[32,1024]{1,0:T(8,128)S(1)} collective-permute-done((f32[32,1024]{1,0:T(8,128)}, f32[32,1024]{1,0:T(8,128)S(1)}, u32[]{:S(2)}, u32[]{:S(2)}) %collective-permute-start.1) | collective-permute-done | bytes 131104 | tf_op jit(solution)/shard_map/column_vectors/ppermute | solution.py:443
  35.9 1.9 %fetch.1.found_ref = f32[16,16,1024]{2,1,0:T(8,128)} custom-call(f32[384,128]{1,0:T(8,128)S(1)} %bitcast.41, bf16[3,512,1024]{2,1,0:T(8,128)(2,1)S(1)} %get-tuple-element.103.pieces_ref, f32[32,1024]{1,0:T(8,128)S(1)} %copy-done.20, f32[32,1024]{1,0:T(8,128)S(1)} %copy-done.17, f32[32,1024]{1,0:T(8,128)S(1)} %copy-done.14, ...), custom_call_target="tpu_custom_call" | custom-call | tf_op jit(solution)/shard_map/primary_rows/fetch/pallas_call | solution.py:48
  37.8 7.7 %all-to-all-start.3 = ((f32[16,16,1024]{2,1,0:T(8,128)}), f32[16,16,1024]{2,1,0:T(8,128)}, u32[]{:S(2)}, u32[]{:S(2)}) async-start(f32[16,16,1024]{2,1,0:T(8,128)} %fetch.1.found_ref), calls=%async_computation.3 | async-start | bytes 2097152 | tf_op jit(solution)/shard_map/primary_rows/all_to_all | solution.py:434
  45.5 3.7 %collective-permute-start.4 = (f32[32,1024]{1,0:T(8,128)}, f32[32,1024]{1,0:T(8,128)S(1)}, u32[]{:S(2)}, u32[]{:S(2)}) collective-permute-start(f32[32,1024]{1,0:T(8,128)} %rest_0_.1), channel_id=1, source_target_pairs={{0,8},{2,10},{4,12},{6,14},{8,0},{10,2},{12,4},{14,6},{1,9},{3,11}... | collective-permute-start | bytes 393224 | tf_op jit(solution)/shard_map/column_vectors/ppermute | solution.py:443
  50.6 1.9 %collective-permute-start.5 = (f32[32,1024]{1,0:T(8,128)}, f32[32,1024]{1,0:T(8,128)S(1)}, u32[]{:S(2)}, u32[]{:S(2)}) collective-permute-start(f32[32,1024]{1,0:T(8,128)} %copy-done.19), channel_id=1, source_target_pairs={{0,14},{2,0},{4,2},{6,4},{8,6},{10,8},{12,10},{14,12},{1,15},{3,1}... | collective-permute-start | bytes 393224 | tf_op jit(solution)/shard_map/column_vectors/ppermute | solution.py:443
  52.6 1.9 %slots.1 = (s32[256,128]{1,0:T(8,128)S(1)}, f32[256,256]{1,0:T(8,128)S(1)}, s32[8,128]{1,0:T(8,128)S(1)}) custom-call(s32[2]{0:T(128)S(1)} %pad_add_fusion.me_ref, f32[384,128]{1,0:T(8,128)S(1)} %bitcast.42, f32[16,16,1024]{2,1,0:T(8,128)} %fetch.1.found_ref), custom_call_target="tpu_custom_call" | custom-call | tf_op jit(solution)/shard_map/slots/pallas_call | solution.py:48
  56.2 2.5 %collective-permute-done.6.rest_2_.rest_5_ = f32[32,1024]{1,0:T(8,128)S(1)} collective-permute-done((f32[32,1024]{1,0:T(8,128)}, f32[32,1024]{1,0:T(8,128)S(1)}, u32[]{:S(2)}, u32[]{:S(2)}) %collective-permute-start.6) | collective-permute-done | bytes 131104 | tf_op jit(solution)/shard_map/column_vectors/ppermute | solution.py:443
  60.5 2.7 %send.3.rest_8_ = f32[256,1024]{1,0:T(8,128)} custom-call(s32[1]{0:T(128)} %constant.12.clone.1.turn_ref.base_ref, bf16[256,256]{1,0:T(8,128)(2,1)S(1)} %get-tuple-element.107.onehot_ref, f32[256,1024]{1,0:T(8,128)} %bitcast.13.in_ref, f32[32,1024]{1,0:T(8,128)S(1)} %collective-permute-done.4.rest_0_.rest_4_, ...), custom_call_target="tpu_custom_call" | custom-call | tf_op jit(solution)/shard_map/primary_across/send/pallas_call | solution.py:48
  63.2 5.2 %all-to-all-start.4 = ((f32[8,32,1024]{2,1,0:T(8,128)}), f32[8,32,1024]{2,1,0:T(8,128)S(1)}, u32[]{:S(2)}, u32[]{:S(2)}) async-start(f32[8,32,1024]{2,1,0:T(8,128)} %bitcast.39), calls=%async_computation.4 | async-start | bytes 2097152 | tf_op jit(solution)/shard_map/primary_across/all_to_all | solution.py:434
  69.8 3.7 %vectors.1 = (f32[64,1024]{1,0:T(8,128)}, f32[64,1024]{1,0:T(8,128)}, f32[64,1024]{1,0:T(8,128)}, f32[64,1024]{1,0:T(8,128)}) custom-call(s32[3]{0:T(128)S(1)} %pad_add_fusion.1.here_ref, f32[256,256]{1,0:T(8,128)S(1)} %get-tuple-element.276.slots_ref, f32[32,1024]{1,0:T(8,128)S(1)} %copy-done.23, f32[32,1024]{1,0:T(8,128)S(1)} %copy-done.15, ...), custom_call_target="tpu_custom_call" | custom-call | tf_op jit(solution)/shard_map/vectors_out/vectors/pallas_call | solution.py:48
  73.5 2.3 %collective-permute-start.8 = (f32[64,1024]{1,0:T(8,128)}, f32[64,1024]{1,0:T(8,128)S(1)}, u32[]{:S(2)}, u32[]{:S(2)}) collective-permute-start(f32[64,1024]{1,0:T(8,128)} %get-tuple-element.110), channel_id=1, source_target_pairs={{0,128},{64,192},{128,0},{192,64},{1,129},{65,193},{129,1},{193,65... | collective-permute-start | bytes 786440 | tf_op jit(solution)/shard_map/vectors_out/ppermute | solution.py:562
  77.0 9.3 %collective-permute-done.7.rest_1_ = f32[64,1024]{1,0:T(8,128)S(1)} collective-permute-done((f32[64,1024]{1,0:T(8,128)}, f32[64,1024]{1,0:T(8,128)S(1)}, u32[]{:S(2)}, u32[]{:S(2)}) %collective-permute-start.7) | collective-permute-done | bytes 262176 | tf_op jit(solution)/shard_map/vectors_out/ppermute | solution.py:562
  97.4 4.8 %collective-permute-done.10.rest_1_ = f32[64,1024]{1,0:T(8,128)S(1)} collective-permute-done((f32[64,1024]{1,0:T(8,128)}, f32[64,1024]{1,0:T(8,128)S(1)}, u32[]{:S(2)}, u32[]{:S(2)}) %collective-permute-start.10) | collective-permute-done | bytes 262176 | tf_op jit(solution)/shard_map/vectors_out/ppermute | solution.py:562
  102.5 2.1 %collective-permute-done.12.rest_3_ = f32[64,1024]{1,0:T(8,128)S(1)} collective-permute-done((f32[64,1024]{1,0:T(8,128)}, f32[64,1024]{1,0:T(8,128)S(1)}, u32[]{:S(2)}, u32[]{:S(2)}) %collective-permute-start.12) | collective-permute-done | bytes 262176 | tf_op jit(solution)/shard_map/vectors_out/ppermute | solution.py:562
  107.5 8.2 %all-to-all-start.5 = ((f32[16,16,1024]{2,1,0:T(8,128)}), f32[16,16,1024]{2,1,0:T(8,128)}, u32[]{:S(2)}, u32[]{:S(2)}) async-start(f32[16,16,1024]{2,1,0:T(8,128)} %bitcast.45), calls=%async_computation.5 | async-start | bytes 2097152 | tf_op jit(solution)/shard_map/primaries_out/all_to_all | solution.py:434
  115.7 1.9 %copy-done.1 = bf16[3,512,1024]{2,1,0:T(8,128)(2,1)S(1)} copy-done((bf16[3,512,1024]{2,1,0:T(8,128)(2,1)S(1)}, bf16[3,512,1024]{2,1,0:T(8,128)(2,1)}, u32[]{:S(2)}) %copy-start.1) | copy-done | bytes 3145752
  121.4 5.3 %near.1 = (f32[256,1024]{1,0:T(8,128)}, f32[256,256]{1,0:T(8,128)}) custom-call(s32[3]{0:T(128)S(1)} %pad_add_fusion.1.here_ref, f32[384,128]{1,0:T(8,128)S(1)} %bitcast.43, bf16[3,512,1024]{2,1,0:T(8,128)(2,1)S(1)} %copy-done.1, f32[8,512]{1,0:T(8,128)S(1)} %get-tuple-element.120.norms_ref, f32[64,1024]{1,0:T(8,128)S(1)} %copy-done.6, ...), custom_call_target="tpu_custom_call" | custom-call | tf_op jit(solution)/shard_map/near/pallas_call | solution.py:48
  126.7 4.2 %all-to-all-done.5 = f32[16,16,1024]{2,1,0:T(8,128)} async-done(((f32[16,16,1024]{2,1,0:T(8,128)}), f32[16,16,1024]{2,1,0:T(8,128)}, u32[]{:S(2)}, u32[]{:S(2)}) %all-to-all-start.5) | async-done | bytes 1048608 | tf_op jit(solution)/shard_map/primaries_out/all_to_all | solution.py:434
  130.9 3.5 %loss.1 = f32[128,128]{1,0:T(8,128)} custom-call(f32[256,1024]{1,0:T(8,128)} %bitcast.20.p_ref, f32[256,1024]{1,0:T(8,128)} %get-tuple-element.121.x_ref, f32[256,256]{1,0:T(8,128)} %get-tuple-element.122.near_ref, bf16[3,512,1024]{2,1,0:T(8,128)(2,1)S(1)} %copy-done.2), custom_call_target="tpu_custom_call" | custom-call | tf_op jit(solution)/shard_map/loss/pallas_call | solution.py:48
  134.4 10.9 %all-to-all-start.6 = ((f32[128,1,128]{2,1,0:T(1,128)}), f32[128,1,128]{2,1,0:T(1,128)S(1)}, u32[]{:S(2)}, u32[]{:S(2)}) async-start(f32[128,1,128]{2,1,0:T(1,128)} %bitcast.22), calls=%async_computation.6 | async-start | bytes 131072 | tf_op jit(solution)/shard_map/losses_back/all_to_all | solution.py:434
  145.4 11.0 %all-to-all-done.6 = f32[128,1,128]{2,1,0:T(1,128)S(1)} async-done(((f32[128,1,128]{2,1,0:T(1,128)}), f32[128,1,128]{2,1,0:T(1,128)S(1)}, u32[]{:S(2)}, u32[]{:S(2)}) %all-to-all-start.6) | async-done | bytes 65568 | tf_op jit(solution)/shard_map/losses_back/all_to_all | solution.py:434
  (82 shorter events, 38.5 us)
Async XLA Ops:
  2.0 31.2 %all-to-all-start.2 = ((f32[128,1,384]{2,1,0:T(1,128)}), f32[128,1,384]{2,1,0:T(1,128)S(1)}, u32[]{:S(2)}, u32[]{:S(2)}) async-start(f32[128,1,384]{2,1,0:T(1,128)} %bitcast.48), calls=%async_computation.2 | async-start | bytes 393216 | tf_op jit(solution)/shard_map/requests/all_to_all | solution.py:434
  17.5 11.1 %collective-permute-start.3 = (f32[32,1024]{1,0:T(8,128)}, f32[32,1024]{1,0:T(8,128)S(1)}, u32[]{:S(2)}, u32[]{:S(2)}) collective-permute-start(f32[32,1024]{1,0:T(8,128)} %rest_0_.1), channel_id=1, source_target_pairs={{0,2},{2,4},{4,6},{6,8},{8,10},{10,12},{12,14},{14,0},{1,3},{3,5},... | collective-permute-start | bytes 393224 | tf_op jit(solution)/shard_map/column_vectors/ppermute | solution.py:443
  19.0 9.5 %collective-permute-start.2 = (f32[32,1024]{1,0:T(8,128)}, f32[32,1024]{1,0:T(8,128)S(1)}, u32[]{:S(2)}, u32[]{:S(2)}) collective-permute-start(f32[32,1024]{1,0:T(8,128)} %rest_0_.1), channel_id=1, source_target_pairs={{0,14},{2,0},{4,2},{6,4},{8,6},{10,8},{12,10},{14,12},{1,15},{3,1}... | collective-permute-start | bytes 393224 | tf_op jit(solution)/shard_map/column_vectors/ppermute | solution.py:443
  20.8 11.1 %collective-permute-start.1 = (f32[32,1024]{1,0:T(8,128)}, f32[32,1024]{1,0:T(8,128)S(1)}, u32[]{:S(2)}, u32[]{:S(2)}) collective-permute-start(f32[32,1024]{1,0:T(8,128)} %rest_0_.1), channel_id=1, source_target_pairs={{0,4},{2,6},{4,8},{6,10},{8,12},{10,14},{12,0},{14,2},{1,5},{3,7},... | collective-permute-start | bytes 393224 | tf_op jit(solution)/shard_map/column_vectors/ppermute | solution.py:443
  22.0 10.6 %collective-permute-start = (f32[32,1024]{1,0:T(8,128)}, f32[32,1024]{1,0:T(8,128)S(1)}, u32[]{:S(2)}, u32[]{:S(2)}) collective-permute-start(f32[32,1024]{1,0:T(8,128)} %rest_0_.1), channel_id=1, source_target_pairs={{0,12},{2,14},{4,0},{6,2},{8,4},{10,6},{12,8},{14,10},{1,13},{3,15... | collective-permute-start | bytes 393224 | tf_op jit(solution)/shard_map/column_vectors/ppermute | solution.py:443
  37.8 22.7 %all-to-all-start.3 = ((f32[16,16,1024]{2,1,0:T(8,128)}), f32[16,16,1024]{2,1,0:T(8,128)}, u32[]{:S(2)}, u32[]{:S(2)}) async-start(f32[16,16,1024]{2,1,0:T(8,128)} %fetch.1.found_ref), calls=%async_computation.3 | async-start | bytes 2097152 | tf_op jit(solution)/shard_map/primary_rows/all_to_all | solution.py:434
  45.5 10.7 %collective-permute-start.4 = (f32[32,1024]{1,0:T(8,128)}, f32[32,1024]{1,0:T(8,128)S(1)}, u32[]{:S(2)}, u32[]{:S(2)}) collective-permute-start(f32[32,1024]{1,0:T(8,128)} %rest_0_.1), channel_id=1, source_target_pairs={{0,8},{2,10},{4,12},{6,14},{8,0},{10,2},{12,4},{14,6},{1,9},{3,11}... | collective-permute-start | bytes 393224 | tf_op jit(solution)/shard_map/column_vectors/ppermute | solution.py:443
  49.2 9.4 %collective-permute-start.6 = (f32[32,1024]{1,0:T(8,128)}, f32[32,1024]{1,0:T(8,128)S(1)}, u32[]{:S(2)}, u32[]{:S(2)}) collective-permute-start(f32[32,1024]{1,0:T(8,128)} %copy-done.16), channel_id=1, source_target_pairs={{0,2},{2,4},{4,6},{6,8},{8,10},{10,12},{12,14},{14,0},{1,3},{3,5},... | collective-permute-start | bytes 393224 | tf_op jit(solution)/shard_map/column_vectors/ppermute | solution.py:443
  50.6 8.1 %collective-permute-start.5 = (f32[32,1024]{1,0:T(8,128)}, f32[32,1024]{1,0:T(8,128)S(1)}, u32[]{:S(2)}, u32[]{:S(2)}) collective-permute-start(f32[32,1024]{1,0:T(8,128)} %copy-done.19), channel_id=1, source_target_pairs={{0,14},{2,0},{4,2},{6,4},{8,6},{10,8},{12,10},{14,12},{1,15},{3,1}... | collective-permute-start | bytes 393224 | tf_op jit(solution)/shard_map/column_vectors/ppermute | solution.py:443
  52.5 16.0 %copy-start.15 = (f32[32,1024]{1,0:T(8,128)S(1)}, f32[32,1024]{1,0:T(8,128)}, u32[]{:S(2)}) copy-start(f32[32,1024]{1,0:T(8,128)} %copy-done.13) | copy-start | bytes 393220
  52.5 16.0 %copy-start.18 = (f32[32,1024]{1,0:T(8,128)S(1)}, f32[32,1024]{1,0:T(8,128)}, u32[]{:S(2)}) copy-start(f32[32,1024]{1,0:T(8,128)} %copy-done.16) | copy-start | bytes 393220
  52.6 16.0 %copy-start.21 = (f32[32,1024]{1,0:T(8,128)S(1)}, f32[32,1024]{1,0:T(8,128)}, u32[]{:S(2)}) copy-start(f32[32,1024]{1,0:T(8,128)} %copy-done.19) | copy-start | bytes 393220
  52.6 16.0 %copy-start.23 = (f32[32,1024]{1,0:T(8,128)S(1)}, f32[32,1024]{1,0:T(8,128)}, u32[]{:S(2)}) copy-start(f32[32,1024]{1,0:T(8,128)} %rest_0_.1) | copy-start | bytes 393220
  63.2 41.4 %all-to-all-start.4 = ((f32[8,32,1024]{2,1,0:T(8,128)}), f32[8,32,1024]{2,1,0:T(8,128)S(1)}, u32[]{:S(2)}, u32[]{:S(2)}) async-start(f32[8,32,1024]{2,1,0:T(8,128)} %bitcast.39), calls=%async_computation.4 | async-start | bytes 2097152 | tf_op jit(solution)/shard_map/primary_across/all_to_all | solution.py:434
  73.4 12.9 %collective-permute-start.7 = (f32[64,1024]{1,0:T(8,128)}, f32[64,1024]{1,0:T(8,128)S(1)}, u32[]{:S(2)}, u32[]{:S(2)}) collective-permute-start(f32[64,1024]{1,0:T(8,128)} %get-tuple-element.109), channel_id=1, source_target_pairs={{0,64},{64,128},{128,192},{192,0},{1,65},{65,129},{129,193},{193,1... | collective-permute-start | bytes 786440 | tf_op jit(solution)/shard_map/vectors_out/ppermute | solution.py:562
  73.5 12.8 %collective-permute-start.8 = (f32[64,1024]{1,0:T(8,128)}, f32[64,1024]{1,0:T(8,128)S(1)}, u32[]{:S(2)}, u32[]{:S(2)}) collective-permute-start(f32[64,1024]{1,0:T(8,128)} %get-tuple-element.110), channel_id=1, source_target_pairs={{0,128},{64,192},{128,0},{192,64},{1,129},{65,193},{129,1},{193,65... | collective-permute-start | bytes 786440 | tf_op jit(solution)/shard_map/vectors_out/ppermute | solution.py:562
  75.8 11.1 %collective-permute-start.9 = (f32[64,1024]{1,0:T(8,128)}, f32[64,1024]{1,0:T(8,128)S(1)}, u32[]{:S(2)}, u32[]{:S(2)}) collective-permute-start(f32[64,1024]{1,0:T(8,128)} %get-tuple-element.111), channel_id=1, source_target_pairs={{0,192},{64,0},{128,64},{192,128},{1,193},{65,1},{129,65},{193,129... | collective-permute-start | bytes 786440 | tf_op jit(solution)/shard_map/vectors_out/ppermute | solution.py:562
  89.7 12.6 %collective-permute-start.10 = (f32[64,1024]{1,0:T(8,128)}, f32[64,1024]{1,0:T(8,128)S(1)}, u32[]{:S(2)}, u32[]{:S(2)}) collective-permute-start(f32[64,1024]{1,0:T(8,128)} %get-tuple-element.113), channel_id=1, source_target_pairs={{0,16},{16,32},{32,48},{48,0},{1,17},{17,33},{33,49},{49,1},{2,18}... | collective-permute-start | bytes 786440 | tf_op jit(solution)/shard_map/vectors_out/ppermute | solution.py:562
  91.5 11.0 %collective-permute-start.11 = (f32[64,1024]{1,0:T(8,128)}, f32[64,1024]{1,0:T(8,128)S(1)}, u32[]{:S(2)}, u32[]{:S(2)}) collective-permute-start(f32[64,1024]{1,0:T(8,128)} %get-tuple-element.114), channel_id=1, source_target_pairs={{0,32},{16,48},{32,0},{48,16},{1,33},{17,49},{33,1},{49,17},{2,34}... | collective-permute-start | bytes 786440 | tf_op jit(solution)/shard_map/vectors_out/ppermute | solution.py:562
  93.2 11.4 %collective-permute-start.12 = (f32[64,1024]{1,0:T(8,128)}, f32[64,1024]{1,0:T(8,128)S(1)}, u32[]{:S(2)}, u32[]{:S(2)}) collective-permute-start(f32[64,1024]{1,0:T(8,128)} %get-tuple-element.115), channel_id=1, source_target_pairs={{0,48},{16,0},{32,16},{48,32},{1,49},{17,1},{33,17},{49,33},{2,50}... | collective-permute-start | bytes 786440 | tf_op jit(solution)/shard_map/vectors_out/ppermute | solution.py:562
  94.9 1.2 collective-permute-start.13
  107.5 23.5 %all-to-all-start.5 = ((f32[16,16,1024]{2,1,0:T(8,128)}), f32[16,16,1024]{2,1,0:T(8,128)}, u32[]{:S(2)}, u32[]{:S(2)}) async-start(f32[16,16,1024]{2,1,0:T(8,128)} %bitcast.45), calls=%async_computation.5 | async-start | bytes 2097152 | tf_op jit(solution)/shard_map/primaries_out/all_to_all | solution.py:434
  126.7 18.6 %copy-start.24 = (s32[32,4]{0,1:T(4,128)S(1)}, s32[32,4]{0,1:T(4,128)}, u32[]{:S(2)}) copy-start(s32[32,4]{0,1:T(4,128)} %param.14) | copy-start | bytes 1540
  134.4 22.0 %all-to-all-start.6 = ((f32[128,1,128]{2,1,0:T(1,128)}), f32[128,1,128]{2,1,0:T(1,128)S(1)}, u32[]{:S(2)}, u32[]{:S(2)}) async-start(f32[128,1,128]{2,1,0:T(1,128)} %bitcast.22), calls=%async_computation.6 | async-start | bytes 131072 | tf_op jit(solution)/shard_map/losses_back/all_to_all | solution.py:434
  (20 other events, 47.2 us)

commit v9 on v6

--- a/solution.py
+++ b/solution.py
@@ -20,7 +20,7 @@
 K = 32
 NEXT = 8
 PER = 3
-FIRST = (2, -2, 1, -1)
+FIRST = (2, -2)
 amplify = 1.0
 tiny = 1e-06
 
@@ -519,7 +519,7 @@
         )
     with jax.named_scope("primary_across"):
         send, take = relay(jnp.int32(0), K)
-        got = across(jnp.int32(0), send, blocks[4], blocks[3], blocks[-3])
+        got = across(jnp.int32(0), send, *[blocks[o] for o in (4, 3, -3, 1, -1)])
         next_send, next_take = relay(jnp.int32(K), NEXT)
         [both] = call(
             functools.partial(put_kernel, D),

time: 150 us -> 150 us (level)
  no operation moved by 1% of the time
where the time goes in v9:
time: 150 us; the launch traced here: 149 us
  starting transfers between devices  46.6 us (31%)
  waiting for transfers between devices  41.5 us (28%)
  blocking collectives  34.7 us (23%)
  Pallas kernels  22.3 us (15%)
  local copies, waits for them, and re-layouts  2.86 us (2%)
    all_to_all x1, blocking collectives, swap(): return lax.all_to_all(a, axes, split_axis=0, concat_axis=0, tiled=True)  34.7 us
    all_to_all x4, starting transfers between devices, swap(): return lax.all_to_all(a, axes, split_axis=0, concat_axis=0, tiled=True)  33.7 us
    all_to_all x4, waiting for transfers between devices, swap(): return lax.all_to_all(a, axes, split_axis=0, concat_axis=0, tiled=True)  32 us
    pallas_call x11, Pallas kernels, call(): pl.pallas_call(kernel, out_shape=out_shape, in_specs=specs, out_specs=[HB...  22.3 us
    ppermute x7, starting transfers between devices, along_z(): return lax.ppermute(block, 'z', [(z, (z - step) % NZ) for z in range(NZ)])  12.9 us
    ppermute x7, waiting for transfers between devices, along_z(): return lax.ppermute(block, 'z', [(z, (z - step) % NZ) for z in range(NZ)])  9.52 us
  transfers between devices with their start and end apart: 12, of which 8 were waited for; matrix products, arithmetic and copies ran while one was open for 0% of the time, Pallas kernels for 7%

profile of v9, /device:TPU:2, one launch (start us, length us, event | category | flops | bytes accessed | tf_op | source)
XLA Modules:
  0.0 149.4 jit_solution(11686290654663477214)
XLA Ops:
  0.0 2.0 %request.1 = f32[384,128]{1,0:T(8,128)} custom-call(s32[1,32]{1,0:T(1,128)} %bitcast.51, s32[1,32]{1,0:T(1,128)} %bitcast.52, s32[4,32]{1,0:T(4,128)} %bitcast.50, s32[32,256]{1,0:T(8,128)} %rows_ref.1), custom_call_target="tpu_custom_call" | custom-call | tf_op jit(solution)/shard_map/requests/request/pallas_call | solution.py:45
  2.0 15.4 %all-to-all-start.2 = ((f32[128,1,384]{2,1,0:T(1,128)}), f32[128,1,384]{2,1,0:T(1,128)S(1)}, u32[]{:S(2)}, u32[]{:S(2)}) async-start(f32[128,1,384]{2,1,0:T(1,128)} %bitcast.49), calls=%async_computation.2 | async-start | bytes 393216 | tf_op jit(solution)/shard_map/requests/all_to_all | solution.py:384
  17.5 3.7 %collective-permute-start = (f32[32,1024]{1,0:T(8,128)}, f32[32,1024]{1,0:T(8,128)S(1)}, u32[]{:S(2)}, u32[]{:S(2)}) collective-permute-start(f32[32,1024]{1,0:T(8,128)} %rest_0_.1), channel_id=1, source_target_pairs={{0,12},{2,14},{4,0},{6,2},{8,4},{10,6},{12,8},{14,10},{1,13},{3,15... | collective-permute-start | bytes 393224 | tf_op jit(solution)/shard_map/column_vectors/ppermute | solution.py:392
  21.1 1.6 %copy-done.2 = f32[512,1024]{1,0:T(8,128)S(1)} copy-done((f32[512,1024]{1,0:T(8,128)S(1)}, f32[512,1024]{1,0:T(8,128)}, u32[]{:S(2)}) %copy-start.2) | copy-done | bytes 2097176
  22.7 1.5 prepare.1
  24.2 5.1 %collective-permute-done.rest_0_.rest_2_ = f32[32,1024]{1,0:T(8,128)S(1)} collective-permute-done((f32[32,1024]{1,0:T(8,128)}, f32[32,1024]{1,0:T(8,128)S(1)}, u32[]{:S(2)}, u32[]{:S(2)}) %collective-permute-start) | collective-permute-done | bytes 131104 | tf_op jit(solution)/shard_map/column_vectors/ppermute | solution.py:392
  30.0 1.9 %fetch.1.found_ref = f32[16,16,1024]{2,1,0:T(8,128)} custom-call(f32[384,128]{1,0:T(8,128)S(1)} %bitcast.39, bf16[3,512,1024]{2,1,0:T(8,128)(2,1)S(1)} %get-tuple-element.88.pieces_ref, f32[32,1024]{1,0:T(8,128)} %copy-done.3, f32[32,1024]{1,0:T(8,128)} %collective-permute-done.1.rest_1_.rest_6_), custom_call_target="tpu_custom_call" | custom-call | tf_op jit(solution)/shard_map/primary_rows/fetch/pallas_call | solution.py:45
  31.9 7.7 %all-to-all-start.3 = ((f32[16,16,1024]{2,1,0:T(8,128)}), f32[16,16,1024]{2,1,0:T(8,128)S(1)}, u32[]{:S(2)}, u32[]{:S(2)}) async-start(f32[16,16,1024]{2,1,0:T(8,128)} %fetch.1.found_ref), calls=%async_computation.3 | async-start | bytes 2097152 | tf_op jit(solution)/shard_map/primary_rows/all_to_all | solution.py:384
  39.7 3.3 %collective-permute-start.2 = (f32[32,1024]{1,0:T(8,128)}, f32[32,1024]{1,0:T(8,128)S(1)}, u32[]{:S(2)}, u32[]{:S(2)}) collective-permute-start(f32[32,1024]{1,0:T(8,128)} %rest_0_.1), channel_id=1, source_target_pairs={{0,8},{2,10},{4,12},{6,14},{8,0},{10,2},{12,4},{14,6},{1,9},{3,11}... | collective-permute-start | bytes 393224 | tf_op jit(solution)/shard_map/column_vectors/ppermute | solution.py:392
  43.0 2.7 %collective-permute-start.5 = (f32[32,1024]{1,0:T(8,128)}, f32[32,1024]{1,0:T(8,128)S(1)}, u32[]{:S(2)}, u32[]{:S(2)}) collective-permute-start(f32[32,1024]{1,0:T(8,128)} %rest_0_.1), channel_id=1, source_target_pairs={{0,14},{2,0},{4,2},{6,4},{8,6},{10,8},{12,10},{14,12},{1,15},{3,1}... | collective-permute-start | bytes 393224 | tf_op jit(solution)/shard_map/column_vectors/ppermute | solution.py:392
  45.6 3.2 %collective-permute-start.3 = (f32[32,1024]{1,0:T(8,128)}, f32[32,1024]{1,0:T(8,128)S(1)}, u32[]{:S(2)}, u32[]{:S(2)}) collective-permute-start(f32[32,1024]{1,0:T(8,128)} %copy-done.3), channel_id=1, source_target_pairs={{0,14},{2,0},{4,2},{6,4},{8,6},{10,8},{12,10},{14,12},{1,15},{3,1}... | collective-permute-start | bytes 393224 | tf_op jit(solution)/shard_map/column_vectors/ppermute | solution.py:392
  49.0 1.9 %slots.1 = (s32[256,128]{1,0:T(8,128)S(1)}, f32[256,256]{1,0:T(8,128)S(1)}, s32[8,128]{1,0:T(8,128)S(1)}) custom-call(s32[2]{0:T(128)S(1)} %pad_add_fusion.me_ref, f32[384,128]{1,0:T(8,128)S(1)} %bitcast.40, f32[16,16,1024]{2,1,0:T(8,128)} %fetch.1.found_ref), custom_call_target="tpu_custom_call" | custom-call | tf_op jit(solution)/shard_map/slots/pallas_call | solution.py:45
  50.9 1.7 %relay.3 = (bf16[256,256]{1,0:T(8,128)(2,1)S(1)}, bf16[256,256]{1,0:T(8,128)(2,1)S(1)}) custom-call(s32[2]{0:T(128)S(1)} %pad_add_fusion.me_ref, s32[1]{0:T(128)} %constant.28.clone.1.turn_ref.base_ref, s32[256,128]{1,0:T(8,128)S(1)} %get-tuple-element.237.info_ref, f32[256,256]{1,0:T(8,128)S(1)} %get-tuple-element.238.slots_ref), custom_call_target="tpu_custom_call" | custom-call | tf_op jit(solution)/shard_map/primary_across/relay/pallas_call | solution.py:45
  52.6 1.5 %collective-permute-done.5.rest_3_.rest_1_ = f32[32,1024]{1,0:T(8,128)S(1)} collective-permute-done((f32[32,1024]{1,0:T(8,128)}, f32[32,1024]{1,0:T(8,128)S(1)}, u32[]{:S(2)}, u32[]{:S(2)}) %collective-permute-start.5) | collective-permute-done | bytes 131104 | tf_op jit(solution)/shard_map/column_vectors/ppermute | solution.py:392
  57.0 1.5 %send.3 = f32[256,1024]{1,0:T(8,128)} custom-call(s32[1]{0:T(128)} %constant.28.clone.1.turn_ref.base_ref, bf16[256,256]{1,0:T(8,128)(2,1)S(1)} %get-tuple-element.92.onehot_ref, f32[256,1024]{1,0:T(8,128)S(1)} %bitcast.44, f32[32,1024]{1,0:T(8,128)} %copy-done.4, f32[32,1024]{1,0:T(8,128)} %copy-done.7, f32[32,1024]{1,0:T(8,128)} %copy-done.8, ...), custom_call_target="tpu_custom_call" | custom-call | tf_op jit(solution)/shard_map/primary_across/send/pallas_call | solution.py:45
  58.5 3.9 %all-to-all-start.4 = ((f32[8,32,1024]{2,1,0:T(8,128)}), f32[8,32,1024]{2,1,0:T(8,128)S(1)}, u32[]{:S(2)}, u32[]{:S(2)}) async-start(f32[8,32,1024]{2,1,0:T(8,128)} %bitcast.48), calls=%async_computation.4 | async-start | bytes 2097152 | tf_op jit(solution)/shard_map/primary_across/all_to_all | solution.py:384
  62.4 2.0 %relay.4 = (bf16[64,256]{1,0:T(8,128)(2,1)S(1)}, bf16[256,64]{1,0:T(8,128)(2,1)S(1)}) custom-call(s32[2]{0:T(128)S(1)} %pad_add_fusion.me_ref, s32[1]{0:T(128)} %constant.29.clone.1.turn_ref, s32[256,128]{1,0:T(8,128)S(1)} %get-tuple-element.237.info_ref, f32[256,256]{1,0:T(8,128)S(1)} %get-tuple-element.238.slots_ref), custom_call_target="tpu_custom_call" | custom-call | tf_op jit(solution)/shard_map/primary_across/relay/pallas_call | solution.py:45
  64.9 3.4 %vectors.1.both_ref = f32[256,2048]{1,0:T(8,128)} custom-call(s32[2]{0:T(128)S(1)} %pad_add_fusion.me_ref, f32[256,256]{1,0:T(8,128)S(1)} %get-tuple-element.238.slots_ref, f32[32,1024]{1,0:T(8,128)} %rest_0_.1, f32[32,1024]{1,0:T(8,128)} %copy-done.5, f32[32,1024]{1,0:T(8,128)} %copy-done.3, f32[32,1024]{1,0:T(8,128)} %copy-done.7, f32[32,1024]{1,0:T(8,128)} %copy-done.4, ...), custom_call_target="tpu_custom_call" | custom-call | tf_op jit(solution)/shard_map/vectors_out/vectors/pallas_call | solution.py:45
  69.6 20.9 %all-to-all-done.4 = f32[8,32,1024]{2,1,0:T(8,128)S(1)} async-done(((f32[8,32,1024]{2,1,0:T(8,128)}), f32[8,32,1024]{2,1,0:T(8,128)S(1)}, u32[]{:S(2)}, u32[]{:S(2)}) %all-to-all-start.4) | async-done | bytes 1048608 | tf_op jit(solution)/shard_map/primary_across/all_to_all | solution.py:384
  90.5 1.6 %put.1 = f32[256,2048]{1,0:T(8,128)} custom-call(bf16[256,256]{1,0:T(8,128)(2,1)S(1)} %get-tuple-element.91.onehot_ref, f32[256,1024]{1,0:T(8,128)S(1)} %bitcast.38, f32[256,2048]{1,0:T(8,128)} %vectors.1.both_ref), custom_call_target="tpu_custom_call", output_to_operand_aliasing={{}: (2, {})} | custom-call | tf_op jit(solution)/shard_map/primary_across/put/pallas_call | solution.py:45
  92.1 34.7 %all_to_all.37 = f32[16,16,2048]{2,1,0:T(8,128)S(1)} all-to-all(f32[16,16,2048]{2,1,0:T(8,128)} %bitcast.43), channel_id=1, replica_groups=mesh['y'=4,'x'=4,'z'=8,'rep'=2] {'y','x'}, dimensions={0} | all-to-all | bytes 4194304 | tf_op jit(solution)/shard_map/out_to_owners/all_to_all | solution.py:384
  126.8 3.6 %loss.1 = f32[128,128]{1,0:T(8,128)} custom-call(f32[256,2048]{1,0:T(8,128)S(1)} %bitcast.37, f32[384,128]{1,0:T(8,128)S(1)} %bitcast.41, bf16[3,512,1024]{2,1,0:T(8,128)(2,1)S(1)} %copy-done.1, f32[8,512]{1,0:T(8,128)S(1)} %get-tuple-element.99.norms_ref), custom_call_target="tpu_custom_call" | custom-call | tf_op jit(solution)/shard_map/loss/pallas_call | solution.py:45
  130.5 6.7 %all-to-all-start.6 = ((f32[128,1,128]{2,1,0:T(1,128)}), f32[128,1,128]{2,1,0:T(1,128)S(1)}, u32[]{:S(2)}, u32[]{:S(2)}) async-start(f32[128,1,128]{2,1,0:T(1,128)} %bitcast.20), calls=%async_computation.6 | async-start | bytes 131072 | tf_op jit(solution)/shard_map/losses_back/all_to_all | solution.py:384
  137.2 11.0 %all-to-all-done.6 = f32[128,1,128]{2,1,0:T(1,128)S(1)} async-done(((f32[128,1,128]{2,1,0:T(1,128)}), f32[128,1,128]{2,1,0:T(1,128)S(1)}, u32[]{:S(2)}, u32[]{:S(2)}) %all-to-all-start.6) | async-done | bytes 65568 | tf_op jit(solution)/shard_map/losses_back/all_to_all | solution.py:384
  (37 shorter events, 5.4 us)
Async XLA Ops:
  2.0 28.0 %all-to-all-start.2 = ((f32[128,1,384]{2,1,0:T(1,128)}), f32[128,1,384]{2,1,0:T(1,128)S(1)}, u32[]{:S(2)}, u32[]{:S(2)}) async-start(f32[128,1,384]{2,1,0:T(1,128)} %bitcast.49), calls=%async_computation.2 | async-start | bytes 393216 | tf_op jit(solution)/shard_map/requests/all_to_all | solution.py:384
  17.5 11.9 %collective-permute-start = (f32[32,1024]{1,0:T(8,128)}, f32[32,1024]{1,0:T(8,128)S(1)}, u32[]{:S(2)}, u32[]{:S(2)}) collective-permute-start(f32[32,1024]{1,0:T(8,128)} %rest_0_.1), channel_id=1, source_target_pairs={{0,12},{2,14},{4,0},{6,2},{8,4},{10,6},{12,8},{14,10},{1,13},{3,15... | collective-permute-start | bytes 393224 | tf_op jit(solution)/shard_map/column_vectors/ppermute | solution.py:392
  21.1 8.8 %collective-permute-start.1 = (f32[32,1024]{1,0:T(8,128)}, f32[32,1024]{1,0:T(8,128)}, u32[]{:S(2)}, u32[]{:S(2)}) collective-permute-start(f32[32,1024]{1,0:T(8,128)} %rest_0_.1), channel_id=1, source_target_pairs={{0,4},{2,6},{4,8},{6,10},{8,12},{10,14},{12,0},{14,2},{1,5},{3,7},... | collective-permute-start | bytes 393224 | tf_op jit(solution)/shard_map/column_vectors/ppermute | solution.py:392
  21.1 1.6 %copy-start.2 = (f32[512,1024]{1,0:T(8,128)S(1)}, f32[512,1024]{1,0:T(8,128)}, u32[]{:S(2)}) copy-start(f32[512,1024]{1,0:T(8,128)} %c_ref.1) | copy-start | bytes 6291460
  24.2 7.7 %copy-start = (bf16[3,512,1024]{2,1,0:T(8,128)(2,1)}, bf16[3,512,1024]{2,1,0:T(8,128)(2,1)S(1)}, u32[]{:S(2)}) copy-start(bf16[3,512,1024]{2,1,0:T(8,128)(2,1)S(1)} %get-tuple-element.88.pieces_ref) | copy-start | bytes 9437188
  29.3 0.6 copy-start.3
  31.9 24.4 %all-to-all-start.3 = ((f32[16,16,1024]{2,1,0:T(8,128)}), f32[16,16,1024]{2,1,0:T(8,128)S(1)}, u32[]{:S(2)}, u32[]{:S(2)}) async-start(f32[16,16,1024]{2,1,0:T(8,128)} %fetch.1.found_ref), calls=%async_computation.3 | async-start | bytes 2097152 | tf_op jit(solution)/shard_map/primary_rows/all_to_all | solution.py:384
  39.7 12.9 %collective-permute-start.2 = (f32[32,1024]{1,0:T(8,128)}, f32[32,1024]{1,0:T(8,128)S(1)}, u32[]{:S(2)}, u32[]{:S(2)}) collective-permute-start(f32[32,1024]{1,0:T(8,128)} %rest_0_.1), channel_id=1, source_target_pairs={{0,8},{2,10},{4,12},{6,14},{8,0},{10,2},{12,4},{14,6},{1,9},{3,11}... | collective-permute-start | bytes 393224 | tf_op jit(solution)/shard_map/column_vectors/ppermute | solution.py:392
  43.0 11.1 %collective-permute-start.5 = (f32[32,1024]{1,0:T(8,128)}, f32[32,1024]{1,0:T(8,128)S(1)}, u32[]{:S(2)}, u32[]{:S(2)}) collective-permute-start(f32[32,1024]{1,0:T(8,128)} %rest_0_.1), channel_id=1, source_target_pairs={{0,14},{2,0},{4,2},{6,4},{8,6},{10,8},{12,10},{14,12},{1,15},{3,1}... | collective-permute-start | bytes 393224 | tf_op jit(solution)/shard_map/column_vectors/ppermute | solution.py:392
  45.6 9.0 %collective-permute-start.6 = (f32[32,1024]{1,0:T(8,128)}, f32[32,1024]{1,0:T(8,128)S(1)}, u32[]{:S(2)}, u32[]{:S(2)}) collective-permute-start(f32[32,1024]{1,0:T(8,128)} %rest_0_.1), channel_id=1, source_target_pairs={{0,2},{2,4},{4,6},{6,8},{8,10},{10,12},{12,14},{14,0},{1,3},{3,5},... | collective-permute-start | bytes 393224 | tf_op jit(solution)/shard_map/column_vectors/ppermute | solution.py:392
  45.6 9.9 %collective-permute-start.3 = (f32[32,1024]{1,0:T(8,128)}, f32[32,1024]{1,0:T(8,128)S(1)}, u32[]{:S(2)}, u32[]{:S(2)}) collective-permute-start(f32[32,1024]{1,0:T(8,128)} %copy-done.3), channel_id=1, source_target_pairs={{0,14},{2,0},{4,2},{6,4},{8,6},{10,8},{12,10},{14,12},{1,15},{3,1}... | collective-permute-start | bytes 393224 | tf_op jit(solution)/shard_map/column_vectors/ppermute | solution.py:392
  48.9 7.4 %collective-permute-start.4 = (f32[32,1024]{1,0:T(8,128)}, f32[32,1024]{1,0:T(8,128)S(1)}, u32[]{:S(2)}, u32[]{:S(2)}) collective-permute-start(f32[32,1024]{1,0:T(8,128)} %collective-permute-done.1.rest_1_.rest_6_), channel_id=1, source_target_pairs={{0,2},{2,4},{4,6},{6,8},{8,10},{10,12},{12,14},{14,0},{1,3},{3,5},... | collective-permute-start | bytes 393224 | tf_op jit(solution)/shard_map/column_vectors/ppermute | solution.py:392
  52.6 3.8 %copy-start.4 = (f32[32,1024]{1,0:T(8,128)}, f32[32,1024]{1,0:T(8,128)S(1)}, u32[]{:S(2)}) copy-start(f32[32,1024]{1,0:T(8,128)S(1)} %collective-permute-done.2.rest_0_.rest_4_) | copy-start | bytes 393220
  54.1 2.2 %copy-start.5 = (f32[32,1024]{1,0:T(8,128)}, f32[32,1024]{1,0:T(8,128)S(1)}, u32[]{:S(2)}) copy-start(f32[32,1024]{1,0:T(8,128)S(1)} %collective-permute-done.5.rest_3_.rest_1_) | copy-start | bytes 393220
  54.6 1.7 %copy-start.6 = (f32[32,1024]{1,0:T(8,128)}, f32[32,1024]{1,0:T(8,128)S(1)}, u32[]{:S(2)}) copy-start(f32[32,1024]{1,0:T(8,128)S(1)} %collective-permute-done.6.rest_4_.rest_7_) | copy-start | bytes 393220
  55.5 0.9 copy-start.7
  56.3 0.7 copy-start.8
  58.5 32.0 %all-to-all-start.4 = ((f32[8,32,1024]{2,1,0:T(8,128)}), f32[8,32,1024]{2,1,0:T(8,128)S(1)}, u32[]{:S(2)}, u32[]{:S(2)}) async-start(f32[8,32,1024]{2,1,0:T(8,128)} %bitcast.48), calls=%async_computation.4 | async-start | bytes 2097152 | tf_op jit(solution)/shard_map/primary_across/all_to_all | solution.py:384
  64.9 3.4 %collective-permute-start.7 = (s32[1,1]{1,0:T(1,128)}, s32[1,1]{1,0:T(1,128)}, u32[]{:S(2)}, u32[]{:S(2)}) collective-permute-start(s32[1,1]{1,0:T(1,128)} %slice.3), channel_id=1, source_target_pairs={{0,1},{1,0},{2,3},{3,2},{4,5},{5,4},{6,7},{7,6},{8,9},{9,8},{10,11... | collective-permute-start | bytes 20 | tf_op jit(solution)/shard_map/ppermute | solution.py:449
  92.1 34.7 %copy-start.1 = (bf16[3,512,1024]{2,1,0:T(8,128)(2,1)S(1)}, bf16[3,512,1024]{2,1,0:T(8,128)(2,1)}, u32[]{:S(2)}) copy-start(bf16[3,512,1024]{2,1,0:T(8,128)(2,1)} %copy-done) | copy-start | bytes 9437188
  126.8 10.3 %copy-start.9 = (s32[32,4]{0,1:T(4,128)S(1)}, s32[32,4]{0,1:T(4,128)}, u32[]{:S(2)}) copy-start(s32[32,4]{0,1:T(4,128)} %param.14) | copy-start | bytes 1540
  130.5 17.8 %all-to-all-start.6 = ((f32[128,1,128]{2,1,0:T(1,128)}), f32[128,1,128]{2,1,0:T(1,128)S(1)}, u32[]{:S(2)}, u32[]{:S(2)}) async-start(f32[128,1,128]{2,1,0:T(1,128)} %bitcast.20), calls=%async_computation.6 | async-start | bytes 131072 | tf_op jit(solution)/shard_map/losses_back/all_to_all | solution.py:384

commit v10 on v9

--- a/solution.py
+++ b/solution.py
@@ -1,5 +1,3 @@
-import functools
-
 import jax
 import jax.numpy as jnp
 from jax import lax
@@ -18,7 +16,7 @@
 SLOTS = COLS * NZ * 2
 SHARDS = COLS * NZ
 K = 32
-NEXT = 8
+WIDER = 40
 PER = 3
 FIRST = (2, -2)
 amplify = 1.0
@@ -279,10 +277,10 @@
     wait_all(copies)
 
 
-def put_kernel(first, onehot_ref, in_ref, both_ref, out_ref, hold, sems):
+def put_kernel(onehot_ref, in_ref, both_ref, out_ref, hold, sems):
     pieces = split3(in_ref[...])
     half = SLOTS // 2
-    at = [out_ref.at[pl.ds(c * half, half), pl.ds(first, D)] for c in range(2)]
+    at = [out_ref.at[pl.ds(c * half, half), pl.ds(D, D)] for c in range(2)]
     copies = []
     for c in range(2):
         hold[c] = pick(onehot_ref[c * half : (c + 1) * half, :], pieces)
@@ -495,16 +493,13 @@
         )
         return both
 
-    def second(state):
-        base, both = state
-        return base + NEXT, add(next_take, across(base, next_send), both)
-
     def more(state):
         base, both = state
         send, take = relay(base, K)
         return base + K, add(take, across(base, send), both)
 
-    with jax.named_scope("vectors_out"):
+    def first(send, take):
+        got = across(jnp.int32(0), send, *[blocks[o] for o in (4, 3, -3, 1, -1)])
         [both] = call(
             vectors_kernel,
             pair,
@@ -517,12 +512,8 @@
             scratch=[pltpu.VMEM((COLV, D), F32), halves[0], copies_semaphores(NZ + 2)],
             name="vectors",
         )
-    with jax.named_scope("primary_across"):
-        send, take = relay(jnp.int32(0), K)
-        got = across(jnp.int32(0), send, *[blocks[o] for o in (4, 3, -3, 1, -1)])
-        next_send, next_take = relay(jnp.int32(K), NEXT)
         [both] = call(
-            functools.partial(put_kernel, D),
+            put_kernel,
             pair,
             take,
             got,
@@ -533,8 +524,14 @@
             scratch=halves,
             name="put",
         )
-        state = (jnp.int32(K), both)
-        state = lax.while_loop(lambda s: (s[0] == K) & (K < most), second, state)
+        return both
+
+    with jax.named_scope("primary_across"):
+        zero = jnp.int32(0)
+        tables = relay(zero, K)
+        calm = most <= K
+        both = lax.cond(calm, lambda: first(*tables), lambda: first(*relay(zero, WIDER)))
+        state = (jnp.where(calm, K, WIDER).astype(I32), both)
         _, both = lax.while_loop(lambda s: s[0] < most, more, state)
     with jax.named_scope("out_to_owners"):
         both = swap(both.reshape(COLS, 16, 2 * D), plane).reshape(SLOTS, 2 * D)

time: 150 us -> 154 us (1.027)
  waiting for transfers between devices: 41.5 us -> 46.3 us
  blocking collectives: 34.7 us -> 32.7 us
    all_to_all x4, waiting for transfers between devices: 32 us -> 35.7 us  [swap(): return lax.all_to_all(a, axes, split_axis=0, concat_axis=0, tiled=True)]
    all_to_all x1, blocking collectives: 34.7 us -> 32.7 us  [swap(): return lax.all_to_all(a, axes, split_axis=0, concat_axis=0, tiled=True)]
    pallas_call x11 -> x10, Pallas kernels: 22.3 us -> 22.2 us  [call(): pl.pallas_call(kernel, out_shape=out_shape, in_specs=specs, out_specs=[HB...]
  transfers between devices with their start and end apart: 12 -> 12, of which waited for: 8 -> 6; matrix products, arithmetic and copies ran while one was open for 0% -> 1% of each run, Pallas kernels for 7% -> 6%
where the time goes in v10:
time: 154 us
  starting transfers between devices  47.2 us (31%)
  waiting for transfers between devices  46.3 us (30%)
  blocking collectives  32.7 us (21%)
  Pallas kernels  22.2 us (14%)
  local copies, waits for them, and re-layouts  3.03 us (2%)
    all_to_all x4, waiting for transfers between devices, swap(): return lax.all_to_all(a, axes, split_axis=0, concat_axis=0, tiled=True)  35.7 us
    all_to_all x4, starting transfers between devices, swap(): return lax.all_to_all(a, axes, split_axis=0, concat_axis=0, tiled=True)  34.3 us
    all_to_all x1, blocking collectives, swap(): return lax.all_to_all(a, axes, split_axis=0, concat_axis=0, tiled=True)  32.7 us
    pallas_call x10, Pallas kernels, call(): pl.pallas_call(kernel, out_shape=out_shape, in_specs=specs, out_specs=[HB...  22.2 us
    ppermute x7, starting transfers between devices, along_z(): return lax.ppermute(block, 'z', [(z, (z - step) % NZ) for z in range(NZ)])  12.9 us
    ppermute x7, waiting for transfers between devices, along_z(): return lax.ppermute(block, 'z', [(z, (z - step) % NZ) for z in range(NZ)])  9.16 us
  transfers between devices with their start and end apart: 12, of which 6 were waited for; matrix products, arithmetic and copies ran while one was open for 1% of the time, Pallas kernels for 6%

profile of v10, /device:TPU:2, one launch (start us, length us, event | category | flops | bytes accessed | tf_op | source)
XLA Modules:
  0.0 153.5 jit_solution(1866359130767440953)
XLA Ops:
  0.0 2.0 %request.1 = f32[384,128]{1,0:T(8,128)} custom-call(s32[1,32]{1,0:T(1,128)} %bitcast.45, s32[1,32]{1,0:T(1,128)} %bitcast.46, s32[4,32]{1,0:T(4,128)} %bitcast.44, s32[32,256]{1,0:T(8,128)} %rows_ref.1), custom_call_target="tpu_custom_call" | custom-call | tf_op jit(solution)/shard_map/requests/request/pallas_call | solution.py:43
  2.0 15.4 %all-to-all-start.3 = ((f32[128,1,384]{2,1,0:T(1,128)}), f32[128,1,384]{2,1,0:T(1,128)S(1)}, u32[]{:S(2)}, u32[]{:S(2)}) async-start(f32[128,1,384]{2,1,0:T(1,128)} %bitcast.43), calls=%async_computation.3 | async-start | bytes 393216 | tf_op jit(solution)/shard_map/requests/all_to_all | solution.py:382
  17.5 3.7 %collective-permute-start = (f32[32,1024]{1,0:T(8,128)}, f32[32,1024]{1,0:T(8,128)S(1)}, u32[]{:S(2)}, u32[]{:S(2)}) collective-permute-start(f32[32,1024]{1,0:T(8,128)} %param.10), channel_id=1, source_target_pairs={{0,12},{2,14},{4,0},{6,2},{8,4},{10,6},{12,8},{14,10},{1,13},{3,15... | collective-permute-start | bytes 393224 | tf_op jit(solution)/shard_map/column_vectors/ppermute | solution.py:390
  21.1 1.6 %copy-done.2 = f32[512,1024]{1,0:T(8,128)S(1)} copy-done((f32[512,1024]{1,0:T(8,128)S(1)}, f32[512,1024]{1,0:T(8,128)}, u32[]{:S(2)}) %copy-start.2) | copy-done | bytes 2097176
  22.7 1.5 prepare.1
  24.2 5.2 %collective-permute-done.rest_0_ = f32[32,1024]{1,0:T(8,128)S(1)} collective-permute-done((f32[32,1024]{1,0:T(8,128)}, f32[32,1024]{1,0:T(8,128)S(1)}, u32[]{:S(2)}, u32[]{:S(2)}) %collective-permute-start) | collective-permute-done | bytes 131104 | tf_op jit(solution)/shard_map/column_vectors/ppermute | solution.py:390
  30.0 1.9 %fetch.1.found_ref = f32[16,16,1024]{2,1,0:T(8,128)} custom-call(f32[384,128]{1,0:T(8,128)S(1)} %bitcast.32, bf16[3,512,1024]{2,1,0:T(8,128)(2,1)S(1)} %get-tuple-element.132.pieces_ref, f32[32,1024]{1,0:T(8,128)} %copy-done.13, f32[32,1024]{1,0:T(8,128)} %collective-permute-done.1.rest_1_), custom_call_target="tpu_custom_call" | custom-call | tf_op jit(solution)/shard_map/primary_rows/fetch/pallas_call | solution.py:43
  31.9 7.7 %all-to-all-start.4 = ((f32[16,16,1024]{2,1,0:T(8,128)}), f32[16,16,1024]{2,1,0:T(8,128)S(1)}, u32[]{:S(2)}, u32[]{:S(2)}) async-start(f32[16,16,1024]{2,1,0:T(8,128)} %fetch.1.found_ref), calls=%async_computation.4 | async-start | bytes 2097152 | tf_op jit(solution)/shard_map/primary_rows/all_to_all | solution.py:382
  39.6 3.4 %collective-permute-start.3 = (f32[32,1024]{1,0:T(8,128)}, f32[32,1024]{1,0:T(8,128)S(1)}, u32[]{:S(2)}, u32[]{:S(2)}) collective-permute-start(f32[32,1024]{1,0:T(8,128)} %param.10), channel_id=1, source_target_pairs={{0,8},{2,10},{4,12},{6,14},{8,0},{10,2},{12,4},{14,6},{1,9},{3,11}... | collective-permute-start | bytes 393224 | tf_op jit(solution)/shard_map/column_vectors/ppermute | solution.py:390
  42.9 2.7 %collective-permute-start.6 = (f32[32,1024]{1,0:T(8,128)}, f32[32,1024]{1,0:T(8,128)S(1)}, u32[]{:S(2)}, u32[]{:S(2)}) collective-permute-start(f32[32,1024]{1,0:T(8,128)} %param.10), channel_id=1, source_target_pairs={{0,14},{2,0},{4,2},{6,4},{8,6},{10,8},{12,10},{14,12},{1,15},{3,1}... | collective-permute-start | bytes 393224 | tf_op jit(solution)/shard_map/column_vectors/ppermute | solution.py:390
  46.3 3.2 %collective-permute-start.4 = (f32[32,1024]{1,0:T(8,128)}, f32[32,1024]{1,0:T(8,128)S(1)}, u32[]{:S(2)}, u32[]{:S(2)}) collective-permute-start(f32[32,1024]{1,0:T(8,128)} %copy-done.13), channel_id=1, source_target_pairs={{0,14},{2,0},{4,2},{6,4},{8,6},{10,8},{12,10},{14,12},{1,15},{3,1}... | collective-permute-start | bytes 393224 | tf_op jit(solution)/shard_map/column_vectors/ppermute | solution.py:390
  49.5 2.1 %slots.1 = (s32[256,128]{1,0:T(8,128)S(1)}, f32[256,256]{1,0:T(8,128)S(1)}, s32[8,128]{1,0:T(8,128)S(1)}) custom-call(s32[2]{0:T(128)} %pad_add_fusion.me_ref, f32[384,128]{1,0:T(8,128)S(1)} %bitcast.33, f32[16,16,1024]{2,1,0:T(8,128)} %fetch.1.found_ref), custom_call_target="tpu_custom_call" | custom-call | tf_op jit(solution)/shard_map/slots/pallas_call | solution.py:43
  53.5 2.4 %relay.4 = (bf16[256,256]{1,0:T(8,128)(2,1)}, bf16[256,256]{1,0:T(8,128)(2,1)}) custom-call(s32[2]{0:T(128)} %pad_add_fusion.me_ref, s32[1]{0:T(128)} %constant.29.clone.1.turn_ref, s32[256,128]{1,0:T(8,128)S(1)} %get-tuple-element.206.info_ref, f32[256,256]{1,0:T(8,128)S(1)} %get-tuple-element.207.slots_ref), custom_call_target="tpu_custom_call" | custom-call | tf_op jit(solution)/shard_map/primary_across/relay/pallas_call | solution.py:43
  57.2 3.3 %collective-permute-done.5 = f32[32,1024]{1,0:T(8,128)S(1)} collective-permute-done((f32[32,1024]{1,0:T(8,128)}, f32[32,1024]{1,0:T(8,128)S(1)}, u32[]{:S(2)}, u32[]{:S(2)}) %collective-permute-start.5) | collective-permute-done | bytes 131104 | tf_op jit(solution)/shard_map/column_vectors/ppermute | solution.py:390
  60.5 36.8 %conditional.1 = (f32[256,2048]{1,0:T(8,128)}) conditional(s32[]{:T(128)} %convert_element_type.3, (s32[2]{0:T(128)}, s32[256,128]{1,0:T(8,128)S(1)}, f32[256,256]{1,0:T(8,128)S(1)}, f32[256,1024]{1,0:T(8,128)S(1)}, f32[32,1024]{1,0:T(8,128)S(1)}, /*index=5*/f32[32,1024]{1,0:T(8,128)S(1)}, f32[32,1024]{1,0:T(8,128)S(1)}, f32[32,1024]{1,0:T(8,128)S(1)}, ...), branch_computations={%region_0.0_spmd, %region_1.0_spmd} | conditional | bytes 6553780 | solution.py:533
  61.4 2.4 %send.4 = f32[256,1024]{1,0:T(8,128)} custom-call(s32[1]{0:T(128)} %constant.7.clone.base_ref, bf16[256,256]{1,0:T(8,128)(2,1)} %get-tuple-element.101.onehot_ref, f32[256,1024]{1,0:T(8,128)S(1)} %get-tuple-element.102.in_ref, f32[32,1024]{1,0:T(8,128)} %copy-done.4, f32[32,1024]{1,0:T(8,128)} %copy-done.10, f32[32,1024]{1,0:T(8,128)} %copy-done.12, ...), custom_call_target="tpu_custom_call" | custom-call | tf_op jit(solution)/shard_map/primary_across/cond/branch_1_fun/send/pallas_call | solution.py:43
  63.8 3.6 %all-to-all-start.1 = ((f32[8,32,1024]{2,1,0:T(8,128)}), f32[8,32,1024]{2,1,0:T(8,128)S(1)}, u32[]{:S(2)}, u32[]{:S(2)}) async-start(f32[8,32,1024]{2,1,0:T(8,128)} %bitcast.42), calls=%async_computation.1 | async-start | bytes 2097152 | tf_op jit(solution)/shard_map/primary_across/cond/branch_1_fun/all_to_all | solution.py:382
  67.4 3.7 %vectors.3.both_ref = f32[256,2048]{1,0:T(8,128)} custom-call(s32[2]{0:T(128)} %get-tuple-element.108.me_ref, f32[256,256]{1,0:T(8,128)S(1)} %get-tuple-element.109.slots_ref, f32[32,1024]{1,0:T(8,128)} %get-tuple-element.110.rest_0_, f32[32,1024]{1,0:T(8,128)} %copy-done.6, f32[32,1024]{1,0:T(8,128)} %get-tuple-element.111.rest_2_, f32[32,1024]{1,0:T(8,128)} %copy-done.10, ...), custom_call_target="tpu_custom_call" | custom-call | tf_op jit(solution)/shard_map/primary_across/cond/branch_1_fun/vectors/pallas_call | solution.py:43
  71.0 24.8 %all-to-all-done.1 = f32[8,32,1024]{2,1,0:T(8,128)S(1)} async-done(((f32[8,32,1024]{2,1,0:T(8,128)}), f32[8,32,1024]{2,1,0:T(8,128)S(1)}, u32[]{:S(2)}, u32[]{:S(2)}) %all-to-all-start.1) | async-done | bytes 1048608 | tf_op jit(solution)/shard_map/primary_across/cond/branch_1_fun/all_to_all | solution.py:382
  95.8 1.5 put.3
  97.4 32.7 %all_to_all.34 = f32[16,16,2048]{2,1,0:T(8,128)S(1)} all-to-all(f32[16,16,2048]{2,1,0:T(8,128)} %bitcast.36), channel_id=1, replica_groups=mesh['y'=4,'x'=4,'z'=8,'rep'=2] {'y','x'}, dimensions={0} | all-to-all | bytes 4194304 | tf_op jit(solution)/shard_map/out_to_owners/all_to_all | solution.py:382
  130.1 3.6 %loss.1 = f32[128,128]{1,0:T(8,128)} custom-call(f32[256,2048]{1,0:T(8,128)S(1)} %bitcast.29, f32[384,128]{1,0:T(8,128)S(1)} %bitcast.34, bf16[3,512,1024]{2,1,0:T(8,128)(2,1)S(1)} %copy-done.1, f32[8,512]{1,0:T(8,128)S(1)} %get-tuple-element.139.norms_ref), custom_call_target="tpu_custom_call" | custom-call | tf_op jit(solution)/shard_map/loss/pallas_call | solution.py:43
  133.7 7.6 %all-to-all-start.6 = ((f32[128,1,128]{2,1,0:T(1,128)}), f32[128,1,128]{2,1,0:T(1,128)S(1)}, u32[]{:S(2)}, u32[]{:S(2)}) async-start(f32[128,1,128]{2,1,0:T(1,128)} %bitcast.19), calls=%async_computation.6 | async-start | bytes 131072 | tf_op jit(solution)/shard_map/losses_back/all_to_all | solution.py:382
  141.4 11.0 %all-to-all-done.6 = f32[128,1,128]{2,1,0:T(1,128)S(1)} async-done(((f32[128,1,128]{2,1,0:T(1,128)}), f32[128,1,128]{2,1,0:T(1,128)S(1)}, u32[]{:S(2)}, u32[]{:S(2)}) %all-to-all-start.6) | async-done | bytes 65568 | tf_op jit(solution)/shard_map/losses_back/all_to_all | solution.py:382
  (38 shorter events, 5.3 us)
Async XLA Ops:
  2.0 28.0 %all-to-all-start.3 = ((f32[128,1,384]{2,1,0:T(1,128)}), f32[128,1,384]{2,1,0:T(1,128)S(1)}, u32[]{:S(2)}, u32[]{:S(2)}) async-start(f32[128,1,384]{2,1,0:T(1,128)} %bitcast.43), calls=%async_computation.3 | async-start | bytes 393216 | tf_op jit(solution)/shard_map/requests/all_to_all | solution.py:382
  17.5 11.9 %collective-permute-start = (f32[32,1024]{1,0:T(8,128)}, f32[32,1024]{1,0:T(8,128)S(1)}, u32[]{:S(2)}, u32[]{:S(2)}) collective-permute-start(f32[32,1024]{1,0:T(8,128)} %param.10), channel_id=1, source_target_pairs={{0,12},{2,14},{4,0},{6,2},{8,4},{10,6},{12,8},{14,10},{1,13},{3,15... | collective-permute-start | bytes 393224 | tf_op jit(solution)/shard_map/column_vectors/ppermute | solution.py:390
  21.1 8.9 %collective-permute-start.1 = (f32[32,1024]{1,0:T(8,128)}, f32[32,1024]{1,0:T(8,128)}, u32[]{:S(2)}, u32[]{:S(2)}) collective-permute-start(f32[32,1024]{1,0:T(8,128)} %param.10), channel_id=1, source_target_pairs={{0,4},{2,6},{4,8},{6,10},{8,12},{10,14},{12,0},{14,2},{1,5},{3,7},... | collective-permute-start | bytes 393224 | tf_op jit(solution)/shard_map/column_vectors/ppermute | solution.py:390
  21.1 1.6 %copy-start.2 = (f32[512,1024]{1,0:T(8,128)S(1)}, f32[512,1024]{1,0:T(8,128)}, u32[]{:S(2)}) copy-start(f32[512,1024]{1,0:T(8,128)} %c_ref.1) | copy-start | bytes 6291460
  24.2 7.7 %copy-start = (bf16[3,512,1024]{2,1,0:T(8,128)(2,1)}, bf16[3,512,1024]{2,1,0:T(8,128)(2,1)S(1)}, u32[]{:S(2)}) copy-start(bf16[3,512,1024]{2,1,0:T(8,128)(2,1)S(1)} %get-tuple-element.132.pieces_ref) | copy-start | bytes 9437188
  29.4 0.7 copy-start.13
  31.9 28.6 %all-to-all-start.4 = ((f32[16,16,1024]{2,1,0:T(8,128)}), f32[16,16,1024]{2,1,0:T(8,128)S(1)}, u32[]{:S(2)}, u32[]{:S(2)}) async-start(f32[16,16,1024]{2,1,0:T(8,128)} %fetch.1.found_ref), calls=%async_computation.4 | async-start | bytes 2097152 | tf_op jit(solution)/shard_map/primary_rows/all_to_all | solution.py:382
  39.6 17.6 %collective-permute-start.3 = (f32[32,1024]{1,0:T(8,128)}, f32[32,1024]{1,0:T(8,128)S(1)}, u32[]{:S(2)}, u32[]{:S(2)}) collective-permute-start(f32[32,1024]{1,0:T(8,128)} %param.10), channel_id=1, source_target_pairs={{0,8},{2,10},{4,12},{6,14},{8,0},{10,2},{12,4},{14,6},{1,9},{3,11}... | collective-permute-start | bytes 393224 | tf_op jit(solution)/shard_map/column_vectors/ppermute | solution.py:390
  42.9 14.2 %collective-permute-start.6 = (f32[32,1024]{1,0:T(8,128)}, f32[32,1024]{1,0:T(8,128)S(1)}, u32[]{:S(2)}, u32[]{:S(2)}) collective-permute-start(f32[32,1024]{1,0:T(8,128)} %param.10), channel_id=1, source_target_pairs={{0,14},{2,0},{4,2},{6,4},{8,6},{10,8},{12,10},{14,12},{1,15},{3,1}... | collective-permute-start | bytes 393224 | tf_op jit(solution)/shard_map/column_vectors/ppermute | solution.py:390
  45.6 11.5 %collective-permute-start.7 = (f32[32,1024]{1,0:T(8,128)}, f32[32,1024]{1,0:T(8,128)S(1)}, u32[]{:S(2)}, u32[]{:S(2)}) collective-permute-start(f32[32,1024]{1,0:T(8,128)} %param.10), channel_id=1, source_target_pairs={{0,2},{2,4},{4,6},{6,8},{8,10},{10,12},{12,14},{14,0},{1,3},{3,5},... | collective-permute-start | bytes 393224 | tf_op jit(solution)/shard_map/column_vectors/ppermute | solution.py:390
  46.3 10.9 %collective-permute-start.4 = (f32[32,1024]{1,0:T(8,128)}, f32[32,1024]{1,0:T(8,128)S(1)}, u32[]{:S(2)}, u32[]{:S(2)}) collective-permute-start(f32[32,1024]{1,0:T(8,128)} %copy-done.13), channel_id=1, source_target_pairs={{0,14},{2,0},{4,2},{6,4},{8,6},{10,8},{12,10},{14,12},{1,15},{3,1}... | collective-permute-start | bytes 393224 | tf_op jit(solution)/shard_map/column_vectors/ppermute | solution.py:390
  52.1 1.4 collective-permute-start.2
  53.5 7.0 %collective-permute-start.5 = (f32[32,1024]{1,0:T(8,128)}, f32[32,1024]{1,0:T(8,128)S(1)}, u32[]{:S(2)}, u32[]{:S(2)}) collective-permute-start(f32[32,1024]{1,0:T(8,128)} %collective-permute-done.1.rest_1_), channel_id=1, source_target_pairs={{0,2},{2,4},{4,6},{6,8},{8,10},{10,12},{12,14},{14,0},{1,3},{3,5},... | collective-permute-start | bytes 393224 | tf_op jit(solution)/shard_map/column_vectors/ppermute | solution.py:390
  60.5 0.6 copy-start.4
  60.5 0.7 copy-start.6
  60.5 0.7 copy-start.8
  60.5 0.8 copy-start.10
  60.5 0.8 copy-start.12
  63.8 32.0 %all-to-all-start.1 = ((f32[8,32,1024]{2,1,0:T(8,128)}), f32[8,32,1024]{2,1,0:T(8,128)S(1)}, u32[]{:S(2)}, u32[]{:S(2)}) async-start(f32[8,32,1024]{2,1,0:T(8,128)} %bitcast.42), calls=%async_computation.1 | async-start | bytes 2097152 | tf_op jit(solution)/shard_map/primary_across/cond/branch_1_fun/all_to_all | solution.py:382
  67.3 28.5 %copy-start.14 = (bf16[256,256]{1,0:T(8,128)(2,1)S(1)}, bf16[256,256]{1,0:T(8,128)(2,1)}, u32[]{:S(2)}) copy-start(bf16[256,256]{1,0:T(8,128)(2,1)} %get-tuple-element.100.onehot_ref) | copy-start | bytes 393220 | tf_op jit(solution)/shard_map/primary_across/cond
  97.4 32.7 %copy-start.1 = (bf16[3,512,1024]{2,1,0:T(8,128)(2,1)S(1)}, bf16[3,512,1024]{2,1,0:T(8,128)(2,1)}, u32[]{:S(2)}) copy-start(bf16[3,512,1024]{2,1,0:T(8,128)(2,1)} %copy-done) | copy-start | bytes 9437188
  130.1 11.2 %copy-start.15 = (s32[32,4]{0,1:T(4,128)S(1)}, s32[32,4]{0,1:T(4,128)}, u32[]{:S(2)}) copy-start(s32[32,4]{0,1:T(4,128)} %param.14) | copy-start | bytes 1540
  133.7 18.6 %all-to-all-start.6 = ((f32[128,1,128]{2,1,0:T(1,128)}), f32[128,1,128]{2,1,0:T(1,128)S(1)}, u32[]{:S(2)}, u32[]{:S(2)}) async-start(f32[128,1,128]{2,1,0:T(1,128)} %bitcast.19), calls=%async_computation.6 | async-start | bytes 131072 | tf_op jit(solution)/shard_map/losses_back/all_to_all | solution.py:382

commit v11 on v9

--- a/solution.py
+++ b/solution.py
@@ -1,5 +1,3 @@
-import functools
-
 import jax
 import jax.numpy as jnp
 from jax import lax
@@ -279,14 +277,15 @@
     wait_all(copies)
 
 
-def put_kernel(first, onehot_ref, in_ref, both_ref, out_ref, hold, sems):
-    pieces = split3(in_ref[...])
+def put_kernel(onehot_ref, in_ref, next_onehot_ref, next_ref, both_ref, out_ref, hold, sems):
+    pieces, next_pieces = split3(in_ref[...]), split3(next_ref[...])
     half = SLOTS // 2
-    at = [out_ref.at[pl.ds(c * half, half), pl.ds(first, D)] for c in range(2)]
     copies = []
     for c in range(2):
-        hold[c] = pick(onehot_ref[c * half : (c + 1) * half, :], pieces)
-        copies.append(pltpu.make_async_copy(hold.at[c], at[c], sems.at[c]))
+        cut = slice(c * half, (c + 1) * half)
+        hold[c] = pick(onehot_ref[cut, :], pieces) + pick(next_onehot_ref[cut, :], next_pieces)
+        target = out_ref.at[pl.ds(c * half, half), pl.ds(D, D)]
+        copies.append(pltpu.make_async_copy(hold.at[c], target, sems.at[c]))
         copies[-1].start()
     wait_all(copies)
 
@@ -496,8 +495,8 @@
         return both
 
     def second(state):
-        base, both = state
-        return base + NEXT, add(next_take, across(base, next_send), both)
+        base, _ = state
+        return base + NEXT, across(base, next_send)
 
     def more(state):
         base, both = state
@@ -521,21 +520,24 @@
         send, take = relay(jnp.int32(0), K)
         got = across(jnp.int32(0), send, *[blocks[o] for o in (4, 3, -3, 1, -1)])
         next_send, next_take = relay(jnp.int32(K), NEXT)
+        got, empty = lax.optimization_barrier((got, jnp.zeros((NZ * NEXT, D), F32)))
+        state = (jnp.int32(K), empty)
+        base, next_got = lax.while_loop(lambda s: (s[0] == K) & (K < most), second, state)
         [both] = call(
-            functools.partial(put_kernel, D),
+            put_kernel,
             pair,
             take,
             got,
+            next_take,
+            next_got,
             both,
-            far_in=(2,),
+            far_in=(4,),
             far_out=(0,),
-            alias={2: 0},
+            alias={4: 0},
             scratch=halves,
             name="put",
         )
-        state = (jnp.int32(K), both)
-        state = lax.while_loop(lambda s: (s[0] == K) & (K < most), second, state)
-        _, both = lax.while_loop(lambda s: s[0] < most, more, state)
+        _, both = lax.while_loop(lambda s: s[0] < most, more, (base, both))
     with jax.named_scope("out_to_owners"):
         both = swap(both.reshape(COLS, 16, 2 * D), plane).reshape(SLOTS, 2 * D)
     [losses] = call(

time: 150 us -> 152 us (1.013)
  no operation moved by 1% of the time
where the time goes in v11:
time: 152 us; the launch traced here: 151 us
  starting transfers between devices  46.5 us (31%)
  waiting for transfers between devices  41.6 us (27%)
  blocking collectives  34.7 us (23%)
  Pallas kernels  23.4 us (15%)
  local copies, waits for them, and re-layouts  3.58 us (2%)
    all_to_all x1, blocking collectives, swap(): return lax.all_to_all(a, axes, split_axis=0, concat_axis=0, tiled=True)  34.7 us
    all_to_all x4, starting transfers between devices, swap(): return lax.all_to_all(a, axes, split_axis=0, concat_axis=0, tiled=True)  33.6 us
    all_to_all x4, waiting for transfers between devices, swap(): return lax.all_to_all(a, axes, split_axis=0, concat_axis=0, tiled=True)  31.9 us
    pallas_call x11, Pallas kernels, call(): pl.pallas_call(kernel, out_shape=out_shape, in_specs=specs, out_specs=[HB...  23.4 us
    ppermute x7, starting transfers between devices, along_z(): return lax.ppermute(block, 'z', [(z, (z - step) % NZ) for z in range(NZ)])  12.9 us
    ppermute x7, waiting for transfers between devices, along_z(): return lax.ppermute(block, 'z', [(z, (z - step) % NZ) for z in range(NZ)])  9.63 us
  transfers between devices with their start and end apart: 12, of which 8 were waited for; matrix products, arithmetic and copies ran while one was open for 0% of the time, Pallas kernels for 7%

profile of v11, /device:TPU:2, one launch (start us, length us, event | category | flops | bytes accessed | tf_op | source)
XLA Modules:
  0.0 151.3 jit_solution(16835013710203730000)
XLA Ops:
  0.0 2.0 %request.1 = f32[384,128]{1,0:T(8,128)} custom-call(s32[1,32]{1,0:T(1,128)} %bitcast.51, s32[1,32]{1,0:T(1,128)} %bitcast.52, s32[4,32]{1,0:T(4,128)} %bitcast.50, s32[32,256]{1,0:T(8,128)} %rows_ref.1), custom_call_target="tpu_custom_call" | custom-call | tf_op jit(solution)/shard_map/requests/request/pallas_call | solution.py:43
  2.0 15.4 %all-to-all-start.2 = ((f32[128,1,384]{2,1,0:T(1,128)}), f32[128,1,384]{2,1,0:T(1,128)S(1)}, u32[]{:S(2)}, u32[]{:S(2)}) async-start(f32[128,1,384]{2,1,0:T(1,128)} %bitcast.49), calls=%async_computation.2 | async-start | bytes 393216 | tf_op jit(solution)/shard_map/requests/all_to_all | solution.py:383
  17.5 3.7 %collective-permute-start = (f32[32,1024]{1,0:T(8,128)}, f32[32,1024]{1,0:T(8,128)S(1)}, u32[]{:S(2)}, u32[]{:S(2)}) collective-permute-start(f32[32,1024]{1,0:T(8,128)} %rest_0_.1), channel_id=1, source_target_pairs={{0,12},{2,14},{4,0},{6,2},{8,4},{10,6},{12,8},{14,10},{1,13},{3,15... | collective-permute-start | bytes 393224 | tf_op jit(solution)/shard_map/column_vectors/ppermute | solution.py:391
  21.1 1.6 %copy-done.2 = f32[512,1024]{1,0:T(8,128)S(1)} copy-done((f32[512,1024]{1,0:T(8,128)S(1)}, f32[512,1024]{1,0:T(8,128)}, u32[]{:S(2)}) %copy-start.2) | copy-done | bytes 2097176
  22.7 1.5 prepare.1
  24.2 5.2 %collective-permute-done.rest_0_.rest_2_ = f32[32,1024]{1,0:T(8,128)S(1)} collective-permute-done((f32[32,1024]{1,0:T(8,128)}, f32[32,1024]{1,0:T(8,128)S(1)}, u32[]{:S(2)}, u32[]{:S(2)}) %collective-permute-start) | collective-permute-done | bytes 131104 | tf_op jit(solution)/shard_map/column_vectors/ppermute | solution.py:391
  30.0 1.9 %fetch.1.found_ref = f32[16,16,1024]{2,1,0:T(8,128)} custom-call(f32[384,128]{1,0:T(8,128)S(1)} %bitcast.38, bf16[3,512,1024]{2,1,0:T(8,128)(2,1)S(1)} %get-tuple-element.84.pieces_ref, f32[32,1024]{1,0:T(8,128)} %copy-done.4, f32[32,1024]{1,0:T(8,128)} %collective-permute-done.1.rest_1_.rest_6_), custom_call_target="tpu_custom_call" | custom-call | tf_op jit(solution)/shard_map/primary_rows/fetch/pallas_call | solution.py:43
  31.9 7.7 %all-to-all-start.3 = ((f32[16,16,1024]{2,1,0:T(8,128)}), f32[16,16,1024]{2,1,0:T(8,128)S(1)}, u32[]{:S(2)}, u32[]{:S(2)}) async-start(f32[16,16,1024]{2,1,0:T(8,128)} %fetch.1.found_ref), calls=%async_computation.3 | async-start | bytes 2097152 | tf_op jit(solution)/shard_map/primary_rows/all_to_all | solution.py:383
  39.6 3.3 %collective-permute-start.2 = (f32[32,1024]{1,0:T(8,128)}, f32[32,1024]{1,0:T(8,128)S(1)}, u32[]{:S(2)}, u32[]{:S(2)}) collective-permute-start(f32[32,1024]{1,0:T(8,128)} %rest_0_.1), channel_id=1, source_target_pairs={{0,8},{2,10},{4,12},{6,14},{8,0},{10,2},{12,4},{14,6},{1,9},{3,11}... | collective-permute-start | bytes 393224 | tf_op jit(solution)/shard_map/column_vectors/ppermute | solution.py:391
  42.9 2.7 %collective-permute-start.5 = (f32[32,1024]{1,0:T(8,128)}, f32[32,1024]{1,0:T(8,128)S(1)}, u32[]{:S(2)}, u32[]{:S(2)}) collective-permute-start(f32[32,1024]{1,0:T(8,128)} %rest_0_.1), channel_id=1, source_target_pairs={{0,14},{2,0},{4,2},{6,4},{8,6},{10,8},{12,10},{14,12},{1,15},{3,1}... | collective-permute-start | bytes 393224 | tf_op jit(solution)/shard_map/column_vectors/ppermute | solution.py:391
  45.6 3.2 %collective-permute-start.3 = (f32[32,1024]{1,0:T(8,128)}, f32[32,1024]{1,0:T(8,128)S(1)}, u32[]{:S(2)}, u32[]{:S(2)}) collective-permute-start(f32[32,1024]{1,0:T(8,128)} %copy-done.4), channel_id=1, source_target_pairs={{0,14},{2,0},{4,2},{6,4},{8,6},{10,8},{12,10},{14,12},{1,15},{3,1}... | collective-permute-start | bytes 393224 | tf_op jit(solution)/shard_map/column_vectors/ppermute | solution.py:391
  48.9 1.9 %slots.1 = (s32[256,128]{1,0:T(8,128)S(1)}, f32[256,256]{1,0:T(8,128)S(1)}, s32[8,128]{1,0:T(8,128)S(1)}) custom-call(s32[2]{0:T(128)S(1)} %pad_add_fusion.me_ref, f32[384,128]{1,0:T(8,128)S(1)} %bitcast.39, f32[16,16,1024]{2,1,0:T(8,128)} %fetch.1.found_ref), custom_call_target="tpu_custom_call" | custom-call | tf_op jit(solution)/shard_map/slots/pallas_call | solution.py:43
  50.8 1.6 %relay.3 = (bf16[256,256]{1,0:T(8,128)(2,1)S(1)}, bf16[256,256]{1,0:T(8,128)(2,1)S(1)}) custom-call(s32[2]{0:T(128)S(1)} %pad_add_fusion.me_ref, s32[1]{0:T(128)} %constant.10.clone.1.turn_ref.base_ref, s32[256,128]{1,0:T(8,128)S(1)} %get-tuple-element.222.info_ref, f32[256,256]{1,0:T(8,128)S(1)} %get-tuple-element.223.slots_ref), custom_call_target="tpu_custom_call" | custom-call | tf_op jit(solution)/shard_map/primary_across/relay/pallas_call | solution.py:43
  52.5 1.5 collective-permute-done.5.rest_3_.rest_1_
  57.0 1.5 send.3
  58.5 3.8 %all-to-all-start.4 = ((f32[8,32,1024]{2,1,0:T(8,128)}), f32[8,32,1024]{2,1,0:T(8,128)S(1)}, u32[]{:S(2)}, u32[]{:S(2)}) async-start(f32[8,32,1024]{2,1,0:T(8,128)} %bitcast.47), calls=%async_computation.4 | async-start | bytes 2097152 | tf_op jit(solution)/shard_map/primary_across/all_to_all | solution.py:383
  62.3 2.0 %relay.4 = (bf16[64,256]{1,0:T(8,128)(2,1)S(1)}, bf16[256,64]{1,0:T(8,128)(2,1)S(1)}) custom-call(s32[2]{0:T(128)S(1)} %pad_add_fusion.me_ref, s32[1]{0:T(128)} %constant.31.clone.1.turn_ref, s32[256,128]{1,0:T(8,128)S(1)} %get-tuple-element.222.info_ref, f32[256,256]{1,0:T(8,128)S(1)} %get-tuple-element.223.slots_ref), custom_call_target="tpu_custom_call" | custom-call | tf_op jit(solution)/shard_map/primary_across/relay/pallas_call | solution.py:43
  64.9 3.4 %vectors.1.both_ref = f32[256,2048]{1,0:T(8,128)} custom-call(s32[2]{0:T(128)S(1)} %pad_add_fusion.me_ref, f32[256,256]{1,0:T(8,128)S(1)} %get-tuple-element.223.slots_ref, f32[32,1024]{1,0:T(8,128)} %rest_0_.1, f32[32,1024]{1,0:T(8,128)} %copy-done.6, f32[32,1024]{1,0:T(8,128)} %copy-done.4, f32[32,1024]{1,0:T(8,128)} %copy-done.8, f32[32,1024]{1,0:T(8,128)} %copy-done.5, ...), custom_call_target="tpu_custom_call" | custom-call | tf_op jit(solution)/shard_map/vectors_out/vectors/pallas_call | solution.py:43
  69.5 20.9 %all-to-all-done.4 = f32[8,32,1024]{2,1,0:T(8,128)S(1)} async-done(((f32[8,32,1024]{2,1,0:T(8,128)}), f32[8,32,1024]{2,1,0:T(8,128)S(1)}, u32[]{:S(2)}, u32[]{:S(2)}) %all-to-all-start.4) | async-done | bytes 1048608 | tf_op jit(solution)/shard_map/primary_across/all_to_all | solution.py:383
  91.2 2.8 %put.1 = f32[256,2048]{1,0:T(8,128)} custom-call(bf16[256,256]{1,0:T(8,128)(2,1)S(1)} %get-tuple-element.92.onehot_ref, f32[256,1024]{1,0:T(8,128)S(1)} %bitcast.37, bf16[256,64]{1,0:T(8,128)(2,1)S(1)} %get-tuple-element.94.next_onehot_ref, f32[64,1024]{1,0:T(8,128)} %get-tuple-element.95.next_ref, ...), custom_call_target="tpu_custom_call", output_to_operand_aliasing={{}: (4, {})} | custom-call | tf_op jit(solution)/shard_map/primary_across/put/pallas_call | solution.py:43
  94.0 34.7 %all_to_all.37 = f32[16,16,2048]{2,1,0:T(8,128)S(1)} all-to-all(f32[16,16,2048]{2,1,0:T(8,128)} %bitcast.44), channel_id=1, replica_groups=mesh['y'=4,'x'=4,'z'=8,'rep'=2] {'y','x'}, dimensions={0} | all-to-all | bytes 4194304 | tf_op jit(solution)/shard_map/out_to_owners/all_to_all | solution.py:383
  128.7 3.6 %loss.1 = f32[128,128]{1,0:T(8,128)} custom-call(f32[256,2048]{1,0:T(8,128)S(1)} %bitcast.36, f32[384,128]{1,0:T(8,128)S(1)} %bitcast.40, bf16[3,512,1024]{2,1,0:T(8,128)(2,1)S(1)} %copy-done.1, f32[8,512]{1,0:T(8,128)S(1)} %get-tuple-element.97.norms_ref), custom_call_target="tpu_custom_call" | custom-call | tf_op jit(solution)/shard_map/loss/pallas_call | solution.py:43
  132.4 6.7 %all-to-all-start.6 = ((f32[128,1,128]{2,1,0:T(1,128)}), f32[128,1,128]{2,1,0:T(1,128)S(1)}, u32[]{:S(2)}, u32[]{:S(2)}) async-start(f32[128,1,128]{2,1,0:T(1,128)} %bitcast.20), calls=%async_computation.6 | async-start | bytes 131072 | tf_op jit(solution)/shard_map/losses_back/all_to_all | solution.py:383
  139.1 11.0 %all-to-all-done.6 = f32[128,1,128]{2,1,0:T(1,128)S(1)} async-done(((f32[128,1,128]{2,1,0:T(1,128)}), f32[128,1,128]{2,1,0:T(1,128)S(1)}, u32[]{:S(2)}, u32[]{:S(2)}) %all-to-all-start.6) | async-done | bytes 65568 | tf_op jit(solution)/shard_map/losses_back/all_to_all | solution.py:383
  (38 shorter events, 6.2 us)
Async XLA Ops:
  2.0 28.0 %all-to-all-start.2 = ((f32[128,1,384]{2,1,0:T(1,128)}), f32[128,1,384]{2,1,0:T(1,128)S(1)}, u32[]{:S(2)}, u32[]{:S(2)}) async-start(f32[128,1,384]{2,1,0:T(1,128)} %bitcast.49), calls=%async_computation.2 | async-start | bytes 393216 | tf_op jit(solution)/shard_map/requests/all_to_all | solution.py:383
  17.5 11.9 %collective-permute-start = (f32[32,1024]{1,0:T(8,128)}, f32[32,1024]{1,0:T(8,128)S(1)}, u32[]{:S(2)}, u32[]{:S(2)}) collective-permute-start(f32[32,1024]{1,0:T(8,128)} %rest_0_.1), channel_id=1, source_target_pairs={{0,12},{2,14},{4,0},{6,2},{8,4},{10,6},{12,8},{14,10},{1,13},{3,15... | collective-permute-start | bytes 393224 | tf_op jit(solution)/shard_map/column_vectors/ppermute | solution.py:391
  21.1 8.9 %collective-permute-start.1 = (f32[32,1024]{1,0:T(8,128)}, f32[32,1024]{1,0:T(8,128)}, u32[]{:S(2)}, u32[]{:S(2)}) collective-permute-start(f32[32,1024]{1,0:T(8,128)} %rest_0_.1), channel_id=1, source_target_pairs={{0,4},{2,6},{4,8},{6,10},{8,12},{10,14},{12,0},{14,2},{1,5},{3,7},... | collective-permute-start | bytes 393224 | tf_op jit(solution)/shard_map/column_vectors/ppermute | solution.py:391
  21.1 1.6 %copy-start.2 = (f32[512,1024]{1,0:T(8,128)S(1)}, f32[512,1024]{1,0:T(8,128)}, u32[]{:S(2)}) copy-start(f32[512,1024]{1,0:T(8,128)} %c_ref.1) | copy-start | bytes 6291460
  24.2 7.7 %copy-start = (bf16[3,512,1024]{2,1,0:T(8,128)(2,1)}, bf16[3,512,1024]{2,1,0:T(8,128)(2,1)S(1)}, u32[]{:S(2)}) copy-start(bf16[3,512,1024]{2,1,0:T(8,128)(2,1)S(1)} %get-tuple-element.84.pieces_ref) | copy-start | bytes 9437188
  29.4 0.7 copy-start.4
  31.9 24.4 %all-to-all-start.3 = ((f32[16,16,1024]{2,1,0:T(8,128)}), f32[16,16,1024]{2,1,0:T(8,128)S(1)}, u32[]{:S(2)}, u32[]{:S(2)}) async-start(f32[16,16,1024]{2,1,0:T(8,128)} %fetch.1.found_ref), calls=%async_computation.3 | async-start | bytes 2097152 | tf_op jit(solution)/shard_map/primary_rows/all_to_all | solution.py:383
  39.6 12.9 %collective-permute-start.2 = (f32[32,1024]{1,0:T(8,128)}, f32[32,1024]{1,0:T(8,128)S(1)}, u32[]{:S(2)}, u32[]{:S(2)}) collective-permute-start(f32[32,1024]{1,0:T(8,128)} %rest_0_.1), channel_id=1, source_target_pairs={{0,8},{2,10},{4,12},{6,14},{8,0},{10,2},{12,4},{14,6},{1,9},{3,11}... | collective-permute-start | bytes 393224 | tf_op jit(solution)/shard_map/column_vectors/ppermute | solution.py:391
  42.9 11.1 %collective-permute-start.5 = (f32[32,1024]{1,0:T(8,128)}, f32[32,1024]{1,0:T(8,128)S(1)}, u32[]{:S(2)}, u32[]{:S(2)}) collective-permute-start(f32[32,1024]{1,0:T(8,128)} %rest_0_.1), channel_id=1, source_target_pairs={{0,14},{2,0},{4,2},{6,4},{8,6},{10,8},{12,10},{14,12},{1,15},{3,1}... | collective-permute-start | bytes 393224 | tf_op jit(solution)/shard_map/column_vectors/ppermute | solution.py:391
  45.6 9.0 %collective-permute-start.6 = (f32[32,1024]{1,0:T(8,128)}, f32[32,1024]{1,0:T(8,128)S(1)}, u32[]{:S(2)}, u32[]{:S(2)}) collective-permute-start(f32[32,1024]{1,0:T(8,128)} %rest_0_.1), channel_id=1, source_target_pairs={{0,2},{2,4},{4,6},{6,8},{8,10},{10,12},{12,14},{14,0},{1,3},{3,5},... | collective-permute-start | bytes 393224 | tf_op jit(solution)/shard_map/column_vectors/ppermute | solution.py:391
  45.6 9.8 %collective-permute-start.3 = (f32[32,1024]{1,0:T(8,128)}, f32[32,1024]{1,0:T(8,128)S(1)}, u32[]{:S(2)}, u32[]{:S(2)}) collective-permute-start(f32[32,1024]{1,0:T(8,128)} %copy-done.4), channel_id=1, source_target_pairs={{0,14},{2,0},{4,2},{6,4},{8,6},{10,8},{12,10},{14,12},{1,15},{3,1}... | collective-permute-start | bytes 393224 | tf_op jit(solution)/shard_map/column_vectors/ppermute | solution.py:391
  48.8 7.5 %collective-permute-start.4 = (f32[32,1024]{1,0:T(8,128)}, f32[32,1024]{1,0:T(8,128)S(1)}, u32[]{:S(2)}, u32[]{:S(2)}) collective-permute-start(f32[32,1024]{1,0:T(8,128)} %collective-permute-done.1.rest_1_.rest_6_), channel_id=1, source_target_pairs={{0,2},{2,4},{4,6},{6,8},{8,10},{10,12},{12,14},{14,0},{1,3},{3,5},... | collective-permute-start | bytes 393224 | tf_op jit(solution)/shard_map/column_vectors/ppermute | solution.py:391
  52.5 3.8 %copy-start.5 = (f32[32,1024]{1,0:T(8,128)}, f32[32,1024]{1,0:T(8,128)S(1)}, u32[]{:S(2)}) copy-start(f32[32,1024]{1,0:T(8,128)S(1)} %collective-permute-done.2.rest_0_.rest_4_) | copy-start | bytes 393220
  54.0 2.3 %copy-start.6 = (f32[32,1024]{1,0:T(8,128)}, f32[32,1024]{1,0:T(8,128)S(1)}, u32[]{:S(2)}) copy-start(f32[32,1024]{1,0:T(8,128)S(1)} %collective-permute-done.5.rest_3_.rest_1_) | copy-start | bytes 393220
  54.6 1.8 %copy-start.7 = (f32[32,1024]{1,0:T(8,128)}, f32[32,1024]{1,0:T(8,128)S(1)}, u32[]{:S(2)}) copy-start(f32[32,1024]{1,0:T(8,128)S(1)} %collective-permute-done.6.rest_4_.rest_7_) | copy-start | bytes 393220
  55.4 0.9 copy-start.8
  56.3 0.6 copy-start.9
  58.5 32.0 %all-to-all-start.4 = ((f32[8,32,1024]{2,1,0:T(8,128)}), f32[8,32,1024]{2,1,0:T(8,128)S(1)}, u32[]{:S(2)}, u32[]{:S(2)}) async-start(f32[8,32,1024]{2,1,0:T(8,128)} %bitcast.47), calls=%async_computation.4 | async-start | bytes 2097152 | tf_op jit(solution)/shard_map/primary_across/all_to_all | solution.py:383
  64.9 3.4 %collective-permute-start.7 = (s32[1,1]{1,0:T(1,128)}, s32[1,1]{1,0:T(1,128)}, u32[]{:S(2)}, u32[]{:S(2)}) collective-permute-start(s32[1,1]{1,0:T(1,128)} %slice.3), channel_id=1, source_target_pairs={{0,1},{1,0},{2,3},{3,2},{4,5},{5,4},{6,7},{7,6},{8,9},{9,8},{10,11... | collective-permute-start | bytes 20 | tf_op jit(solution)/shard_map/ppermute | solution.py:448
  94.0 34.7 %copy-start.1 = (bf16[3,512,1024]{2,1,0:T(8,128)(2,1)S(1)}, bf16[3,512,1024]{2,1,0:T(8,128)(2,1)}, u32[]{:S(2)}) copy-start(bf16[3,512,1024]{2,1,0:T(8,128)(2,1)} %copy-done) | copy-start | bytes 9437188
  128.7 10.3 %copy-start.10 = (s32[32,4]{0,1:T(4,128)S(1)}, s32[32,4]{0,1:T(4,128)}, u32[]{:S(2)}) copy-start(s32[32,4]{0,1:T(4,128)} %param.14) | copy-start | bytes 1540
  132.4 17.8 %all-to-all-start.6 = ((f32[128,1,128]{2,1,0:T(1,128)}), f32[128,1,128]{2,1,0:T(1,128)S(1)}, u32[]{:S(2)}, u32[]{:S(2)}) async-start(f32[128,1,128]{2,1,0:T(1,128)} %bitcast.20), calls=%async_computation.6 | async-start | bytes 131072 | tf_op jit(solution)/shard_map/losses_back/all_to_all | solution.py:383
